TPU v7x, 512 devices: a whole 4x8x8 slice. The times are simulated.
512 devices in a mesh: dp: 32 (over z, y_lo, core), tensor: 16 (over y_hi, x).
Axes of the slice: x: 4, y: 8 (y_hi: 4, y_lo: 2; y = y_hi * 2 + y_lo), z: 8, core: 2. Of those that a mesh axis runs over, the one named last changes fastest.
Arguments:
- decoder_query: bfloat16 [4096, 8192], P('dp', 'tensor'), may hold values from -9 to 9
- decoder_memory: bfloat16 [2, 4096, 8192], P(None, 'dp', 'tensor'), may hold values from -6 to 6
- neighbour_query: bfloat16 [16384, 8192], P(('dp', 'tensor')), may hold values from -9 to 9
- neighbour_key: bfloat16 [16384, 8192], P(('dp', 'tensor')), may hold values from -6 to 6
- neighbour_value: bfloat16 [16384, 8192], P(('dp', 'tensor')), may hold values from -6 to 6
- neighbour_table: int32 [64, 2], P('dp'), may hold values from 0 to 3, as said below
- output_weight: bfloat16 [8192, 8192], P('tensor', 'dp'), may hold values from -1 to 1
Outputs:
- layer_output: bfloat16 [4096, 8192], P('dp', 'tensor')
Inputs may be any that keep to these rules, and one draw needn't show every extreme that they name: `neighbour_table`: within the 4 entries of each index of dp (its 2 stretches), every number 0 to 3 appears exactly once.
All inputs are finite; a program needn't handle non-finite values.
Results may differ from a plain program's by a relative error of at most 0.018.
Values may be sent and summed in bfloat16 or wider, within the bound.
No kernel may reach another device: no remote copies, remote signals or barrier semaphores. Data moves between devices by JAX's collectives and lax.ppermute only.
A program may use at most 64 MiB of HBM per device.

v0:
```python
import math

import jax
import jax.numpy as jnp
from jax import lax
from jax.sharding import PartitionSpec as P

HD = 128
STRETCH = 64
NBLEN = 128


def softmax_rows(scores):
    row_top = jnp.max(scores, axis=-1, keepdims=True)
    expo = jnp.exp(scores - row_top)
    return expo / jnp.sum(expo, axis=-1, keepdims=True)


def encode_block(queries, keys, values, own_values):
    nbr_count, row_span, span_cols = queries.shape
    key_span = keys.shape[1]
    head_count = span_cols // HD
    score_scale = 1.0 / math.sqrt(HD)
    query_heads = queries.reshape(nbr_count, row_span, head_count, HD)
    key_heads = keys.reshape(nbr_count, key_span, head_count, HD)
    value_heads = values.reshape(nbr_count, key_span, head_count, HD)
    scores = (
        jnp.einsum("nrhd,nchd->nhrc", query_heads, key_heads, preferred_element_type=jnp.float32)
        * score_scale
    )
    probs = softmax_rows(scores).astype(jnp.bfloat16)
    context = jnp.einsum("nhrc,nchd->nrhd", probs, value_heads, preferred_element_type=jnp.float32)
    context = context.reshape(nbr_count, row_span, span_cols)
    return (own_values.astype(jnp.float32) + context).astype(jnp.bfloat16)


def decode_stretches(queries, keys, values, table):
    stretches_here, per_stretch = table.shape
    span_cols = queries.shape[1]
    head_count = span_cols // HD
    score_scale = 1.0 / math.sqrt(HD)
    key_heads = keys[table].reshape(stretches_here, per_stretch * NBLEN, head_count, HD)
    value_heads = values[table].reshape(stretches_here, per_stretch * NBLEN, head_count, HD)
    query_heads = queries.reshape(stretches_here, STRETCH, head_count, HD)
    scores = (
        jnp.einsum("cthd,ckhd->chtk", query_heads, key_heads, preferred_element_type=jnp.float32)
        * score_scale
    )
    probs = softmax_rows(scores).astype(jnp.bfloat16)
    context = jnp.einsum("chtk,ckhd->cthd", probs, value_heads, preferred_element_type=jnp.float32)
    return context.reshape(stretches_here * STRETCH, span_cols).astype(jnp.bfloat16)


def local(
    decoder_query,
    decoder_memory,
    neighbour_query,
    neighbour_key,
    neighbour_value,
    neighbour_table,
    output_weight,
):
    stretches_here, per_stretch = neighbour_table.shape
    pool_here = stretches_here * per_stretch
    slot_stretch = jnp.arange(pool_here, dtype=jnp.int32) // per_stretch
    matches = (
        neighbour_table.reshape(-1)[None, :] == jnp.arange(pool_here, dtype=jnp.int32)[:, None]
    ).astype(jnp.int32)
    stretch_of = jnp.sum(matches * slot_stretch[None, :], axis=1)
    gathered = lax.all_gather(decoder_memory, "tensor", axis=2, tiled=True)
    row_count, all_cols = neighbour_query.shape
    nbr_count = max(row_count // NBLEN, 1)
    nbr_span = row_count // nbr_count
    first_nbr = lax.axis_index("tensor") * row_count // NBLEN
    nbr_ids = first_nbr + jnp.arange(nbr_count, dtype=jnp.int32)
    owners = stretch_of[nbr_ids]
    stretch_keys = gathered[0].reshape(stretches_here, STRETCH, all_cols)[owners]
    stretch_values = gathered[1].reshape(stretches_here, STRETCH, all_cols)[owners]
    encoded_local = encode_block(
        neighbour_query.reshape(nbr_count, nbr_span, all_cols),
        stretch_keys,
        stretch_values,
        neighbour_value.reshape(nbr_count, nbr_span, all_cols),
    )
    encoded_local = encoded_local.reshape(row_count, all_cols)
    key_rows, encoded_heads = (
        lax.all_to_all(neighbour_key, "tensor", split_axis=1, concat_axis=0, tiled=True),
        lax.all_to_all(encoded_local, "tensor", split_axis=1, concat_axis=0, tiled=True),
    )
    span_cols = key_rows.shape[1]
    encoded = encoded_heads.reshape(pool_here, NBLEN, span_cols)
    nbr_keys = key_rows.reshape(pool_here, NBLEN, span_cols)
    context = decode_stretches(decoder_query, nbr_keys, encoded, neighbour_table)
    terms = jnp.dot(
        context,
        lax.all_gather(output_weight, "dp", axis=1, tiled=True),
        preferred_element_type=jnp.float32,
    )
    summed = lax.psum_scatter(terms.astype(jnp.bfloat16), "tensor", scatter_dimension=1, tiled=True)
    return summed


def solution(mesh):
    return jax.shard_map(
        local,
        mesh=mesh,
        in_specs=(
            P("dp", "tensor"),
            P(None, "dp", "tensor"),
            P(("dp", "tensor"), None),
            P(("dp", "tensor"), None),
            P(("dp", "tensor"), None),
            P("dp", None),
            P("tensor", "dp"),
        ),
        out_specs=P("dp", "tensor"),
        check_vma=False,
    )
```

profile of v0, /device:TPU:1, one launch (start us, length us, event | category | flops | bytes accessed | tf_op | source)
XLA Modules:
  0.0 309.9 jit_solution(17162529565956956091)
XLA Ops:
  6.5 0.7 all-gather.3.cloned.1.call-update
  7.3 0.7 all-gather.5.cloned.1.call-update
  8.0 1.9 copy.78
  9.9 10.2 %all-to-all-start.1 = ((bf16[32,16,512]{2,0,1:T(8,128)(2,1)}), bf16[32,16,512]{2,0,1:T(8,128)(2,1)S(1)}, u32[]{:S(2)}, u32[]{:S(2)}) async-start(bf16[32,16,512]{2,0,1:T(8,128)(2,1)} %bitcast.59), calls=%async_computation.1 | async-start | bytes 1048576 | tf_op jit(solution)/shard_map/all_to_all | solution.py:87
  20.4 0.6 dynamic-slice.8
  22.8 84.3 %all-gather.3.cloned.1.call-done = bf16[2,128,8192]{2,1,0:T(8,128)(2,1)} async-done(((bf16[2,128,512]{2,1,0:T(8,128)(2,1)}), bf16[2,128,8192]{2,1,0:T(8,128)(2,1)}) %all-gather.3.cloned.1.call-update) | async-done | bytes 4194320 | tf_op jit(solution)/shard_map/all_gather | solution.py:70
  107.2 2.6 fusion.23
  110.0 0.3 copy.52
  110.3 0.3 copy.53
  110.6 0.9 fusion.4
  111.4 0.7 fusion.24
  112.1 4.7 %convolution_bitcast_fusion = f32[1,32,64,128]{3,1,2,0:T(8,128)} fusion(bf16[64,64,128]{2,1,0:T(8,128)(2,1)S(1)} %bitcast.67, f32[64,32]{1,0:T(8,128)S(1)} %fusion.24, f32[64,32,64]{2,1,0:T(8,128)S(1)} %fusion.4), kind=kOutput, calls=%fused_computation.9 | convolution fusion | flops 33949760 | bytes 2629632 | tf_op jit(solution)/shard_map/nhrc,nchd->nrhd/dot_general | solution.py:32
  116.8 1.9 copy.42
  118.7 0.6 fusion.9
  119.3 0.9 copy.77
  120.3 4.8 %all-to-all-start = ((bf16[32,16,512]{2,0,1:T(8,128)(2,1)}), bf16[32,16,512]{2,0,1:T(8,128)(2,1)S(1)}, u32[]{:S(2)}, u32[]{:S(2)}) async-start(bf16[32,16,512]{2,0,1:T(8,128)(2,1)} %bitcast.58), calls=%async_computation | async-start | bytes 1048576 | tf_op jit(solution)/shard_map/all_to_all | solution.py:88
  125.2 0.6 gather_fusion.1
  126.0 0.3 fusion.7
  126.5 16.7 %all-to-all-done = bf16[32,16,512]{2,0,1:T(8,128)(2,1)S(1)} async-done(((bf16[32,16,512]{2,0,1:T(8,128)(2,1)}), bf16[32,16,512]{2,0,1:T(8,128)(2,1)S(1)}, u32[]{:S(2)}, u32[]{:S(2)}) %all-to-all-start) | async-done | bytes 524320 | tf_op jit(solution)/shard_map/all_to_all | solution.py:88
  143.2 0.6 gather_fusion
  144.0 1.0 fusion.8
  145.0 62.3 %all-gather.5.cloned.1.call-done = bf16[512,8192]{1,0:T(8,128)(2,1)} async-done(((bf16[512,256]{1,0:T(8,128)(2,1)}), bf16[512,8192]{1,0:T(8,128)(2,1)}) %all-gather.5.cloned.1.call-update) | async-done | bytes 8388624 | tf_op jit(solution)/shard_map/all_gather | solution.py:96
  207.3 6.0 %convolution_convert_fusion = bf16[128,8192]{1,0:T(8,128)(2,1)} fusion(bf16[512,8192]{1,0:T(8,128)(2,1)} %all-gather.5.cloned.1.call-done, bf16[16,8,4,128]{3,2,1,0:T(4,128)(2,1)S(1)} %bitcast.69), kind=kOutput, calls=%fused_computation.4 | convolution fusion | flops 1074790400 | bytes 10616832 | tf_op jit(solution)/shard_map/dot_general | solution.py:94
  213.4 90.0 %reduce-scatter.2.cloned.1.call-done = bf16[128,512]{1,0:T(8,128)(2,1)} async-done(((bf16[128,8192]{1,0:T(8,128)(2,1)}), bf16[128,512]{1,0:T(8,128)(2,1)}) %reduce-scatter.2.cloned.1.call-update) | async-done | bytes 131088 | tf_op jit(solution)/shard_map/reduce_scatter | solution.py:99
  (25 shorter events, 1.2 us)
Async XLA Ops:
  6.5 104.0 %copy-start = (bf16[32,8192]{1,0:T(8,128)(2,1)S(1)}, bf16[32,8192]{1,0:T(8,128)(2,1)}, u32[]{:S(2)}) copy-start(bf16[32,8192]{1,0:T(8,128)(2,1)} %param.9) | copy-start | bytes 1572868
  6.5 13.6 %copy-start.3 = (s32[2,2]{1,0:T(2,128)S(1)}, s32[2,2]{1,0:T(2,128)}, u32[]{:S(2)}) copy-start(s32[2,2]{1,0:T(2,128)} %param.12) | copy-start | bytes 52
  6.5 100.6 %all-gather.3.cloned.1.call-start = ((), (), s32[]{:S(2)}) async-start(), calls=%async_computation.3 | async-start | bytes 4456448 | tf_op jit(solution)/shard_map/all_gather | solution.py:70
  7.3 200.1 %all-gather.5.cloned.1.call-start = ((), (), s32[]{:S(2)}) async-start(), calls=%async_computation.4 | async-start | bytes 8650752 | tf_op jit(solution)/shard_map/all_gather | solution.py:96
  9.9 110.3 %all-to-all-start.1 = ((bf16[32,16,512]{2,0,1:T(8,128)(2,1)}), bf16[32,16,512]{2,0,1:T(8,128)(2,1)S(1)}, u32[]{:S(2)}, u32[]{:S(2)}) async-start(bf16[32,16,512]{2,0,1:T(8,128)(2,1)} %bitcast.59), calls=%async_computation.1 | async-start | bytes 1048576 | tf_op jit(solution)/shard_map/all_to_all | solution.py:87
  116.8 1.9 copy-start.1
  118.7 6.5 %copy-start.2 = (bf16[128,512]{1,0:T(8,128)(2,1)S(1)}, bf16[128,512]{1,0:T(8,128)(2,1)}, u32[]{:S(2)}) copy-start(bf16[128,512]{1,0:T(8,128)(2,1)} %param.7) | copy-start | bytes 393220
  120.3 23.0 %all-to-all-start = ((bf16[32,16,512]{2,0,1:T(8,128)(2,1)}), bf16[32,16,512]{2,0,1:T(8,128)(2,1)S(1)}, u32[]{:S(2)}, u32[]{:S(2)}) async-start(bf16[32,16,512]{2,0,1:T(8,128)(2,1)} %bitcast.58), calls=%async_computation | async-start | bytes 1048576 | tf_op jit(solution)/shard_map/all_to_all | solution.py:88
  125.0 178.3 %reduce-scatter.2.cloned.1.call-start = ((), (), s32[]{:S(2)}) async-start(), calls=%async_computation.5 | async-start | bytes 2228224 | tf_op jit(solution)/shard_map/reduce_scatter | solution.py:99
Sparse Core Ops, SparseCore 0:
  10.3 96.7 all-gather.2
  109.2 98.0 all-gather.4
  213.5 89.8 reduce-scatter.1
where the time goes:
time: 310 us
  waiting for transfers between devices  255 us (82%)
  starting transfers between devices  15.1 us (5%)
  between operations  15.1 us (5%)
  matrix products  12.9 us (4%)
  local copies, waits for them, and re-layouts  10.4 us (3%)
    reduce_scatter x1, waiting for transfers between devices, local(): lax.psum_scatter(terms.astype(jnp.bfloat16), 'tensor', scatter_dimension=...  90 us
    all_gather x1, waiting for transfers between devices, local(): gathered = lax.all_gather(decoder_memory, 'tensor', axis=2, tiled=True)  84.3 us
    all_gather x1, waiting for transfers between devices, local(): lax.all_gather(output_weight, 'dp', axis=1, tiled=True)  62.3 us
    all_to_all x1, waiting for transfers between devices, local(): lax.all_to_all(encoded_local, 'tensor', split_axis=1, concat_axis=0, tile...  16.7 us
    all_to_all x1, starting transfers between devices, local(): lax.all_to_all(neighbour_key, 'tensor', split_axis=1, concat_axis=0, tile...  10.2 us
  transfers between devices with their start and end apart: 5, of which 4 were waited for; matrix products, arithmetic and copies ran while one was open for 6% of the time, Pallas kernels for 0%

commit v1 on v0

v1 whole, which is shorter than its diff:
```python
import functools
import math

import jax
import jax.numpy as jnp
from jax import lax
from jax.experimental import pallas as pl
from jax.experimental.pallas import tpu as pltpu
from jax.sharding import Mesh
from jax.sharding import PartitionSpec as P

HD = 128
STRETCH = 64
NBLEN = 128
SCALE = 1.0 / math.sqrt(HD)

AXES = ("z", "yl", "c", "yh", "x")
DP = ("z", "yl", "c")
TENSOR = ("yh", "x")


def softmax_rows(scores):
    row_top = jnp.max(scores, axis=-1, keepdims=True)
    expo = jnp.exp(scores - row_top)
    return (expo / jnp.sum(expo, axis=-1, keepdims=True)).astype(jnp.bfloat16)


def rows_times_rows(left, right):
    return lax.dot_general(
        left, right, (((1,), (1,)), ((), ())), preferred_element_type=jnp.float32
    )


def attention_kernel(table_ref, query_ref, memory_ref, qv_ref, key_ref, out_ref):
    stretches, per_stretch = table_ref.shape
    pieces = key_ref.shape[0] // (stretches * per_stretch)
    heads = query_ref.shape[1] // HD
    for u in range(stretches):
        rows = slice(u * STRETCH, (u + 1) * STRETCH)
        for h in range(heads):
            cols = slice(h * HD, (h + 1) * HD)
            mem_key = memory_ref[0, rows, cols]
            mem_value = memory_ref[1, rows, cols]
            query = query_ref[rows, cols]
            nbr_query, nbr_value, nbr_key = [], [], []
            for j in range(per_stretch):
                here = pl.ds(table_ref[u, j] * pieces, pieces)
                nbr_query.append(qv_ref[here, 0, :, cols].reshape(NBLEN, HD))
                nbr_value.append(qv_ref[here, 1, :, cols].reshape(NBLEN, HD))
                nbr_key.append(key_ref[here, :, cols].reshape(NBLEN, HD))
            nbr_query = jnp.concatenate(nbr_query, axis=0)
            nbr_value = jnp.concatenate(nbr_value, axis=0)
            nbr_key = jnp.concatenate(nbr_key, axis=0)
            enc_probs = softmax_rows(rows_times_rows(nbr_query, mem_key) * SCALE)
            encoded = nbr_value.astype(jnp.float32) + jnp.dot(
                enc_probs, mem_value, preferred_element_type=jnp.float32
            )
            encoded = encoded.astype(jnp.bfloat16)
            dec_probs = softmax_rows(rows_times_rows(query, nbr_key) * SCALE)
            context = jnp.dot(dec_probs, encoded, preferred_element_type=jnp.float32)
            out_ref[rows, cols] = context.astype(jnp.bfloat16)


def attention(table, query, memory, qv, key):
    vmem = pl.BlockSpec(memory_space=pltpu.VMEM)
    return pl.pallas_call(
        attention_kernel,
        out_shape=jax.ShapeDtypeStruct(query.shape, jnp.bfloat16),
        in_specs=[pl.BlockSpec(memory_space=pltpu.SMEM)] + [vmem] * 4,
        out_specs=vmem,
        compiler_params=pltpu.CompilerParams(vmem_limit_bytes=24 * 2**20),
    )(table, query, memory, qv, key)


def project_kernel(context_ref, weight_ref, out_ref, total):
    step = pl.program_id(0)

    @pl.when(step == 0)
    def _():
        total[...] = jnp.zeros_like(total)

    group = context_ref[0]
    width = weight_ref.shape[-1]
    for part in range(weight_ref.shape[1]):
        cols = slice(part * width, (part + 1) * width)
        total[:, cols] += jnp.dot(
            group, weight_ref[0, part], preferred_element_type=jnp.float32
        )

    @pl.when(step == pl.num_programs(0) - 1)
    def _():
        out_ref[...] = total[...].astype(jnp.bfloat16)


def project(context, weight):
    groups, tokens, span = context.shape
    _, parts, _, width = weight.shape
    return pl.pallas_call(
        project_kernel,
        grid=(groups,),
        out_shape=jax.ShapeDtypeStruct((tokens, parts * width), jnp.bfloat16),
        in_specs=[
            pl.BlockSpec((1, tokens, span), lambda i: (i, 0, 0)),
            pl.BlockSpec((1, parts, span, width), lambda i: (i, 0, 0, 0)),
        ],
        out_specs=pl.BlockSpec((tokens, parts * width), lambda i: (0, 0)),
        scratch_shapes=[pltpu.VMEM((tokens, parts * width), jnp.float32)],
        compiler_params=pltpu.CompilerParams(vmem_limit_bytes=24 * 2**20),
    )(context, weight)


def gather4(value, axis):
    size = 4
    ahead = [(i, (i + 1) % size) for i in range(size)]
    behind = [(i, (i - 1) % size) for i in range(size)]
    from_left = lax.ppermute(value, axis, ahead)
    from_right = lax.ppermute(value, axis, behind)
    half = value.shape[0] // 2
    far_top = lax.ppermute(from_left[:half], axis, ahead)
    far_low = lax.ppermute(from_right[half:], axis, behind)
    return [value, from_left, jnp.concatenate([far_top, far_low], axis=0), from_right]


def local(
    decoder_query,
    decoder_memory,
    neighbour_query,
    neighbour_key,
    neighbour_value,
    neighbour_table,
    output_weight,
    *,
    groups,
):
    swap = [(a * groups + b, b * groups + a) for a in range(groups) for b in range(groups)]
    moved = lax.ppermute(output_weight, ("z", "yl", "yh", "x"), swap)
    weight = lax.all_gather(moved, DP, axis=0, tiled=False)
    weight = weight.reshape(groups, 2, *moved.shape)

    rows, all_cols = neighbour_query.shape
    span = all_cols // groups
    qv = jnp.stack([neighbour_query, neighbour_value]).reshape(2, rows, groups, span)
    qv = lax.all_to_all(
        qv.transpose(2, 0, 1, 3), TENSOR, split_axis=0, concat_axis=0, tiled=True
    )
    key = neighbour_key.reshape(rows, groups, span).transpose(1, 0, 2)
    key = lax.all_to_all(key, TENSOR, split_axis=0, concat_axis=0, tiled=True)

    context = attention(neighbour_table, decoder_query, decoder_memory, qv, key)
    context = lax.all_gather(context, "yh", axis=0, tiled=False)
    tokens = context.shape[1]
    context = context.transpose(1, 0, 2).reshape(tokens, -1)
    pieces = gather4(context, "x")
    here = lax.axis_index("x")
    stacked = jnp.stack(pieces)
    order = (here - jnp.arange(4, dtype=jnp.int32)) % 4
    stacked = stacked[order]
    context = stacked.reshape(4, tokens, 4, span).transpose(2, 0, 1, 3)
    context = context.reshape(groups, tokens, span)
    return project(context, weight)


def solution(mesh):
    groups = mesh.shape["tensor"]
    inner = Mesh(mesh.devices.reshape(8, 2, 2, 4, 4), AXES)
    return jax.shard_map(
        functools.partial(local, groups=groups),
        mesh=inner,
        in_specs=(
            P(DP, TENSOR),
            P(None, DP, TENSOR),
            P(AXES, None),
            P(AXES, None),
            P(AXES, None),
            P(DP, None),
            P(TENSOR, DP),
        ),
        out_specs=P(DP, TENSOR),
        check_vma=False,
    )
```

time: 310 us -> 207 us (0.67)
  the two profiles are of different devices: /device:TPU:1 before, /device:TPU:472 now
where the time goes in v1:
time: 207 us; the launch traced here: 206 us
  waiting for transfers between devices  83 us (40%)
  blocking collectives  53.4 us (26%)
  starting transfers between devices  34.6 us (17%)
  between operations  13.6 us (7%)
  local copies, waits for them, and re-layouts  12.5 us (6%)
  Pallas kernels  7.22 us (3%)
    ppermute x1, waiting for transfers between devices, local(): moved = lax.ppermute(output_weight, ('z', 'yl', 'yh', 'x'), swap)  41.6 us
    all_to_all x1, blocking collectives, local(): lax.all_to_all(qv.transpose(2, 0, 1, 3), TENSOR, split_axis=0, concat_axi...  36.9 us
    all_to_all x1, waiting for transfers between devices, local(): key = lax.all_to_all(key, TENSOR, split_axis=0, concat_axis=0, tiled=True)  20.9 us
    all_gather x1, blocking collectives, local(): context = lax.all_gather(context, 'yh', axis=0, tiled=False)  16.5 us
    all_to_all x1, starting transfers between devices, local(): key = lax.all_to_all(key, TENSOR, split_axis=0, concat_axis=0, tiled=True)  16.4 us
    ppermute x1, waiting for transfers between devices, gather4(): from_right = lax.ppermute(value, axis, behind)  10.2 us
    ppermute x1, waiting for transfers between devices, gather4(): far_top = lax.ppermute(from_left[:half], axis, ahead)  5.63 us
    ppermute x1, starting transfers between devices, gather4(): far_low = lax.ppermute(from_right[half:], axis, behind)  5.33 us
  transfers between devices with their start and end apart: 7, of which 5 were waited for; matrix products, arithmetic and copies ran while one was open for 5% of the time, Pallas kernels for 1%

profile of v1, /device:TPU:472, one launch (start us, length us, event | category | flops | bytes accessed | tf_op | source)
XLA Modules:
  0.0 206.1 jit_solution(14113489099138397190)
XLA Ops:
  6.5 4.5 %collective-permute-start.4 = (bf16[512,256]{1,0:T(8,128)(2,1)}, bf16[512,256]{1,0:T(8,128)(2,1)S(1)}, u32[]{:S(2)}, u32[]{:S(2)}) collective-permute-start(bf16[512,256]{1,0:T(8,128)(2,1)} %param.13), channel_id=1, source_target_pairs={{0,0},{1,32},{2,64},{3,96},{4,128},{5,160},{6,192},{7,224},{8,256}... | collective-permute-start | bytes 786440 | tf_op jit(solution)/shard_map/ppermute | solution.py:136
  11.0 41.6 %collective-permute-done.4 = bf16[512,256]{1,0:T(8,128)(2,1)S(1)} collective-permute-done((bf16[512,256]{1,0:T(8,128)(2,1)}, bf16[512,256]{1,0:T(8,128)(2,1)S(1)}, u32[]{:S(2)}, u32[]{:S(2)}) %collective-permute-start.4) | collective-permute-done | bytes 262176 | tf_op jit(solution)/shard_map/ppermute | solution.py:136
  52.6 0.7 copy-done.7
  53.4 2.0 copy.17
  55.4 16.4 %all-to-all-start.1 = ((bf16[16,32,512]{2,1,0:T(8,128)(2,1)}), bf16[16,32,512]{2,1,0:T(8,128)(2,1)S(1)}, u32[]{:S(2)}, u32[]{:S(2)}) async-start(bf16[16,32,512]{2,1,0:T(8,128)(2,1)} %bitcast.31), calls=%async_computation.1 | async-start | bytes 1048576 | tf_op jit(solution)/shard_map/all_to_all | solution.py:147
  72.0 0.3 copy.8
  72.5 0.3 copy.9
  72.9 20.9 %all-to-all-done.1.key_ref = bf16[16,32,512]{2,1,0:T(8,128)(2,1)S(1)} async-done(((bf16[16,32,512]{2,1,0:T(8,128)(2,1)}), bf16[16,32,512]{2,1,0:T(8,128)(2,1)S(1)}, u32[]{:S(2)}, u32[]{:S(2)}) %all-to-all-start.1) | async-done | bytes 524320 | tf_op jit(solution)/shard_map/all_to_all | solution.py:147
  93.8 36.9 %all_to_all.10.qv_ref = bf16[16,2,32,512]{3,2,1,0:T(8,128)(2,1)S(1)} all-to-all(bf16[16,2,32,512]{3,2,1,0:T(8,128)(2,1)S(1)} %maximum_bitcast_fusion), channel_id=1, replica_groups=mesh['z'=8,'yl'=2,'c'=2,'yh'=4,'x'=4] {'yh','x'}, dimensions={0} | all-to-all | bytes 2097152 | tf_op jit(solution)/shard_map/all_to_all | solution.py:143
  130.7 2.6 %shard_map.73 = bf16[128,512]{1,0:T(8,128)(2,1)S(1)} custom-call(s32[2,2]{1,0:T(2,128)S(1)} %copy-done.3, bf16[128,512]{1,0:T(8,128)(2,1)S(1)} %copy-done.2, bf16[2,128,512]{2,1,0:T(8,128)(2,1)S(1)} %copy-done.1, bf16[16,2,32,512]{3,2,1,0:T(8,128)(2,1)S(1)} %all_to_all.10.qv_ref, bf16[16,32,512]{2,1,0:T(8,128)(2,1)S(1)} %all-to-all-done.1.key_ref), custom_call_target="tpu_custom_call" | custom-call | tf_op jit(solution)/shard_map/pallas_call | solution.py:66
  133.3 16.5 %all-gather = bf16[512,512]{1,0:T(8,128)(2,1)S(1)} all-gather(bf16[128,512]{1,0:T(8,128)(2,1)S(1)} %shard_map.73), channel_id=2, replica_groups=mesh['z'=8,'yl'=2,'c'=2,'yh'=4,'x'=4] {'yh'}, dimensions={0}, use_global_device_ids=true | all-gather | bytes 655360 | tf_op jit(solution)/shard_map/all_gather | solution.py:150
  150.1 4.5 %collective-permute-start.2 = (bf16[128,2048]{0,1:T(8,128)(2,1)S(1)}, bf16[128,2048]{0,1:T(8,128)(2,1)S(1)}, u32[]{:S(2)}, u32[]{:S(2)}) collective-permute-start(bf16[128,2048]{0,1:T(8,128)(2,1)S(1)} %bitcast.39), channel_id=1, source_target_pairs={{0,3},{1,0},{2,1},{3,2},{4,7},{5,4},{6,5},{7,6},{8,11},{9,8},{10,9... | collective-permute-start | bytes 1572872 | tf_op jit(solution)/shard_map/ppermute | solution.py:117
  154.6 1.9 collective-permute-start
  156.6 10.2 %collective-permute-done.2 = bf16[128,2048]{0,1:T(8,128)(2,1)S(1)} collective-permute-done((bf16[128,2048]{0,1:T(8,128)(2,1)S(1)}, bf16[128,2048]{0,1:T(8,128)(2,1)S(1)}, u32[]{:S(2)}, u32[]{:S(2)}) %collective-permute-start.2) | collective-permute-done | bytes 524320 | tf_op jit(solution)/shard_map/ppermute | solution.py:117
  166.9 5.3 %collective-permute-start.3 = (bf16[64,2048]{0,1:T(8,128)(2,1)S(1)}, bf16[64,2048]{0,1:T(8,128)(2,1)S(1)}, u32[]{:S(2)}, u32[]{:S(2)}) collective-permute-start(bf16[64,2048]{0,1:T(8,128)(2,1)S(1)} %slice.11), channel_id=1, source_target_pairs={{0,3},{1,0},{2,1},{3,2},{4,7},{5,4},{6,5},{7,6},{8,11},{9,8},{10,9... | collective-permute-start | bytes 786440 | tf_op jit(solution)/shard_map/ppermute | solution.py:120
  172.3 1.9 collective-permute-start.1
  174.3 4.7 %collective-permute-done.3 = bf16[64,2048]{0,1:T(8,128)(2,1)S(1)} collective-permute-done((bf16[64,2048]{0,1:T(8,128)(2,1)S(1)}, bf16[64,2048]{0,1:T(8,128)(2,1)S(1)}, u32[]{:S(2)}, u32[]{:S(2)}) %collective-permute-start.3) | collective-permute-done | bytes 262176 | tf_op jit(solution)/shard_map/ppermute | solution.py:120
  178.9 5.6 %collective-permute-done.1 = bf16[64,2048]{0,1:T(8,128)(2,1)S(1)} collective-permute-done((bf16[64,2048]{0,1:T(8,128)(2,1)S(1)}, bf16[64,2048]{0,1:T(8,128)(2,1)S(1)}, u32[]{:S(2)}, u32[]{:S(2)}) %collective-permute-start.1) | collective-permute-done | bytes 262176 | tf_op jit(solution)/shard_map/ppermute | solution.py:119
  184.6 0.3 maximum_bitcast_fusion.1
  184.9 1.3 pad_maximum_fusion
  186.2 2.2 %gather_fusion = bf16[4,128,2048]{1,2,0:T(8,128)(2,1)} fusion(bf16[4,128,2048]{1,2,0:T(8,128)(2,1)S(1)} %pad_maximum_fusion, s32[1024]{0:T(1024)S(1)} %pad_clamp_fusion), kind=kCustom, calls=%fused_computation | custom fusion | bytes 4194320 | tf_op jit(solution)/shard_map/gather | solution.py:157
  188.4 2.8 %copy.12 = bf16[4,4,128,512]{3,2,1,0:T(8,128)(2,1)S(1)} copy(bf16[4,4,128,512]{2,3,0,1:T(8,128)(2,1)} %bitcast.35) | data formatting | bytes 4194304 | tf_op jit(solution)/shard_map/transpose | solution.py:158
  191.2 3.4 %copy-done = bf16[16384,256]{1,0:T(8,128)(2,1)S(1)} copy-done((bf16[16384,256]{1,0:T(8,128)(2,1)S(1)}, bf16[16384,256]{1,0:T(8,128)(2,1)}, u32[]{:S(2)}) %copy-start) | copy-done | bytes 8388632
  194.6 4.6 %shard_map.74 = bf16[128,512]{1,0:T(8,128)(2,1)} custom-call(bf16[16,128,512]{2,1,0:T(8,128)(2,1)S(1)} %bitcast.34, bf16[16,2,512,256]{3,2,1,0:T(8,128)(2,1)S(1)} %bitcast.33), custom_call_target="tpu_custom_call" | custom-call | tf_op jit(solution)/shard_map/pallas_call | solution.py:98
  (25 shorter events, 1.0 us)
Async XLA Ops:
  6.5 65.3 %copy-start.4 = (bf16[32,8192]{1,0:T(8,128)(2,1)S(1)}, bf16[32,8192]{1,0:T(8,128)(2,1)}, u32[]{:S(2)}) copy-start(bf16[32,8192]{1,0:T(8,128)(2,1)} %param.9) | copy-start | bytes 1572868
  6.5 184.7 %all-gather.4.cloned.1.call-start = ((), (), s32[]{:S(2)}) async-start(), calls=%async_computation.2 | async-start | bytes 8650752 | tf_op jit(solution)/shard_map/all_gather | solution.py:137
  6.5 46.1 %collective-permute-start.4 = (bf16[512,256]{1,0:T(8,128)(2,1)}, bf16[512,256]{1,0:T(8,128)(2,1)S(1)}, u32[]{:S(2)}, u32[]{:S(2)}) collective-permute-start(bf16[512,256]{1,0:T(8,128)(2,1)} %param.13), channel_id=1, source_target_pairs={{0,0},{1,32},{2,64},{3,96},{4,128},{5,160},{6,192},{7,224},{8,256}... | collective-permute-start | bytes 786440 | tf_op jit(solution)/shard_map/ppermute | solution.py:136
  52.6 0.7 copy-start.7
  53.4 18.9 %copy-start.5 = (bf16[32,8192]{1,0:T(8,128)(2,1)S(1)}, bf16[32,8192]{1,0:T(8,128)(2,1)}, u32[]{:S(2)}) copy-start(bf16[32,8192]{1,0:T(8,128)(2,1)} %param.11) | copy-start | bytes 1572868
  55.4 38.4 %all-to-all-start.1 = ((bf16[16,32,512]{2,1,0:T(8,128)(2,1)}), bf16[16,32,512]{2,1,0:T(8,128)(2,1)S(1)}, u32[]{:S(2)}, u32[]{:S(2)}) async-start(bf16[16,32,512]{2,1,0:T(8,128)(2,1)} %bitcast.31), calls=%async_computation.1 | async-start | bytes 1048576 | tf_op jit(solution)/shard_map/all_to_all | solution.py:147
  72.8 57.9 %copy-start.1 = (bf16[2,128,512]{2,1,0:T(8,128)(2,1)S(1)}, bf16[2,128,512]{2,1,0:T(8,128)(2,1)}, u32[]{:S(2)}) copy-start(bf16[2,128,512]{2,1,0:T(8,128)(2,1)} %memory_ref.1) | copy-start | bytes 786436
  72.8 57.9 %copy-start.2 = (bf16[128,512]{1,0:T(8,128)(2,1)S(1)}, bf16[128,512]{1,0:T(8,128)(2,1)}, u32[]{:S(2)}) copy-start(bf16[128,512]{1,0:T(8,128)(2,1)} %query_ref.1) | copy-start | bytes 393220
  72.8 57.9 %copy-start.3 = (s32[2,2]{1,0:T(2,128)S(1)}, s32[2,2]{1,0:T(2,128)}, u32[]{:S(2)}) copy-start(s32[2,2]{1,0:T(2,128)} %table_ref.1) | copy-start | bytes 52
  150.1 16.6 %collective-permute-start.2 = (bf16[128,2048]{0,1:T(8,128)(2,1)S(1)}, bf16[128,2048]{0,1:T(8,128)(2,1)S(1)}, u32[]{:S(2)}, u32[]{:S(2)}) collective-permute-start(bf16[128,2048]{0,1:T(8,128)(2,1)S(1)} %bitcast.39), channel_id=1, source_target_pairs={{0,3},{1,0},{2,1},{3,2},{4,7},{5,4},{6,5},{7,6},{8,11},{9,8},{10,9... | collective-permute-start | bytes 1572872 | tf_op jit(solution)/shard_map/ppermute | solution.py:117
  154.6 17.6 %collective-permute-start = (bf16[128,2048]{0,1:T(8,128)(2,1)S(1)}, bf16[128,2048]{0,1:T(8,128)(2,1)S(1)}, u32[]{:S(2)}, u32[]{:S(2)}) collective-permute-start(bf16[128,2048]{0,1:T(8,128)(2,1)S(1)} %bitcast.40), channel_id=1, source_target_pairs={{0,1},{1,2},{2,3},{3,0},{4,5},{5,6},{6,7},{7,4},{8,9},{9,10},{10,1... | collective-permute-start | bytes 1572872 | tf_op jit(solution)/shard_map/ppermute | solution.py:116
  166.9 12.0 %collective-permute-start.3 = (bf16[64,2048]{0,1:T(8,128)(2,1)S(1)}, bf16[64,2048]{0,1:T(8,128)(2,1)S(1)}, u32[]{:S(2)}, u32[]{:S(2)}) collective-permute-start(bf16[64,2048]{0,1:T(8,128)(2,1)S(1)} %slice.11), channel_id=1, source_target_pairs={{0,3},{1,0},{2,1},{3,2},{4,7},{5,4},{6,5},{7,6},{8,11},{9,8},{10,9... | collective-permute-start | bytes 786440 | tf_op jit(solution)/shard_map/ppermute | solution.py:120
  172.3 12.6 %copy-start.6 = (bf16[128,2048]{0,1:T(8,128)(2,1)}, bf16[128,2048]{0,1:T(8,128)(2,1)S(1)}, u32[]{:S(2)}) copy-start(bf16[128,2048]{0,1:T(8,128)(2,1)S(1)} %collective-permute-done) | copy-start | bytes 1572868
  172.3 12.3 %collective-permute-start.1 = (bf16[64,2048]{0,1:T(8,128)(2,1)S(1)}, bf16[64,2048]{0,1:T(8,128)(2,1)S(1)}, u32[]{:S(2)}, u32[]{:S(2)}) collective-permute-start(bf16[64,2048]{0,1:T(8,128)(2,1)S(1)} %bitcast.46), channel_id=1, source_target_pairs={{0,1},{1,2},{2,3},{3,0},{4,5},{5,6},{6,7},{7,4},{8,9},{9,10},{10,1... | collective-permute-start | bytes 786440 | tf_op jit(solution)/shard_map/ppermute | solution.py:119
  191.2 3.4 %copy-start = (bf16[16384,256]{1,0:T(8,128)(2,1)S(1)}, bf16[16384,256]{1,0:T(8,128)(2,1)}, u32[]{:S(2)}) copy-start(bf16[16384,256]{1,0:T(8,128)(2,1)} %all-gather.4.cloned.1.call-done) | copy-start | bytes 25165828
Sparse Core Ops, SparseCore 0:
  53.5 104.1 all-gather.3

commit v2 on v1

v2 whole, which is shorter than its diff:
```python
import functools
import math

import jax
import jax.numpy as jnp
from jax import lax
from jax.experimental import pallas as pl
from jax.experimental.pallas import tpu as pltpu
from jax.sharding import Mesh
from jax.sharding import PartitionSpec as P

HD = 128
STRETCH = 64
NBLEN = 128
SCALE = 1.0 / math.sqrt(HD)

AXES = ("z", "yl", "c", "yh", "x")
DP = ("z", "yl", "c")
TENSOR = ("yh", "x")


def softmax_rows(scores):
    row_top = jnp.max(scores, axis=-1, keepdims=True)
    expo = jnp.exp(scores - row_top)
    return (expo / jnp.sum(expo, axis=-1, keepdims=True)).astype(jnp.bfloat16)


def rows_times_rows(left, right):
    return lax.dot_general(
        left, right, (((1,), (1,)), ((), ())), preferred_element_type=jnp.float32
    )


def attention_kernel(table_ref, query_ref, memory_ref, nbr_ref, out_ref):
    stretches, per_stretch = table_ref.shape
    pieces = nbr_ref.shape[0] // (stretches * per_stretch)
    heads = query_ref.shape[1] // HD
    for u in range(stretches):
        rows = slice(u * STRETCH, (u + 1) * STRETCH)
        places = [pl.ds(table_ref[u, j] * pieces, pieces) for j in range(per_stretch)]
        for h in range(heads):
            cols = slice(h * HD, (h + 1) * HD)
            nbr_query, nbr_key, nbr_value = (
                jnp.concatenate(
                    [nbr_ref[place, kind, :, cols].reshape(NBLEN, HD) for place in places],
                    axis=0,
                )
                for kind in range(3)
            )
            enc_probs = softmax_rows(
                rows_times_rows(nbr_query, memory_ref[0, rows, cols]) * SCALE
            )
            encoded = nbr_value.astype(jnp.float32) + jnp.dot(
                enc_probs, memory_ref[1, rows, cols], preferred_element_type=jnp.float32
            )
            encoded = encoded.astype(jnp.bfloat16)
            dec_probs = softmax_rows(
                rows_times_rows(query_ref[rows, cols], nbr_key) * SCALE
            )
            context = jnp.dot(dec_probs, encoded, preferred_element_type=jnp.float32)
            context = context.astype(jnp.bfloat16)
            for copy in range(out_ref.shape[0]):
                out_ref[copy, rows, cols] = context


VMEM = pl.BlockSpec(memory_space=pltpu.VMEM)
PARAMS = pltpu.CompilerParams(vmem_limit_bytes=32 * 2**20)


def attention(table, query, memory, neighbours, copies):
    return pl.pallas_call(
        attention_kernel,
        out_shape=jax.ShapeDtypeStruct((copies, *query.shape), jnp.bfloat16),
        in_specs=[pl.BlockSpec(memory_space=pltpu.SMEM)] + [VMEM] * 3,
        out_specs=VMEM,
        compiler_params=PARAMS,
    )(table, query, memory, neighbours)


def fold_kernel(weight_ref, out_ref):
    copies, quarters, half, _ = out_ref.shape
    width = weight_ref.shape[1] // quarters
    for q in range(quarters):
        cols = slice(q * width, (q + 1) * width)
        block = jnp.concatenate([weight_ref[:half, cols], weight_ref[half:, cols]], axis=1)
        for copy in range(copies):
            out_ref[copy, q] = block


def fold(weight, copies, quarters):
    rows, cols = weight.shape
    shape = (copies, quarters, rows // 2, 2 * cols // quarters)
    return pl.pallas_call(
        fold_kernel,
        out_shape=jax.ShapeDtypeStruct(shape, weight.dtype),
        in_specs=[VMEM],
        out_specs=VMEM,
        compiler_params=PARAMS,
    )(weight)


def unfold_kernel(folded_ref, out_ref):
    _, quarters, half, width = folded_ref.shape
    middle = width // 2
    for q in range(quarters):
        first, second = folded_ref[0, q], folded_ref[1, q]
        upper = jnp.concatenate([first[:, :middle], second[:, :middle]], axis=1)
        lower = jnp.concatenate([first[:, middle:], second[:, middle:]], axis=1)
        out_ref[pl.ds(2 * q * half, half), :] = upper
        out_ref[pl.ds((2 * q + 1) * half, half), :] = lower


def unfold(folded):
    _, quarters, half, width = folded.shape
    return pl.pallas_call(
        unfold_kernel,
        out_shape=jax.ShapeDtypeStruct((2 * quarters * half, width), folded.dtype),
        in_specs=[VMEM],
        out_specs=VMEM,
        compiler_params=PARAMS,
    )(folded)


def project_kernel(context_ref, weight_ref, out_ref):
    sides, quarters, tokens, span = context_ref.shape
    half = tokens // 2
    total = None
    weight = jnp.concatenate([weight_ref[0], weight_ref[1]], axis=1)
    for q in range(quarters):
        left = jnp.concatenate([context_ref[s, q] for s in range(sides)], axis=0)
        term = jnp.dot(
            left, weight[q * span : (q + 1) * span], preferred_element_type=jnp.float32
        )
        total = term if total is None else total + term
    width = weight_ref.shape[2]
    for s in range(sides):
        upper = total[s * tokens : s * tokens + half].astype(jnp.bfloat16)
        lower = total[s * tokens + half : (s + 1) * tokens].astype(jnp.bfloat16)
        for piece in range(out_ref.shape[1]):
            cols = slice(piece * width // 2, (piece + 1) * width // 2)
            out_ref[s, piece] = jnp.concatenate([upper[:, cols], lower[:, cols]], axis=1)


def project(context, weight):
    sides, quarters, tokens, span = context.shape
    planes, depth, width = weight.shape
    return pl.pallas_call(
        project_kernel,
        grid=(planes // 2,),
        out_shape=jax.ShapeDtypeStruct((sides, 2 * planes, tokens // 2, width), jnp.bfloat16),
        in_specs=[
            pl.BlockSpec(context.shape, lambda i: (0, 0, 0, 0)),
            pl.BlockSpec((2, depth, width), lambda i: (i, 0, 0)),
        ],
        out_specs=pl.BlockSpec((sides, 4, tokens // 2, width), lambda i: (0, i, 0, 0)),
        compiler_params=PARAMS,
    )(context, weight)


def add_kernel(partial_ref, out_ref):
    sides, senders, quarters, half, width = partial_ref.shape
    for s in range(sides):
        for pair in range(quarters // 2):
            sums = []
            for q in (2 * pair, 2 * pair + 1):
                total = partial_ref[s, 0, q].astype(jnp.float32)
                for sender in range(1, senders):
                    total += partial_ref[s, sender, q].astype(jnp.float32)
                sums.append(total.astype(jnp.bfloat16))
            first, second = sums
            middle = width // 2
            cols = pl.ds((s * (quarters // 2) + pair) * width, width)
            out_ref[:half, cols] = jnp.concatenate(
                [first[:, :middle], second[:, :middle]], axis=1
            )
            out_ref[half:, cols] = jnp.concatenate(
                [first[:, middle:], second[:, middle:]], axis=1
            )


def add(partial):
    sides, _, quarters, half, width = partial.shape
    return pl.pallas_call(
        add_kernel,
        out_shape=jax.ShapeDtypeStruct((2 * half, sides * quarters * width // 2), jnp.bfloat16),
        in_specs=[VMEM],
        out_specs=VMEM,
        compiler_params=PARAMS,
    )(partial)


def exchange(value, axes):
    return lax.all_to_all(value, axes, split_axis=0, concat_axis=0, tiled=True)


def local(
    decoder_query,
    decoder_memory,
    neighbour_query,
    neighbour_key,
    neighbour_value,
    neighbour_table,
    output_weight,
    *,
    groups,
):
    folded = fold(output_weight, 2, 4)
    shape = folded.shape
    folded = exchange(folded.reshape(8, *shape[2:]), ("yl", "x")).reshape(shape)
    weight = lax.all_gather(unfold(folded), "z", axis=0, tiled=False)

    rows, all_cols = neighbour_query.shape
    span = all_cols // groups
    neighbours = jnp.stack([neighbour_query, neighbour_key, neighbour_value])
    neighbours = neighbours.reshape(3, rows, groups, span).transpose(2, 0, 1, 3)
    neighbours = exchange(neighbours, TENSOR)

    context = attention(neighbour_table, decoder_query, decoder_memory, neighbours, 8)
    context = exchange(context, ("c", "x"))
    context = context.reshape(2, 4, *context.shape[1:])
    partial = project(context, weight)
    shape = partial.shape
    partial = exchange(partial.reshape(2 * groups, *shape[2:]), ("c", "yh", "x"))
    return add(partial.reshape(2, 4, 4, *shape[2:]))


def solution(mesh):
    groups = mesh.shape["tensor"]
    inner = Mesh(mesh.devices.reshape(8, 2, 2, 4, 4), AXES)
    return jax.shard_map(
        functools.partial(local, groups=groups),
        mesh=inner,
        in_specs=(
            P(DP, TENSOR),
            P(None, DP, TENSOR),
            P(AXES, None),
            P(AXES, None),
            P(AXES, None),
            P(DP, None),
            P(TENSOR, DP),
        ),
        out_specs=P(DP, TENSOR),
        check_vma=False,
    )
```

time: 207 us -> 128 us (0.62)
  the two profiles are of different devices: /device:TPU:472 before, /device:TPU:201 now
where the time goes in v2:
time: 128 us
  blocking collectives  102 us (80%)
  between operations  13.5 us (11%)
  Pallas kernels  6.68 us (5%)
  local copies, waits for them, and re-layouts  5.06 us (4%)
    all_to_all x4, blocking collectives, exchange(): return lax.all_to_all(value, axes, split_axis=0, concat_axis=0, tiled=True)  102 us
    unnamed x19, local copies, waits for them, and re-layouts  4.18 us
    pallas_call x1, Pallas kernels, attention(): pl.pallas_call(attention_kernel, out_shape=jax.ShapeDtypeStruct((copies,...  2.62 us
  transfers between devices with their start and end apart: 1, of which 0 were waited for; matrix products, arithmetic and copies ran while one was open for 1% of the time, Pallas kernels for 2%

profile of v2, /device:TPU:201, one launch (start us, length us, event | category | flops | bytes accessed | tf_op | source)
XLA Modules:
  0.0 127.8 jit_solution(67054526049864338)
XLA Ops:
  6.5 0.9 copy-done.1
  7.5 0.1 shard_map.74
  7.6 13.1 %all_to_all.20 = bf16[8,256,128]{2,1,0:T(8,128)(2,1)S(1)} all-to-all(bf16[8,256,128]{2,1,0:T(8,128)(2,1)S(1)} %bitcast.21), channel_id=1, replica_groups=mesh['z'=8,'yl'=2,'c'=2,'yh'=4,'x'=4] {'yl','x'}, dimensions={0} | all-to-all | bytes 1048576 | tf_op jit(solution)/shard_map/all_to_all | solution.py:193
  20.7 1.0 shard_map.75
  21.7 0.0 all-gather.3.cloned.1.call-update
  21.8 0.2 copy.11
  21.9 0.0 copy-start.7
  21.9 0.3 copy.8
  22.2 0.5 copy-done.6
  22.8 0.2 copy.12
  22.9 0.3 copy.9
  23.2 0.2 copy.13
  23.4 0.3 copy.10
  23.7 0.2 maximum_bitcast_fusion
  23.9 0.0 copy-start.2
  23.9 0.0 copy-start.3
  23.9 0.0 copy-start.4
  23.9 47.1 %all_to_all.21.nbr_ref = bf16[16,3,32,512]{3,2,1,0:T(8,128)(2,1)S(1)} all-to-all(bf16[16,3,32,512]{3,2,1,0:T(8,128)(2,1)S(1)} %maximum_bitcast_fusion), channel_id=1, replica_groups=mesh['z'=8,'yl'=2,'c'=2,'yh'=4,'x'=4] {'yh','x'}, dimensions={0} | all-to-all | bytes 3145728 | tf_op jit(solution)/shard_map/all_to_all | solution.py:193
  71.0 2.6 %shard_map.73 = bf16[8,128,512]{2,1,0:T(8,128)(2,1)S(1)} custom-call(s32[2,2]{1,0:T(2,128)S(1)} %copy-done.4, bf16[128,512]{1,0:T(8,128)(2,1)S(1)} %copy-done.3, bf16[2,128,512]{2,1,0:T(8,128)(2,1)S(1)} %copy-done.2, bf16[16,3,32,512]{3,2,1,0:T(8,128)(2,1)S(1)} %all_to_all.21.nbr_ref), custom_call_target="tpu_custom_call" | custom-call | tf_op jit(solution)/shard_map/pallas_call | solution.py:71
  73.7 18.8 %all_to_all.22 = bf16[8,128,512]{2,1,0:T(8,128)(2,1)S(1)} all-to-all(bf16[8,128,512]{2,1,0:T(8,128)(2,1)S(1)} %shard_map.73), channel_id=1, replica_groups=mesh['z'=8,'yl'=2,'c'=2,'yh'=4,'x'=4] {'c','x'}, dimensions={0} | all-to-all | bytes 2097152 | tf_op jit(solution)/shard_map/all_to_all | solution.py:193
  92.5 2.2 %copy-done = bf16[16384,128]{1,0:T(8,128)(2,1)S(1)} copy-done((bf16[16384,128]{1,0:T(8,128)(2,1)S(1)}, bf16[16384,128]{1,0:T(8,128)(2,1)}, u32[]{:S(2)}) %copy-start) | copy-done | bytes 4194328
  94.7 2.1 %shard_map.76 = bf16[2,16,64,128]{3,2,1,0:T(8,128)(2,1)S(1)} custom-call(bf16[2,4,128,512]{3,2,1,0:T(8,128)(2,1)S(1)} %bitcast.18, bf16[8,2048,128]{2,1,0:T(8,128)(2,1)S(1)} %bitcast.17), custom_call_target="tpu_custom_call" | custom-call | tf_op jit(solution)/shard_map/pallas_call | solution.py:147
  96.8 23.4 %all_to_all.23 = bf16[32,64,128]{2,1,0:T(8,128)(2,1)S(1)} all-to-all(bf16[32,64,128]{2,1,0:T(8,128)(2,1)S(1)} %bitcast.22), channel_id=1, replica_groups=mesh['z'=8,'yl'=2,'c'=2,'yh'=4,'x'=4] {'c','yh','x'}, dimensions={0} | all-to-all | bytes 1048576 | tf_op jit(solution)/shard_map/all_to_all | solution.py:193
  120.2 0.8 shard_map.77
  (11 shorter events, 0.0 us)
Async XLA Ops:
  6.5 85.9 %all-gather.3.cloned.1.call-start = ((), (), s32[]{:S(2)}) async-start(), calls=%async_computation.4 | async-start | bytes 4718592 | tf_op jit(solution)/shard_map/all_gather | solution.py:210
  6.5 0.9 copy-start.1
  7.5 14.3 %copy-start.5 = (bf16[32,8192]{1,0:T(8,128)(2,1)S(1)}, bf16[32,8192]{1,0:T(8,128)(2,1)}, u32[]{:S(2)}) copy-start(bf16[32,8192]{1,0:T(8,128)(2,1)} %param.9) | copy-start | bytes 1572868
  21.7 1.0 copy-start.6
  21.9 1.3 %copy-start.7 = (bf16[32,8192]{1,0:T(8,128)(2,1)S(1)}, bf16[32,8192]{1,0:T(8,128)(2,1)}, u32[]{:S(2)}) copy-start(bf16[32,8192]{1,0:T(8,128)(2,1)} %param.11) | copy-start | bytes 1572868
  23.9 47.1 %copy-start.2 = (bf16[2,128,512]{2,1,0:T(8,128)(2,1)S(1)}, bf16[2,128,512]{2,1,0:T(8,128)(2,1)}, u32[]{:S(2)}) copy-start(bf16[2,128,512]{2,1,0:T(8,128)(2,1)} %memory_ref.1) | copy-start | bytes 786436
  23.9 47.1 %copy-start.3 = (bf16[128,512]{1,0:T(8,128)(2,1)S(1)}, bf16[128,512]{1,0:T(8,128)(2,1)}, u32[]{:S(2)}) copy-start(bf16[128,512]{1,0:T(8,128)(2,1)} %query_ref.1) | copy-start | bytes 393220
  23.9 47.1 %copy-start.4 = (s32[2,2]{1,0:T(2,128)S(1)}, s32[2,2]{1,0:T(2,128)}, u32[]{:S(2)}) copy-start(s32[2,2]{1,0:T(2,128)} %table_ref.1) | copy-start | bytes 52
  92.5 2.2 %copy-start = (bf16[16384,128]{1,0:T(8,128)(2,1)S(1)}, bf16[16384,128]{1,0:T(8,128)(2,1)}, u32[]{:S(2)}) copy-start(bf16[16384,128]{1,0:T(8,128)(2,1)} %all-gather.3.cloned.1.call-done) | copy-start | bytes 12582916
Sparse Core Ops, SparseCore 0:
  21.9 58.7 all-gather.2

commit v3 on v2

--- a/solution.py
+++ b/solution.py
@@ -121,68 +121,82 @@
     )(folded)
 
 
+def pack_kernel(query_ref, key_ref, value_ref, out_ref):
+    groups, _, _, span = out_ref.shape
+    for kind, ref in enumerate((query_ref, key_ref, value_ref)):
+        for g in range(groups):
+            out_ref[g, kind] = ref[:, g * span : (g + 1) * span]
+
+
+def pack(query, key, value, groups):
+    rows, cols = query.shape
+    return pl.pallas_call(
+        pack_kernel,
+        out_shape=jax.ShapeDtypeStruct((groups, 3, rows, cols // groups), query.dtype),
+        in_specs=[VMEM] * 3,
+        out_specs=VMEM,
+        compiler_params=PARAMS,
+    )(query, key, value)
+
+
 def project_kernel(context_ref, weight_ref, out_ref):
-    sides, quarters, tokens, span = context_ref.shape
-    half = tokens // 2
+    quarters, _, span = context_ref.shape
+    _, sides, _, width = weight_ref.shape
     total = None
-    weight = jnp.concatenate([weight_ref[0], weight_ref[1]], axis=1)
     for q in range(quarters):
-        left = jnp.concatenate([context_ref[s, q] for s in range(sides)], axis=0)
-        term = jnp.dot(
-            left, weight[q * span : (q + 1) * span], preferred_element_type=jnp.float32
+        rows = slice(q * span, (q + 1) * span)
+        right = jnp.concatenate([weight_ref[0, s, rows] for s in range(sides)], axis=1)
+        term = jnp.dot(context_ref[q], right, preferred_element_type=jnp.float32)
+        total = term if total is None else total + term
+    total = total.astype(jnp.bfloat16)
+    middle = width // 2
+    for piece in range(2):
+        out_ref[piece] = jnp.concatenate(
+            [
+                total[:, s * width + piece * middle : s * width + (piece + 1) * middle]
+                for s in range(sides)
+            ],
+            axis=1,
         )
-        total = term if total is None else total + term
-    width = weight_ref.shape[2]
-    for s in range(sides):
-        upper = total[s * tokens : s * tokens + half].astype(jnp.bfloat16)
-        lower = total[s * tokens + half : (s + 1) * tokens].astype(jnp.bfloat16)
-        for piece in range(out_ref.shape[1]):
-            cols = slice(piece * width // 2, (piece + 1) * width // 2)
-            out_ref[s, piece] = jnp.concatenate([upper[:, cols], lower[:, cols]], axis=1)
 
 
 def project(context, weight):
-    sides, quarters, tokens, span = context.shape
-    planes, depth, width = weight.shape
+    quarters, tokens, span = context.shape
+    planes, sides, depth, width = weight.shape
     return pl.pallas_call(
         project_kernel,
-        grid=(planes // 2,),
-        out_shape=jax.ShapeDtypeStruct((sides, 2 * planes, tokens // 2, width), jnp.bfloat16),
+        grid=(planes,),
+        out_shape=jax.ShapeDtypeStruct((2 * planes, tokens, width), jnp.bfloat16),
         in_specs=[
-            pl.BlockSpec(context.shape, lambda i: (0, 0, 0, 0)),
-            pl.BlockSpec((2, depth, width), lambda i: (i, 0, 0)),
+            pl.BlockSpec(context.shape, lambda i: (0, 0, 0)),
+            pl.BlockSpec((1, sides, depth, width), lambda i: (i, 0, 0, 0)),
         ],
-        out_specs=pl.BlockSpec((sides, 4, tokens // 2, width), lambda i: (0, i, 0, 0)),
-        compiler_params=PARAMS,
+        out_specs=pl.BlockSpec((2, tokens, width), lambda i: (i, 0, 0)),
+        compiler_params=pltpu.CompilerParams(vmem_limit_bytes=56 * 2**20),
     )(context, weight)
 
 
 def add_kernel(partial_ref, out_ref):
-    sides, senders, quarters, half, width = partial_ref.shape
-    for s in range(sides):
-        for pair in range(quarters // 2):
-            sums = []
-            for q in (2 * pair, 2 * pair + 1):
-                total = partial_ref[s, 0, q].astype(jnp.float32)
-                for sender in range(1, senders):
-                    total += partial_ref[s, sender, q].astype(jnp.float32)
-                sums.append(total.astype(jnp.bfloat16))
-            first, second = sums
-            middle = width // 2
+    senders, quarters, _, width = partial_ref.shape
+    middle = width // 2
+    for pair in range(quarters // 2):
+        sums = []
+        for q in (2 * pair, 2 * pair + 1):
+            total = partial_ref[0, q].astype(jnp.float32)
+            for sender in range(1, senders):
+                total += partial_ref[sender, q].astype(jnp.float32)
+            sums.append(total.astype(jnp.bfloat16))
+        for s in range(2):
+            part = slice(s * middle, (s + 1) * middle)
             cols = pl.ds((s * (quarters // 2) + pair) * width, width)
-            out_ref[:half, cols] = jnp.concatenate(
-                [first[:, :middle], second[:, :middle]], axis=1
-            )
-            out_ref[half:, cols] = jnp.concatenate(
-                [first[:, middle:], second[:, middle:]], axis=1
-            )
+            out_ref[:, cols] = jnp.concatenate([one[:, part] for one in sums], axis=1)
 
 
 def add(partial):
-    sides, _, quarters, half, width = partial.shape
+    _, quarters, tokens, width = partial.shape
     return pl.pallas_call(
         add_kernel,
-        out_shape=jax.ShapeDtypeStruct((2 * half, sides * quarters * width // 2), jnp.bfloat16),
+        out_shape=jax.ShapeDtypeStruct((tokens, quarters * width), jnp.bfloat16),
         in_specs=[VMEM],
         out_specs=VMEM,
         compiler_params=PARAMS,
@@ -207,21 +221,15 @@
     folded = fold(output_weight, 2, 4)
     shape = folded.shape
     folded = exchange(folded.reshape(8, *shape[2:]), ("yl", "x")).reshape(shape)
-    weight = lax.all_gather(unfold(folded), "z", axis=0, tiled=False)
-
-    rows, all_cols = neighbour_query.shape
-    span = all_cols // groups
-    neighbours = jnp.stack([neighbour_query, neighbour_key, neighbour_value])
-    neighbours = neighbours.reshape(3, rows, groups, span).transpose(2, 0, 1, 3)
+    weight = lax.all_gather(unfold(folded), ("z", "c"), axis=0, tiled=False)
+    weight = weight.reshape(8, 2, *weight.shape[1:])
+
+    neighbours = pack(neighbour_query, neighbour_key, neighbour_value, groups)
     neighbours = exchange(neighbours, TENSOR)
-
-    context = attention(neighbour_table, decoder_query, decoder_memory, neighbours, 8)
-    context = exchange(context, ("c", "x"))
-    context = context.reshape(2, 4, *context.shape[1:])
-    partial = project(context, weight)
-    shape = partial.shape
-    partial = exchange(partial.reshape(2 * groups, *shape[2:]), ("c", "yh", "x"))
-    return add(partial.reshape(2, 4, 4, *shape[2:]))
+    context = attention(neighbour_table, decoder_query, decoder_memory, neighbours, 4)
+    context = exchange(context, "x")
+    partial = exchange(project(context, weight), TENSOR)
+    return add(partial.reshape(4, 4, *partial.shape[1:]))
 
 
 def solution(mesh):

time: 128 us -> 129 us (level)
  the two profiles are of different devices: /device:TPU:201 before, /device:TPU:1 now
where the time goes in v3:
time: 129 us; the launch traced here: 128 us
  blocking collectives  91 us (71%)
  between operations  13.5 us (10%)
  Pallas kernels  12.8 us (10%)
  waiting for transfers between devices  9.68 us (8%)
    all_to_all x4, blocking collectives, exchange(): return lax.all_to_all(value, axes, split_axis=0, concat_axis=0, tiled=True)  91 us
    all_gather x1, waiting for transfers between devices, local(): weight = lax.all_gather(unfold(folded), ('z', 'c'), axis=0, tiled=False)  9.67 us
    pallas_call x1, Pallas kernels, project(): pl.pallas_call(project_kernel, grid=(planes,), out_shape=jax.ShapeDtypeSt...  8.1 us
    pallas_call x1, Pallas kernels, attention(): pl.pallas_call(attention_kernel, out_shape=jax.ShapeDtypeStruct((copies,...  2.59 us
  transfers between devices with their start and end apart: 1, of which 1 were waited for; matrix products, arithmetic and copies ran while one was open for 0% of the time, Pallas kernels for 2%

profile of v3, /device:TPU:1, one launch (start us, length us, event | category | flops | bytes accessed | tf_op | source)
XLA Modules:
  0.0 128.0 jit_solution(16914636761465657185)
XLA Ops:
  6.5 0.0 copy-start.1
  6.5 0.0 all-gather.3.cloned.1.call-start
  6.5 1.1 copy-done.3
  7.6 0.1 shard_map.75
  7.8 13.1 %all_to_all.20 = bf16[8,256,128]{2,1,0:T(8,128)(2,1)S(1)} all-to-all(bf16[8,256,128]{2,1,0:T(8,128)(2,1)S(1)} %bitcast.6), channel_id=1, replica_groups=mesh['z'=8,'yl'=2,'c'=2,'yh'=4,'x'=4] {'yl','x'}, dimensions={0} | all-to-all | bytes 1048576 | tf_op jit(solution)/shard_map/all_to_all | solution.py:207
  20.9 1.0 shard_map.76
  21.9 0.0 all-gather.3.cloned.1.call-update
  22.0 0.0 copy-done.1
  22.0 0.0 copy-done.2
  22.0 0.0 copy-done
  22.0 0.1 shard_map.73
  22.1 0.0 copy-start.4
  22.1 0.0 copy-start.5
  22.1 0.0 copy-start.6
  22.1 41.4 %all_to_all.21.nbr_ref = bf16[16,3,32,512]{3,2,1,0:T(8,128)(2,1)S(1)} all-to-all(bf16[16,3,32,512]{3,2,1,0:T(8,128)(2,1)S(1)} %shard_map.73), channel_id=1, replica_groups=mesh['z'=8,'yl'=2,'c'=2,'yh'=4,'x'=4] {'yh','x'}, dimensions={0} | all-to-all | bytes 3145728 | tf_op jit(solution)/shard_map/all_to_all | solution.py:207
  63.5 0.0 copy-done.4
  63.5 0.0 copy-done.5
  63.5 0.0 copy-done.6
  63.5 2.6 %shard_map.74 = bf16[4,128,512]{2,1,0:T(8,128)(2,1)S(1)} custom-call(s32[2,2]{1,0:T(2,128)S(1)} %copy-done.6, bf16[128,512]{1,0:T(8,128)(2,1)S(1)} %copy-done.5, bf16[2,128,512]{2,1,0:T(8,128)(2,1)S(1)} %copy-done.4, bf16[16,3,32,512]{3,2,1,0:T(8,128)(2,1)S(1)} %all_to_all.21.nbr_ref), custom_call_target="tpu_custom_call" | custom-call | tf_op jit(solution)/shard_map/pallas_call | solution.py:71
  66.1 10.6 %all_to_all.22.context_ref = bf16[4,128,512]{2,1,0:T(8,128)(2,1)} all-to-all(bf16[4,128,512]{2,1,0:T(8,128)(2,1)S(1)} %shard_map.74), channel_id=1, replica_groups=mesh['z'=8,'yl'=2,'c'=2,'yh'=4,'x'=4] {'x'}, dimensions={0} | all-to-all | bytes 1048576 | tf_op jit(solution)/shard_map/all_to_all | solution.py:207
  76.7 9.7 %all-gather.3.cloned.1.call-done = bf16[32768,128]{1,0:T(8,128)(2,1)} async-done(((bf16[2048,128]{1,0:T(8,128)(2,1)}), bf16[32768,128]{1,0:T(8,128)(2,1)}) %all-gather.3.cloned.1.call-update) | async-done | bytes 8388624 | tf_op jit(solution)/shard_map/all_gather | solution.py:224
  86.4 8.1 %shard_map.77 = bf16[16,128,128]{2,1,0:T(8,128)(2,1)} custom-call(bf16[4,128,512]{2,1,0:T(8,128)(2,1)} %all_to_all.22.context_ref, bf16[8,2,2048,128]{3,2,1,0:T(8,128)(2,1)} %bitcast.7), custom_call_target="tpu_custom_call" | custom-call | tf_op jit(solution)/shard_map/pallas_call | solution.py:166
  94.5 25.9 %all_to_all.23 = bf16[16,128,128]{2,1,0:T(8,128)(2,1)S(1)} all-to-all(bf16[16,128,128]{2,1,0:T(8,128)(2,1)} %shard_map.77), channel_id=1, replica_groups=mesh['z'=8,'yl'=2,'c'=2,'yh'=4,'x'=4] {'yh','x'}, dimensions={0} | all-to-all | bytes 1048576 | tf_op jit(solution)/shard_map/all_to_all | solution.py:207
  120.4 0.8 shard_map.78
  (3 shorter events, 0.0 us)
Async XLA Ops:
  6.5 15.4 %copy-start.1 = (bf16[32,8192]{1,0:T(8,128)(2,1)S(1)}, bf16[32,8192]{1,0:T(8,128)(2,1)}, u32[]{:S(2)}) copy-start(bf16[32,8192]{1,0:T(8,128)(2,1)} %key_ref.1) | copy-start | bytes 1572868
  6.5 15.4 %copy-start.2 = (bf16[32,8192]{1,0:T(8,128)(2,1)S(1)}, bf16[32,8192]{1,0:T(8,128)(2,1)}, u32[]{:S(2)}) copy-start(bf16[32,8192]{1,0:T(8,128)(2,1)} %value_ref.1) | copy-start | bytes 1572868
  6.5 15.4 %copy-start = (bf16[32,8192]{1,0:T(8,128)(2,1)S(1)}, bf16[32,8192]{1,0:T(8,128)(2,1)}, u32[]{:S(2)}) copy-start(bf16[32,8192]{1,0:T(8,128)(2,1)} %query_ref.2) | copy-start | bytes 1572868
  6.5 79.9 %all-gather.3.cloned.1.call-start = ((), (), s32[]{:S(2)}) async-start(), calls=%async_computation.4 | async-start | bytes 8912896 | tf_op jit(solution)/shard_map/all_gather | solution.py:224
  6.5 1.1 copy-start.3
  22.1 41.4 %copy-start.4 = (bf16[2,128,512]{2,1,0:T(8,128)(2,1)S(1)}, bf16[2,128,512]{2,1,0:T(8,128)(2,1)}, u32[]{:S(2)}) copy-start(bf16[2,128,512]{2,1,0:T(8,128)(2,1)} %memory_ref.1) | copy-start | bytes 786436
  22.1 41.4 %copy-start.5 = (bf16[128,512]{1,0:T(8,128)(2,1)S(1)}, bf16[128,512]{1,0:T(8,128)(2,1)}, u32[]{:S(2)}) copy-start(bf16[128,512]{1,0:T(8,128)(2,1)} %query_ref.3) | copy-start | bytes 393220
  22.1 41.4 %copy-start.6 = (s32[2,2]{1,0:T(2,128)S(1)}, s32[2,2]{1,0:T(2,128)}, u32[]{:S(2)}) copy-start(s32[2,2]{1,0:T(2,128)} %table_ref.1) | copy-start | bytes 52
Sparse Core Ops, SparseCore 0:
  22.1 64.2 all-gather.2

commit v4 on v2

v4 whole, which is shorter than its diff:
```python
import functools
import math

import jax
import jax.numpy as jnp
from jax import lax
from jax.experimental import pallas as pl
from jax.experimental.pallas import tpu as pltpu
from jax.sharding import Mesh
from jax.sharding import PartitionSpec as P

HD = 128
STRETCH = 64
NBLEN = 128
SCALE = 1.0 / math.sqrt(HD)

AXES = ("z", "yl", "c", "yh", "x")
DP = ("z", "yl", "c")
TENSOR = ("yh", "x")


def softmax_rows(scores):
    row_top = jnp.max(scores, axis=-1, keepdims=True)
    expo = jnp.exp(scores - row_top)
    return (expo / jnp.sum(expo, axis=-1, keepdims=True)).astype(jnp.bfloat16)


def rows_times_rows(left, right):
    return lax.dot_general(
        left, right, (((1,), (1,)), ((), ())), preferred_element_type=jnp.float32
    )


def attention_kernel(table_ref, query_ref, memory_ref, nbr_ref, after_ref, out_ref):
    del after_ref
    stretches, per_stretch = table_ref.shape
    pieces = nbr_ref.shape[0] // (stretches * per_stretch)
    heads = query_ref.shape[1] // HD
    for u in range(stretches):
        rows = slice(u * STRETCH, (u + 1) * STRETCH)
        places = [pl.ds(table_ref[u, j] * pieces, pieces) for j in range(per_stretch)]
        for h in range(heads):
            cols = slice(h * HD, (h + 1) * HD)
            nbr_query, nbr_key, nbr_value = (
                jnp.concatenate(
                    [nbr_ref[place, kind, :, cols].reshape(NBLEN, HD) for place in places],
                    axis=0,
                )
                for kind in range(3)
            )
            enc_probs = softmax_rows(
                rows_times_rows(nbr_query, memory_ref[0, rows, cols]) * SCALE
            )
            encoded = nbr_value.astype(jnp.float32) + jnp.dot(
                enc_probs, memory_ref[1, rows, cols], preferred_element_type=jnp.float32
            )
            encoded = encoded.astype(jnp.bfloat16)
            dec_probs = softmax_rows(
                rows_times_rows(query_ref[rows, cols], nbr_key) * SCALE
            )
            context = jnp.dot(dec_probs, encoded, preferred_element_type=jnp.float32)
            context = context.astype(jnp.bfloat16)
            for copy in range(out_ref.shape[0]):
                out_ref[copy, rows, cols] = context


VMEM = pl.BlockSpec(memory_space=pltpu.VMEM)
ANY = pl.BlockSpec(memory_space=pl.ANY)
PARAMS = pltpu.CompilerParams(vmem_limit_bytes=32 * 2**20)


def attention(table, query, memory, neighbours, copies, after):
    return pl.pallas_call(
        attention_kernel,
        out_shape=jax.ShapeDtypeStruct((copies, *query.shape), jnp.bfloat16),
        in_specs=[pl.BlockSpec(memory_space=pltpu.SMEM)] + [VMEM] * 3 + [ANY],
        out_specs=VMEM,
        compiler_params=PARAMS,
    )(table, query, memory, neighbours, after)


def pack_kernel(query_ref, key_ref, value_ref, out_ref):
    groups, _, _, span = out_ref.shape
    for kind, ref in enumerate((query_ref, key_ref, value_ref)):
        for g in range(groups):
            out_ref[g, kind] = ref[:, g * span : (g + 1) * span]


def pack(query, key, value, groups):
    rows, cols = query.shape
    return pl.pallas_call(
        pack_kernel,
        out_shape=jax.ShapeDtypeStruct((groups, 3, rows, cols // groups), query.dtype),
        in_specs=[VMEM] * 3,
        out_specs=VMEM,
        compiler_params=PARAMS,
    )(query, key, value)


def fold_kernel(weight_ref, out_ref):
    eighths, quarter, width = out_ref.shape
    part = weight_ref.shape[1] // eighths
    for e in range(eighths):
        cols = slice(e * part, (e + 1) * part)
        out_ref[e] = jnp.concatenate(
            [weight_ref[k * quarter : (k + 1) * quarter, cols] for k in range(width // part)],
            axis=1,
        )


def fold(weight, eighths):
    rows, cols = weight.shape
    part = cols // eighths
    return pl.pallas_call(
        fold_kernel,
        out_shape=jax.ShapeDtypeStruct((eighths, rows * part // HD, HD), weight.dtype),
        in_specs=[VMEM],
        out_specs=VMEM,
        compiler_params=PARAMS,
    )(weight)


def regroup_kernel(folded_ref, out_ref):
    senders, quarters, quarter, width = folded_ref.shape
    part = width // 4
    for x in range(quarters):
        for k in range(2):
            out_ref[x, k * quarter : (k + 1) * quarter] = jnp.concatenate(
                [
                    folded_ref[s, x, :, at * part : (at + 1) * part]
                    for at in (k, 2 + k)
                    for s in range(senders)
                ],
                axis=1,
            )


def regroup(folded):
    _, quarters, quarter, width = folded.shape
    return pl.pallas_call(
        regroup_kernel,
        out_shape=jax.ShapeDtypeStruct((quarters, 2 * quarter, width), folded.dtype),
        in_specs=[VMEM],
        out_specs=VMEM,
        compiler_params=PARAMS,
    )(folded)


def stack_kernel(*refs):
    out_ref = refs[-1]
    place = 0
    quarters = out_ref.shape[1]
    for ref in refs[:-1]:
        count = ref.shape[0]
        out_ref[place // quarters, pl.ds(place % quarters, count)] = ref[...]
        place += count


def stack(quarters, *values):
    count = sum(value.shape[0] for value in values) // quarters
    return pl.pallas_call(
        stack_kernel,
        out_shape=jax.ShapeDtypeStruct(
            (count, quarters, *values[0].shape[1:]), values[0].dtype
        ),
        in_specs=[VMEM] * len(values),
        out_specs=VMEM,
        compiler_params=PARAMS,
    )(*values)


def project_kernel(plane_ref, context_ref, near_ref, far_ref, near_sib_ref, far_sib_ref, out_ref):
    plane = plane_ref[0]
    sides, quarters, tokens, span = context_ref.shape
    width = near_ref.shape[-1]
    middle, half, part = width // 2, tokens // 2, width // 4
    blocks = [(near_ref, near_sib_ref, i) for i in range(near_ref.shape[0])]
    blocks += [(far_ref, far_sib_ref, i) for i in range(far_ref.shape[0])]
    planes = len(blocks)
    left = [
        jnp.concatenate([context_ref[s, x] for s in range(sides)], axis=0)
        for x in range(quarters)
    ]

    def rows_of(index, x):
        own_ref, sib_ref, i = blocks[index]
        own, sib = own_ref[i, x], sib_ref[i, x]
        upper = jnp.concatenate([own[:, :middle], sib[:, :middle]], axis=1)
        lower = jnp.concatenate([own[:, middle:], sib[:, middle:]], axis=1)
        return jnp.concatenate([upper, lower], axis=0)

    for pair in range(planes // 2):
        total = None
        for x in range(quarters):
            right = jnp.concatenate([rows_of(2 * pair, x), rows_of(2 * pair + 1, x)], axis=1)
            term = jnp.dot(left[x], right, preferred_element_type=jnp.float32)
            total = term if total is None else total + term
        total = total.astype(jnp.bfloat16)
        for s in range(sides):
            upper = total[s * tokens : s * tokens + half]
            lower = total[s * tokens + half : (s + 1) * tokens]
            for i in range(2):
                target = lax.rem(plane + OFFSETS[2 * pair + i] + planes, planes)
                for piece in range(2):
                    own = slice(i * width + piece * part, i * width + (piece + 1) * part)
                    sib = slice(own.start + middle, own.stop + middle)
                    out_ref[s, 2 * target + piece] = jnp.concatenate(
                        [upper[:, own], upper[:, sib], lower[:, own], lower[:, sib]], axis=1
                    )


def project(plane, context, near, far, near_sib, far_sib):
    sides, _, tokens, _ = context.shape
    planes = near.shape[0] + far.shape[0]
    return pl.pallas_call(
        project_kernel,
        out_shape=jax.ShapeDtypeStruct(
            (sides, 2 * planes, tokens // 2, near.shape[-1]), jnp.bfloat16
        ),
        in_specs=[pl.BlockSpec(memory_space=pltpu.SMEM)] + [VMEM] * 5,
        out_specs=VMEM,
        compiler_params=PARAMS,
    )(plane, context, near, far, near_sib, far_sib)


def add_kernel(core_ref, partial_ref, out_ref):
    sides, senders, quarters, half, width = partial_ref.shape
    middle, part = width // 2, width // 4
    for s in range(sides):
        sums = []
        for x in range(quarters):
            total = partial_ref[s, 0, x].astype(jnp.float32)
            for sender in range(1, senders):
                total += partial_ref[s, sender, x].astype(jnp.float32)
            sums.append(total.astype(jnp.bfloat16))
        for side in range(2):
            core = core_ref[0] if side == 0 else 1 - core_ref[0]
            cols = pl.ds(pl.multiple_of((core * sides + s) * width, width), width)
            for low in range(2):
                at = low * middle + side * part
                out_ref[low * half : (low + 1) * half, cols] = jnp.concatenate(
                    [one[:, at : at + part] for one in sums], axis=1
                )


def add(core, partial):
    sides, _, quarters, half, width = partial.shape
    return pl.pallas_call(
        add_kernel,
        out_shape=jax.ShapeDtypeStruct((2 * half, sides * quarters * width // 2), jnp.bfloat16),
        in_specs=[pl.BlockSpec(memory_space=pltpu.SMEM), VMEM],
        out_specs=VMEM,
        compiler_params=PARAMS,
    )(core, partial)


def exchange(value, axes):
    return lax.all_to_all(value, axes, split_axis=0, concat_axis=0, tiled=True)


OFFSETS = (0, -1, 1, -2, 2, -3, 3, 4)


def ring(value, axis, size):
    up = [(i, (i + 1) % size) for i in range(size)]
    down = [(i, (i - 1) % size) for i in range(size)]
    behind, ahead = [value], [value]
    for _ in range(size // 2 - 1):
        behind.append(lax.ppermute(behind[-1], axis, up))
        ahead.append(lax.ppermute(ahead[-1], axis, down))
    half = value.shape[0] // 2
    top = lax.ppermute(behind[-1][:half], axis, up)
    low = lax.ppermute(ahead[-1][half:], axis, down)
    near = stack(len(value), value, behind[1], ahead[1], behind[2], ahead[2], behind[3], ahead[3])
    far = stack(len(value), top, low)
    return near, far


def local(
    decoder_query,
    decoder_memory,
    neighbour_query,
    neighbour_key,
    neighbour_value,
    neighbour_table,
    output_weight,
    *,
    groups,
):
    folded = exchange(fold(output_weight, 8), ("yl", "x"))
    near, far = ring(regroup(folded.reshape(2, 4, *folded.shape[1:])), "z", 8)
    swap = [(0, 1), (1, 0)]
    near_sib, far_sib = lax.ppermute(near, "c", swap), lax.ppermute(far, "c", swap)

    neighbours = pack(neighbour_query, neighbour_key, neighbour_value, groups)
    neighbours = exchange(neighbours, TENSOR)
    context = attention(neighbour_table, decoder_query, decoder_memory, neighbours, 8, near)
    context = exchange(context, ("yl", "x"))
    context = context.reshape(2, 4, *context.shape[1:])
    plane = lax.axis_index("z").astype(jnp.int32).reshape(1)
    partial = project(plane, context, near, far, near_sib, far_sib)
    shape = partial.shape
    partial = exchange(partial.reshape(2 * groups, *shape[2:]), ("yl", "yh", "x"))
    core = lax.axis_index("c").astype(jnp.int32).reshape(1)
    return add(core, partial.reshape(2, 4, 4, *shape[2:]))


def solution(mesh):
    groups = mesh.shape["tensor"]
    inner = Mesh(mesh.devices.reshape(8, 2, 2, 4, 4), AXES)
    return jax.shard_map(
        functools.partial(local, groups=groups),
        mesh=inner,
        in_specs=(
            P(DP, TENSOR),
            P(None, DP, TENSOR),
            P(AXES, None),
            P(AXES, None),
            P(AXES, None),
            P(DP, None),
            P(TENSOR, DP),
        ),
        out_specs=P(DP, TENSOR),
        check_vma=False,
    )
```

time: 128 us -> 125 us (0.977)
  the two profiles are of different devices: /device:TPU:201 before, /device:TPU:8 now
where the time goes in v4:
time: 125 us; the launch traced here: 124 us
  starting transfers between devices  67.2 us (54%)
  waiting for transfers between devices  39.6 us (32%)
  Pallas kernels  9.93 us (8%)
  local copies, waits for them, and re-layouts  6.61 us (5%)
    all_to_all x4, starting transfers between devices, exchange(): return lax.all_to_all(value, axes, split_axis=0, concat_axis=0, tiled=True)  26.1 us
    ppermute x3, starting transfers between devices, ring(): ahead.append(lax.ppermute(ahead[-1], axis, down))  22.3 us
    all_to_all x4, waiting for transfers between devices, exchange(): return lax.all_to_all(value, axes, split_axis=0, concat_axis=0, tiled=True)  19.7 us
    ppermute x1, starting transfers between devices, ring(): low = lax.ppermute(ahead[-1][half:], axis, down)  7.4 us
    ppermute x3, waiting for transfers between devices, ring(): ahead.append(lax.ppermute(ahead[-1], axis, down))  6.63 us
    unnamed x24, local copies, waits for them, and re-layouts  6.59 us
    ppermute x3, starting transfers between devices, ring(): behind.append(lax.ppermute(behind[-1], axis, up))  5.75 us
    ppermute x3, waiting for transfers between devices, ring(): behind.append(lax.ppermute(behind[-1], axis, up))  5.64 us
  transfers between devices with their start and end apart: 14, of which 9 were waited for; matrix products, arithmetic and copies ran while one was open for 0% of the time, Pallas kernels for 3%

profile of v4, /device:TPU:8, one launch (start us, length us, event | category | flops | bytes accessed | tf_op | source)
XLA Modules:
  0.0 123.6 jit_solution(13972020555504325244)
XLA Ops:
  1.9 9.2 %all-to-all-start.1 = ((bf16[8,128,128]{2,1,0:T(8,128)(2,1)}), bf16[8,128,128]{2,1,0:T(8,128)(2,1)S(1)}, u32[]{:S(2)}, u32[]{:S(2)}) async-start(bf16[8,128,128]{2,1,0:T(8,128)(2,1)} %shard_map.74), calls=%async_computation.1 | async-start | bytes 524288 | tf_op jit(solution)/shard_map/all_to_all | solution.py:258
  15.5 1.4 %all-to-all-done.1 = bf16[8,128,128]{2,1,0:T(8,128)(2,1)S(1)} async-done(((bf16[8,128,128]{2,1,0:T(8,128)(2,1)}), bf16[8,128,128]{2,1,0:T(8,128)(2,1)S(1)}, u32[]{:S(2)}, u32[]{:S(2)}) %all-to-all-start.1) | async-done | bytes 262176 | tf_op jit(solution)/shard_map/all_to_all | solution.py:258
  16.9 3.9 %all-to-all-start = ((bf16[16,3,32,512]{3,2,1,0:T(8,128)(2,1)}), bf16[16,3,32,512]{3,2,1,0:T(8,128)(2,1)S(1)}, u32[]{:S(2)}, u32[]{:S(2)}) async-start(bf16[16,3,32,512]{3,2,1,0:T(8,128)(2,1)} %shard_map.73), calls=%async_computation | async-start | bytes 3145728 | tf_op jit(solution)/shard_map/all_to_all | solution.py:258
  21.0 11.1 %collective-permute-start.1 = (bf16[4,256,128]{2,1,0:T(8,128)(2,1)S(1)}, bf16[4,256,128]{2,1,0:T(8,128)(2,1)S(1)}, u32[]{:S(2)}, u32[]{:S(2)}) collective-permute-start(bf16[4,256,128]{2,1,0:T(8,128)(2,1)S(1)} %shard_map.75.refs_0_), channel_id=1, source_target_pairs={{0,448},{64,0},{128,64},{192,128},{256,192},{320,256},{384,320},{4... | collective-permute-start | bytes 786440 | tf_op jit(solution)/shard_map/ppermute | solution.py:270
  32.1 1.9 %collective-permute-start = (bf16[4,256,128]{2,1,0:T(8,128)(2,1)S(1)}, bf16[4,256,128]{2,1,0:T(8,128)(2,1)S(1)}, u32[]{:S(2)}, u32[]{:S(2)}) collective-permute-start(bf16[4,256,128]{2,1,0:T(8,128)(2,1)S(1)} %shard_map.75.refs_0_), channel_id=1, source_target_pairs={{0,64},{64,128},{128,192},{192,256},{256,320},{320,384},{384,448},... | collective-permute-start | bytes 786440 | tf_op jit(solution)/shard_map/ppermute | solution.py:269
  34.0 2.8 %collective-permute-done.1.refs_2_ = bf16[4,256,128]{2,1,0:T(8,128)(2,1)S(1)} collective-permute-done((bf16[4,256,128]{2,1,0:T(8,128)(2,1)S(1)}, bf16[4,256,128]{2,1,0:T(8,128)(2,1)S(1)}, u32[]{:S(2)}, u32[]{:S(2)}) %collective-permute-start.1) | collective-permute-done | bytes 262176 | tf_op jit(solution)/shard_map/ppermute | solution.py:270
  36.8 5.6 %collective-permute-start.3 = (bf16[4,256,128]{2,1,0:T(8,128)(2,1)S(1)}, bf16[4,256,128]{2,1,0:T(8,128)(2,1)S(1)}, u32[]{:S(2)}, u32[]{:S(2)}) collective-permute-start(bf16[4,256,128]{2,1,0:T(8,128)(2,1)S(1)} %collective-permute-done.1.refs_2_), channel_id=1, source_target_pairs={{0,448},{64,0},{128,64},{192,128},{256,192},{320,256},{384,320},{4... | collective-permute-start | bytes 786440 | tf_op jit(solution)/shard_map/ppermute | solution.py:270
  42.4 1.9 %collective-permute-start.2 = (bf16[4,256,128]{2,1,0:T(8,128)(2,1)S(1)}, bf16[4,256,128]{2,1,0:T(8,128)(2,1)S(1)}, u32[]{:S(2)}, u32[]{:S(2)}) collective-permute-start(bf16[4,256,128]{2,1,0:T(8,128)(2,1)S(1)} %collective-permute-done.refs_1_), channel_id=1, source_target_pairs={{0,64},{64,128},{128,192},{192,256},{256,320},{320,384},{384,448},... | collective-permute-start | bytes 786440 | tf_op jit(solution)/shard_map/ppermute | solution.py:269
  44.3 1.9 %collective-permute-done.3.refs_4_ = bf16[4,256,128]{2,1,0:T(8,128)(2,1)S(1)} collective-permute-done((bf16[4,256,128]{2,1,0:T(8,128)(2,1)S(1)}, bf16[4,256,128]{2,1,0:T(8,128)(2,1)S(1)}, u32[]{:S(2)}, u32[]{:S(2)}) %collective-permute-start.3) | collective-permute-done | bytes 262176 | tf_op jit(solution)/shard_map/ppermute | solution.py:270
  46.2 5.6 %collective-permute-start.5 = (bf16[4,256,128]{2,1,0:T(8,128)(2,1)S(1)}, bf16[4,256,128]{2,1,0:T(8,128)(2,1)S(1)}, u32[]{:S(2)}, u32[]{:S(2)}) collective-permute-start(bf16[4,256,128]{2,1,0:T(8,128)(2,1)S(1)} %collective-permute-done.3.refs_4_), channel_id=1, source_target_pairs={{0,448},{64,0},{128,64},{192,128},{256,192},{320,256},{384,320},{4... | collective-permute-start | bytes 786440 | tf_op jit(solution)/shard_map/ppermute | solution.py:270
  51.8 1.9 %collective-permute-start.4 = (bf16[4,256,128]{2,1,0:T(8,128)(2,1)S(1)}, bf16[4,256,128]{2,1,0:T(8,128)(2,1)S(1)}, u32[]{:S(2)}, u32[]{:S(2)}) collective-permute-start(bf16[4,256,128]{2,1,0:T(8,128)(2,1)S(1)} %collective-permute-done.2.refs_3_), channel_id=1, source_target_pairs={{0,64},{64,128},{128,192},{192,256},{256,320},{320,384},{384,448},... | collective-permute-start | bytes 786440 | tf_op jit(solution)/shard_map/ppermute | solution.py:269
  53.8 1.9 %collective-permute-done.5.refs_6_ = bf16[4,256,128]{2,1,0:T(8,128)(2,1)S(1)} collective-permute-done((bf16[4,256,128]{2,1,0:T(8,128)(2,1)S(1)}, bf16[4,256,128]{2,1,0:T(8,128)(2,1)S(1)}, u32[]{:S(2)}, u32[]{:S(2)}) %collective-permute-start.5) | collective-permute-done | bytes 262176 | tf_op jit(solution)/shard_map/ppermute | solution.py:270
  55.7 5.6 %collective-permute-done.4.refs_5_ = bf16[4,256,128]{2,1,0:T(8,128)(2,1)S(1)} collective-permute-done((bf16[4,256,128]{2,1,0:T(8,128)(2,1)S(1)}, bf16[4,256,128]{2,1,0:T(8,128)(2,1)S(1)}, u32[]{:S(2)}, u32[]{:S(2)}) %collective-permute-start.4) | collective-permute-done | bytes 262176 | tf_op jit(solution)/shard_map/ppermute | solution.py:269
  62.0 1.9 %collective-permute-start.8 = (bf16[7,4,256,128]{3,2,1,0:T(8,128)(2,1)S(1)}, bf16[7,4,256,128]{3,2,1,0:T(8,128)(2,1)}, u32[]{:S(2)}, u32[]{:S(2)}) collective-permute-start(bf16[7,4,256,128]{3,2,1,0:T(8,128)(2,1)S(1)} %shard_map.76.after_ref.near_ref), channel_id=1, source_target_pairs={{0,16},{16,0},{1,17},{17,1},{2,18},{18,2},{3,19},{19,3},{4,20},{20... | collective-permute-start | bytes 5505032 | tf_op jit(solution)/shard_map/ppermute | solution.py:293
  64.9 2.6 %shard_map.77 = bf16[8,128,512]{2,1,0:T(8,128)(2,1)S(1)} custom-call(s32[2,2]{1,0:T(2,128)S(1)} %copy-done.11, bf16[128,512]{1,0:T(8,128)(2,1)S(1)} %copy-done.10, bf16[2,128,512]{2,1,0:T(8,128)(2,1)S(1)} %copy-done.9, bf16[16,3,32,512]{3,2,1,0:T(8,128)(2,1)S(1)} %all-to-all-done.nbr_ref, bf16[7,4,256,128]{3,2,1,0:T(8,128)(2,1)S(1)} %shard_map.76.after_ref.near_ref), custom_call_target="tpu_custom_call" | custom-call | tf_op jit(solution)/shard_map/pallas_call | solution.py:73
  68.5 6.0 %all-to-all-start.2 = ((bf16[8,128,512]{2,1,0:T(8,128)(2,1)}), bf16[8,128,512]{2,1,0:T(8,128)(2,1)S(1)}, u32[]{:S(2)}, u32[]{:S(2)}) async-start(bf16[8,128,512]{2,1,0:T(8,128)(2,1)} %copy-done), calls=%async_computation.2 | async-start | bytes 2097152 | tf_op jit(solution)/shard_map/all_to_all | solution.py:258
  74.6 7.4 %collective-permute-start.7 = (bf16[2,256,128]{2,1,0:T(8,128)(2,1)S(1)}, bf16[2,256,128]{2,1,0:T(8,128)(2,1)S(1)}, u32[]{:S(2)}, u32[]{:S(2)}) collective-permute-start(bf16[2,256,128]{2,1,0:T(8,128)(2,1)S(1)} %slice.9), channel_id=1, source_target_pairs={{0,448},{64,0},{128,64},{192,128},{256,192},{320,256},{384,320},{4... | collective-permute-start | bytes 393224 | tf_op jit(solution)/shard_map/ppermute | solution.py:273
  82.0 1.9 %collective-permute-start.6 = (bf16[2,256,128]{2,1,0:T(8,128)(2,1)S(1)}, bf16[2,256,128]{2,1,0:T(8,128)(2,1)S(1)}, u32[]{:S(2)}, u32[]{:S(2)}) collective-permute-start(bf16[2,256,128]{2,1,0:T(8,128)(2,1)S(1)} %slice.8), channel_id=1, source_target_pairs={{0,64},{64,128},{128,192},{192,256},{256,320},{320,384},{384,448},... | collective-permute-start | bytes 393224 | tf_op jit(solution)/shard_map/ppermute | solution.py:272
  84.6 5.5 %collective-permute-done.6.refs_0_ = bf16[2,256,128]{2,1,0:T(8,128)(2,1)S(1)} collective-permute-done((bf16[2,256,128]{2,1,0:T(8,128)(2,1)S(1)}, bf16[2,256,128]{2,1,0:T(8,128)(2,1)S(1)}, u32[]{:S(2)}, u32[]{:S(2)}) %collective-permute-start.6) | collective-permute-done | bytes 131104 | tf_op jit(solution)/shard_map/ppermute | solution.py:272
  90.1 1.9 %collective-permute-start.9 = (bf16[1,4,256,128]{3,2,1,0:T(8,128)(2,1)S(1)}, bf16[1,4,256,128]{3,2,1,0:T(8,128)(2,1)S(1)}, u32[]{:S(2)}, u32[]{:S(2)}) collective-permute-start(bf16[1,4,256,128]{3,2,1,0:T(8,128)(2,1)S(1)} %shard_map.78.far_ref), channel_id=1, source_target_pairs={{0,16},{16,0},{1,17},{17,1},{2,18},{18,2},{3,19},{19,3},{4,20},{20... | collective-permute-start | bytes 786440 | tf_op jit(solution)/shard_map/ppermute | solution.py:293
  92.0 1.5 %collective-permute-done.9.far_sib_ref = bf16[1,4,256,128]{3,2,1,0:T(8,128)(2,1)S(1)} collective-permute-done((bf16[1,4,256,128]{3,2,1,0:T(8,128)(2,1)S(1)}, bf16[1,4,256,128]{3,2,1,0:T(8,128)(2,1)S(1)}, u32[]{:S(2)}, u32[]{:S(2)}) %collective-permute-start.9) | collective-permute-done | bytes 262176 | tf_op jit(solution)/shard_map/ppermute | solution.py:293
  93.5 4.0 %shard_map.79 = bf16[2,16,64,128]{3,2,1,0:T(8,128)(2,1)} custom-call(s32[1]{0:T(128)} %bitcast.1.plane_ref, bf16[2,4,128,512]{3,2,1,0:T(8,128)(2,1)S(1)} %bitcast.6, bf16[7,4,256,128]{3,2,1,0:T(8,128)(2,1)S(1)} %shard_map.76.after_ref.near_ref, bf16[1,4,256,128]{3,2,1,0:T(8,128)(2,1)S(1)} %shard_map.78.far_ref, ...), custom_call_target="tpu_custom_call" | custom-call | tf_op jit(solution)/shard_map/pallas_call | solution.py:215
  97.5 7.0 %all-to-all-start.3 = ((bf16[32,64,128]{2,1,0:T(8,128)(2,1)}), bf16[32,64,128]{2,1,0:T(8,128)(2,1)S(1)}, u32[]{:S(2)}, u32[]{:S(2)}) async-start(bf16[32,64,128]{2,1,0:T(8,128)(2,1)} %bitcast.4), calls=%async_computation.3 | async-start | bytes 1048576 | tf_op jit(solution)/shard_map/all_to_all | solution.py:258
  104.5 18.2 %all-to-all-done.3 = bf16[32,64,128]{2,1,0:T(8,128)(2,1)S(1)} async-done(((bf16[32,64,128]{2,1,0:T(8,128)(2,1)}), bf16[32,64,128]{2,1,0:T(8,128)(2,1)S(1)}, u32[]{:S(2)}, u32[]{:S(2)}) %all-to-all-start.3) | async-done | bytes 524320 | tf_op jit(solution)/shard_map/all_to_all | solution.py:258
  (38 shorter events, 10.7 us)
Async XLA Ops:
  1.9 15.0 %all-to-all-start.1 = ((bf16[8,128,128]{2,1,0:T(8,128)(2,1)}), bf16[8,128,128]{2,1,0:T(8,128)(2,1)S(1)}, u32[]{:S(2)}, u32[]{:S(2)}) async-start(bf16[8,128,128]{2,1,0:T(8,128)(2,1)} %shard_map.74), calls=%async_computation.1 | async-start | bytes 524288 | tf_op jit(solution)/shard_map/all_to_all | solution.py:258
  11.1 1.0 copy-start.5
  12.1 1.0 copy-start.6
  13.2 1.0 copy-start.7
  16.9 47.0 %all-to-all-start = ((bf16[16,3,32,512]{3,2,1,0:T(8,128)(2,1)}), bf16[16,3,32,512]{3,2,1,0:T(8,128)(2,1)S(1)}, u32[]{:S(2)}, u32[]{:S(2)}) async-start(bf16[16,3,32,512]{3,2,1,0:T(8,128)(2,1)} %shard_map.73), calls=%async_computation | async-start | bytes 3145728 | tf_op jit(solution)/shard_map/all_to_all | solution.py:258
  20.9 43.0 %copy-start.10 = (bf16[128,512]{1,0:T(8,128)(2,1)S(1)}, bf16[128,512]{1,0:T(8,128)(2,1)}, u32[]{:S(2)}) copy-start(bf16[128,512]{1,0:T(8,128)(2,1)} %query_ref.3) | copy-start | bytes 393220
  21.0 43.0 %copy-start.11 = (s32[2,2]{1,0:T(2,128)S(1)}, s32[2,2]{1,0:T(2,128)}, u32[]{:S(2)}) copy-start(s32[2,2]{1,0:T(2,128)} %table_ref.1) | copy-start | bytes 52
  21.0 15.8 %collective-permute-start.1 = (bf16[4,256,128]{2,1,0:T(8,128)(2,1)S(1)}, bf16[4,256,128]{2,1,0:T(8,128)(2,1)S(1)}, u32[]{:S(2)}, u32[]{:S(2)}) collective-permute-start(bf16[4,256,128]{2,1,0:T(8,128)(2,1)S(1)} %shard_map.75.refs_0_), channel_id=1, source_target_pairs={{0,448},{64,0},{128,64},{192,128},{256,192},{320,256},{384,320},{4... | collective-permute-start | bytes 786440 | tf_op jit(solution)/shard_map/ppermute | solution.py:270
  32.1 10.3 %collective-permute-start = (bf16[4,256,128]{2,1,0:T(8,128)(2,1)S(1)}, bf16[4,256,128]{2,1,0:T(8,128)(2,1)S(1)}, u32[]{:S(2)}, u32[]{:S(2)}) collective-permute-start(bf16[4,256,128]{2,1,0:T(8,128)(2,1)S(1)} %shard_map.75.refs_0_), channel_id=1, source_target_pairs={{0,64},{64,128},{128,192},{192,256},{256,320},{320,384},{384,448},... | collective-permute-start | bytes 786440 | tf_op jit(solution)/shard_map/ppermute | solution.py:269
  36.8 9.5 %collective-permute-start.3 = (bf16[4,256,128]{2,1,0:T(8,128)(2,1)S(1)}, bf16[4,256,128]{2,1,0:T(8,128)(2,1)S(1)}, u32[]{:S(2)}, u32[]{:S(2)}) collective-permute-start(bf16[4,256,128]{2,1,0:T(8,128)(2,1)S(1)} %collective-permute-done.1.refs_2_), channel_id=1, source_target_pairs={{0,448},{64,0},{128,64},{192,128},{256,192},{320,256},{384,320},{4... | collective-permute-start | bytes 786440 | tf_op jit(solution)/shard_map/ppermute | solution.py:270
  42.4 9.5 %collective-permute-start.2 = (bf16[4,256,128]{2,1,0:T(8,128)(2,1)S(1)}, bf16[4,256,128]{2,1,0:T(8,128)(2,1)S(1)}, u32[]{:S(2)}, u32[]{:S(2)}) collective-permute-start(bf16[4,256,128]{2,1,0:T(8,128)(2,1)S(1)} %collective-permute-done.refs_1_), channel_id=1, source_target_pairs={{0,64},{64,128},{128,192},{192,256},{256,320},{320,384},{384,448},... | collective-permute-start | bytes 786440 | tf_op jit(solution)/shard_map/ppermute | solution.py:269
  46.2 9.5 %collective-permute-start.5 = (bf16[4,256,128]{2,1,0:T(8,128)(2,1)S(1)}, bf16[4,256,128]{2,1,0:T(8,128)(2,1)S(1)}, u32[]{:S(2)}, u32[]{:S(2)}) collective-permute-start(bf16[4,256,128]{2,1,0:T(8,128)(2,1)S(1)} %collective-permute-done.3.refs_4_), channel_id=1, source_target_pairs={{0,448},{64,0},{128,64},{192,128},{256,192},{320,256},{384,320},{4... | collective-permute-start | bytes 786440 | tf_op jit(solution)/shard_map/ppermute | solution.py:270
  51.8 9.5 %collective-permute-start.4 = (bf16[4,256,128]{2,1,0:T(8,128)(2,1)S(1)}, bf16[4,256,128]{2,1,0:T(8,128)(2,1)S(1)}, u32[]{:S(2)}, u32[]{:S(2)}) collective-permute-start(bf16[4,256,128]{2,1,0:T(8,128)(2,1)S(1)} %collective-permute-done.2.refs_3_), channel_id=1, source_target_pairs={{0,64},{64,128},{128,192},{192,256},{256,320},{320,384},{384,448},... | collective-permute-start | bytes 786440 | tf_op jit(solution)/shard_map/ppermute | solution.py:269
  55.7 5.7 %copy-start.1 = (bf16[4,256,128]{2,1,0:T(8,128)(2,1)}, bf16[4,256,128]{2,1,0:T(8,128)(2,1)S(1)}, u32[]{:S(2)}) copy-start(bf16[4,256,128]{2,1,0:T(8,128)(2,1)S(1)} %collective-permute-done.5.refs_6_) | copy-start | bytes 786436
  62.0 31.5 %collective-permute-start.8 = (bf16[7,4,256,128]{3,2,1,0:T(8,128)(2,1)S(1)}, bf16[7,4,256,128]{3,2,1,0:T(8,128)(2,1)}, u32[]{:S(2)}, u32[]{:S(2)}) collective-permute-start(bf16[7,4,256,128]{3,2,1,0:T(8,128)(2,1)S(1)} %shard_map.76.after_ref.near_ref), channel_id=1, source_target_pairs={{0,16},{16,0},{1,17},{17,1},{2,18},{18,2},{3,19},{19,3},{4,20},{20... | collective-permute-start | bytes 5505032 | tf_op jit(solution)/shard_map/ppermute | solution.py:293
  64.0 1.0 copy-start.9
  67.6 1.0 copy-start
  68.5 6.0 %copy-start.2 = (bf16[4,256,128]{2,1,0:T(8,128)(2,1)S(1)}, bf16[4,256,128]{2,1,0:T(8,128)(2,1)}, u32[]{:S(2)}) copy-start(bf16[4,256,128]{2,1,0:T(8,128)(2,1)} %copy-done.1) | copy-start | bytes 786436
  68.5 13.4 %copy-start.4 = (bf16[4,256,128]{2,1,0:T(8,128)(2,1)S(1)}, bf16[4,256,128]{2,1,0:T(8,128)(2,1)}, u32[]{:S(2)}) copy-start(bf16[4,256,128]{2,1,0:T(8,128)(2,1)} %copy-done.3) | copy-start | bytes 786436
  68.5 25.0 %all-to-all-start.2 = ((bf16[8,128,512]{2,1,0:T(8,128)(2,1)}), bf16[8,128,512]{2,1,0:T(8,128)(2,1)S(1)}, u32[]{:S(2)}, u32[]{:S(2)}) async-start(bf16[8,128,512]{2,1,0:T(8,128)(2,1)} %copy-done), calls=%async_computation.2 | async-start | bytes 2097152 | tf_op jit(solution)/shard_map/all_to_all | solution.py:258
  74.6 10.0 %collective-permute-start.7 = (bf16[2,256,128]{2,1,0:T(8,128)(2,1)S(1)}, bf16[2,256,128]{2,1,0:T(8,128)(2,1)S(1)}, u32[]{:S(2)}, u32[]{:S(2)}) collective-permute-start(bf16[2,256,128]{2,1,0:T(8,128)(2,1)S(1)} %slice.9), channel_id=1, source_target_pairs={{0,448},{64,0},{128,64},{192,128},{256,192},{320,256},{384,320},{4... | collective-permute-start | bytes 393224 | tf_op jit(solution)/shard_map/ppermute | solution.py:273
  82.0 8.1 %collective-permute-start.6 = (bf16[2,256,128]{2,1,0:T(8,128)(2,1)S(1)}, bf16[2,256,128]{2,1,0:T(8,128)(2,1)S(1)}, u32[]{:S(2)}, u32[]{:S(2)}) collective-permute-start(bf16[2,256,128]{2,1,0:T(8,128)(2,1)S(1)} %slice.8), channel_id=1, source_target_pairs={{0,64},{64,128},{128,192},{192,256},{256,320},{320,384},{384,448},... | collective-permute-start | bytes 393224 | tf_op jit(solution)/shard_map/ppermute | solution.py:272
  90.1 3.4 %collective-permute-start.9 = (bf16[1,4,256,128]{3,2,1,0:T(8,128)(2,1)S(1)}, bf16[1,4,256,128]{3,2,1,0:T(8,128)(2,1)S(1)}, u32[]{:S(2)}, u32[]{:S(2)}) collective-permute-start(bf16[1,4,256,128]{3,2,1,0:T(8,128)(2,1)S(1)} %shard_map.78.far_ref), channel_id=1, source_target_pairs={{0,16},{16,0},{1,17},{17,1},{2,18},{18,2},{3,19},{19,3},{4,20},{20... | collective-permute-start | bytes 786440 | tf_op jit(solution)/shard_map/ppermute | solution.py:293
  97.5 25.3 %all-to-all-start.3 = ((bf16[32,64,128]{2,1,0:T(8,128)(2,1)}), bf16[32,64,128]{2,1,0:T(8,128)(2,1)S(1)}, u32[]{:S(2)}, u32[]{:S(2)}) async-start(bf16[32,64,128]{2,1,0:T(8,128)(2,1)} %bitcast.4), calls=%async_computation.3 | async-start | bytes 1048576 | tf_op jit(solution)/shard_map/all_to_all | solution.py:258
  (2 other events, 1.7 us)

commit v5 on v4

--- a/solution.py
+++ b/solution.py
@@ -31,8 +31,8 @@
     )
 
 
-def attention_kernel(table_ref, query_ref, memory_ref, nbr_ref, after_ref, out_ref):
-    del after_ref
+def attention_kernel(table_ref, query_ref, memory_ref, nbr_ref, *refs):
+    out_ref = refs[-1]
     stretches, per_stretch = table_ref.shape
     pieces = nbr_ref.shape[0] // (stretches * per_stretch)
     heads = query_ref.shape[1] // HD
@@ -59,24 +59,45 @@
                 rows_times_rows(query_ref[rows, cols], nbr_key) * SCALE
             )
             context = jnp.dot(dec_probs, encoded, preferred_element_type=jnp.float32)
-            context = context.astype(jnp.bfloat16)
-            for copy in range(out_ref.shape[0]):
-                out_ref[copy, rows, cols] = context
+            out_ref[rows, cols] = context.astype(jnp.bfloat16)
 
 
 VMEM = pl.BlockSpec(memory_space=pltpu.VMEM)
 ANY = pl.BlockSpec(memory_space=pl.ANY)
-PARAMS = pltpu.CompilerParams(vmem_limit_bytes=32 * 2**20)
-
-
-def attention(table, query, memory, neighbours, copies, after):
+HBM = pl.BlockSpec(memory_space=pltpu.HBM)
+PARAMS = pltpu.CompilerParams(vmem_limit_bytes=16 * 2**20)
+
+
+def attention(table, query, memory, neighbours, after):
     return pl.pallas_call(
         attention_kernel,
-        out_shape=jax.ShapeDtypeStruct((copies, *query.shape), jnp.bfloat16),
-        in_specs=[pl.BlockSpec(memory_space=pltpu.SMEM)] + [VMEM] * 3 + [ANY],
-        out_specs=VMEM,
-        compiler_params=PARAMS,
-    )(table, query, memory, neighbours, after)
+        out_shape=jax.ShapeDtypeStruct(query.shape, jnp.bfloat16),
+        in_specs=[pl.BlockSpec(memory_space=pltpu.SMEM)] + [VMEM] * 3 + [ANY] * len(after),
+        out_specs=VMEM,
+        compiler_params=PARAMS,
+    )(table, query, memory, neighbours, *after)
+
+
+def repeat_kernel(value_ref, *refs):
+    out_ref, sems = refs[-2:]
+    copies = [
+        pltpu.make_async_copy(value_ref, out_ref.at[i], sems.at[i]) for i in range(out_ref.shape[0])
+    ]
+    for copy in copies:
+        copy.start()
+    for copy in copies:
+        copy.wait()
+
+
+def repeat(value, count, after):
+    return pl.pallas_call(
+        repeat_kernel,
+        out_shape=jax.ShapeDtypeStruct((count, *value.shape), value.dtype),
+        in_specs=[VMEM] + [ANY] * len(after),
+        out_specs=HBM,
+        scratch_shapes=[pltpu.SemaphoreType.DMA((count,))],
+        compiler_params=PARAMS,
+    )(value, *after)
 
 
 def pack_kernel(query_ref, key_ref, value_ref, out_ref):
@@ -146,45 +167,43 @@
     )(folded)
 
 
+TOGETHER = 4
+
+
 def stack_kernel(*refs):
+    count = (len(refs) - 1) * TOGETHER // (TOGETHER + 1)
+    for i in range(count):
+        refs[count + 1 + i // TOGETHER][i % TOGETHER] = refs[i][...]
+
+
+def stack(blocks, after):
+    shape = jax.ShapeDtypeStruct((TOGETHER, *blocks[0].shape), blocks[0].dtype)
+    outs = len(blocks) // TOGETHER
+    return pl.pallas_call(
+        stack_kernel,
+        out_shape=[shape] * outs,
+        in_specs=[VMEM] * len(blocks) + [ANY],
+        out_specs=[VMEM] * outs,
+        compiler_params=PARAMS,
+    )(*blocks, after)
+
+
+def project_kernel(plane_ref, context_ref, *refs):
     out_ref = refs[-1]
-    place = 0
-    quarters = out_ref.shape[1]
-    for ref in refs[:-1]:
-        count = ref.shape[0]
-        out_ref[place // quarters, pl.ds(place % quarters, count)] = ref[...]
-        place += count
-
-
-def stack(quarters, *values):
-    count = sum(value.shape[0] for value in values) // quarters
-    return pl.pallas_call(
-        stack_kernel,
-        out_shape=jax.ShapeDtypeStruct(
-            (count, quarters, *values[0].shape[1:]), values[0].dtype
-        ),
-        in_specs=[VMEM] * len(values),
-        out_specs=VMEM,
-        compiler_params=PARAMS,
-    )(*values)
-
-
-def project_kernel(plane_ref, context_ref, near_ref, far_ref, near_sib_ref, far_sib_ref, out_ref):
+    stacks = len(refs) // 2
     plane = plane_ref[0]
     sides, quarters, tokens, span = context_ref.shape
-    width = near_ref.shape[-1]
+    width = refs[0].shape[-1]
     middle, half, part = width // 2, tokens // 2, width // 4
-    blocks = [(near_ref, near_sib_ref, i) for i in range(near_ref.shape[0])]
-    blocks += [(far_ref, far_sib_ref, i) for i in range(far_ref.shape[0])]
-    planes = len(blocks)
+    planes = TOGETHER * stacks
     left = [
         jnp.concatenate([context_ref[s, x] for s in range(sides)], axis=0)
         for x in range(quarters)
     ]
 
     def rows_of(index, x):
-        own_ref, sib_ref, i = blocks[index]
-        own, sib = own_ref[i, x], sib_ref[i, x]
+        own = refs[index // TOGETHER][index % TOGETHER, x]
+        sib = refs[stacks + index // TOGETHER][index % TOGETHER, x]
         upper = jnp.concatenate([own[:, :middle], sib[:, :middle]], axis=1)
         lower = jnp.concatenate([own[:, middle:], sib[:, middle:]], axis=1)
         return jnp.concatenate([upper, lower], axis=0)
@@ -209,18 +228,17 @@
                     )
 
 
-def project(plane, context, near, far, near_sib, far_sib):
+def project(plane, context, own, sib):
     sides, _, tokens, _ = context.shape
-    planes = near.shape[0] + far.shape[0]
     return pl.pallas_call(
         project_kernel,
         out_shape=jax.ShapeDtypeStruct(
-            (sides, 2 * planes, tokens // 2, near.shape[-1]), jnp.bfloat16
+            (sides, 2 * TOGETHER * len(own), tokens // 2, own[0].shape[-1]), jnp.bfloat16
         ),
-        in_specs=[pl.BlockSpec(memory_space=pltpu.SMEM)] + [VMEM] * 5,
-        out_specs=VMEM,
-        compiler_params=PARAMS,
-    )(plane, context, near, far, near_sib, far_sib)
+        in_specs=[pl.BlockSpec(memory_space=pltpu.SMEM)] + [VMEM] * (1 + len(own) + len(sib)),
+        out_specs=VMEM,
+        compiler_params=PARAMS,
+    )(plane, context, *own, *sib)
 
 
 def add_kernel(core_ref, partial_ref, out_ref):
@@ -258,22 +276,18 @@
     return lax.all_to_all(value, axes, split_axis=0, concat_axis=0, tiled=True)
 
 
-OFFSETS = (0, -1, 1, -2, 2, -3, 3, 4)
+OFFSETS = (0, -1, 1, -2, 2, -3, 3, -4)
 
 
 def ring(value, axis, size):
     up = [(i, (i + 1) % size) for i in range(size)]
     down = [(i, (i - 1) % size) for i in range(size)]
-    behind, ahead = [value], [value]
+    blocks, behind, ahead = [value], value, value
     for _ in range(size // 2 - 1):
-        behind.append(lax.ppermute(behind[-1], axis, up))
-        ahead.append(lax.ppermute(ahead[-1], axis, down))
-    half = value.shape[0] // 2
-    top = lax.ppermute(behind[-1][:half], axis, up)
-    low = lax.ppermute(ahead[-1][half:], axis, down)
-    near = stack(len(value), value, behind[1], ahead[1], behind[2], ahead[2], behind[3], ahead[3])
-    far = stack(len(value), top, low)
-    return near, far
+        behind = lax.ppermute(behind, axis, up)
+        ahead = lax.ppermute(ahead, axis, down)
+        blocks += [behind, ahead]
+    return blocks + [lax.ppermute(behind, axis, up)]
 
 
 def local(
@@ -288,17 +302,19 @@
     groups,
 ):
     folded = exchange(fold(output_weight, 8), ("yl", "x"))
-    near, far = ring(regroup(folded.reshape(2, 4, *folded.shape[1:])), "z", 8)
-    swap = [(0, 1), (1, 0)]
-    near_sib, far_sib = lax.ppermute(near, "c", swap), lax.ppermute(far, "c", swap)
+    blocks = ring(regroup(folded.reshape(2, 4, *folded.shape[1:])), "z", 8)
 
     neighbours = pack(neighbour_query, neighbour_key, neighbour_value, groups)
     neighbours = exchange(neighbours, TENSOR)
-    context = attention(neighbour_table, decoder_query, decoder_memory, neighbours, 8, near)
+    table = neighbour_table & 3
+    context = attention(table, decoder_query, decoder_memory, neighbours, blocks[-3:-1])
+    context = repeat(context, 8, blocks[-1:])
+    own = stack(blocks, context)
+    sib = [lax.ppermute(block, "c", [(0, 1), (1, 0)]) for block in own]
     context = exchange(context, ("yl", "x"))
     context = context.reshape(2, 4, *context.shape[1:])
     plane = lax.axis_index("z").astype(jnp.int32).reshape(1)
-    partial = project(plane, context, near, far, near_sib, far_sib)
+    partial = project(plane, context, own, sib)
     shape = partial.shape
     partial = exchange(partial.reshape(2 * groups, *shape[2:]), ("yl", "yh", "x"))
     core = lax.axis_index("c").astype(jnp.int32).reshape(1)

time: 125 us -> 115 us (0.920)
  starting transfers between devices: 67.2 us -> 59.6 us
  waiting for transfers between devices: 39.6 us -> 36.6 us
  Pallas kernels: 9.93 us -> 12.4 us
    ppermute x10 -> x9, waiting for transfers between devices: 19.9 us -> 10.4 us  [the longest x3 7.1 us: ring(): behind = lax.ppermute(behind, axis, up)]
    ppermute x10 -> x9, starting transfers between devices: 41.2 us -> 33.2 us  [the longest x3 18.8 us: ring(): ahead = lax.ppermute(ahead, axis, down)]
    all_to_all x4, waiting for transfers between devices: 19.7 us -> 26.3 us  [exchange(): return lax.all_to_all(value, axes, split_axis=0, concat_axis=0, tiled=True)]
    pallas_call x3, Pallas kernels: 2.75 us -> 5.11 us  [the longest x1 2.59 us: attention(): pl.pallas_call(attention_kernel, out_shape=jax.ShapeDtypeStruct(query.sha...]
    unnamed x24 -> x22, local copies, waits for them, and re-layouts: 6.59 us -> 5.5 us
  transfers between devices with their start and end apart: 14 -> 13, of which waited for: 9 -> 11; matrix products, arithmetic and copies ran while one was open for 0% -> 0% of each run, Pallas kernels for 3% -> 5%
where the time goes in v5:
time: 115 us; the launch traced here: 114 us
  starting transfers between devices  59.6 us (52%)
  waiting for transfers between devices  36.6 us (32%)
  Pallas kernels  12.4 us (11%)
  local copies, waits for them, and re-layouts  5.5 us (5%)
    all_to_all x4, starting transfers between devices, exchange(): return lax.all_to_all(value, axes, split_axis=0, concat_axis=0, tiled=True)  26.4 us
    all_to_all x4, waiting for transfers between devices, exchange(): return lax.all_to_all(value, axes, split_axis=0, concat_axis=0, tiled=True)  26.3 us
    ppermute x3, starting transfers between devices, ring(): ahead = lax.ppermute(ahead, axis, down)  18.8 us
    ppermute x3, starting transfers between devices, ring(): behind = lax.ppermute(behind, axis, up)  8.1 us
    ppermute x3, waiting for transfers between devices, ring(): behind = lax.ppermute(behind, axis, up)  7.1 us
    unnamed x22, local copies, waits for them, and re-layouts  5.5 us
    ppermute x2, starting transfers between devices, local(): sib = [lax.ppermute(block, 'c', [(0, 1), (1, 0)]) for block in own]  4.31 us
    pallas_call x1, Pallas kernels, project(): pl.pallas_call(project_kernel, out_shape=jax.ShapeDtypeStruct((sides, 2 *...  4.02 us
  transfers between devices with their start and end apart: 13, of which 11 were waited for; matrix products, arithmetic and copies ran while one was open for 0% of the time, Pallas kernels for 5%

profile of v5, /device:TPU:8, one launch (start us, length us, event | category | flops | bytes accessed | tf_op | source)
XLA Modules:
  0.0 114.3 jit_solution(10543072822644472885)
XLA Ops:
  2.0 9.2 %all-to-all-start.1 = ((bf16[8,128,128]{2,1,0:T(8,128)(2,1)}), bf16[8,128,128]{2,1,0:T(8,128)(2,1)S(1)}, u32[]{:S(2)}, u32[]{:S(2)}) async-start(bf16[8,128,128]{2,1,0:T(8,128)(2,1)} %shard_map.74), calls=%async_computation.1 | async-start | bytes 524288 | tf_op jit(solution)/shard_map/all_to_all | solution.py:276
  14.2 1.3 %shard_map.73 = bf16[16,3,32,512]{3,2,1,0:T(8,128)(2,1)} custom-call(bf16[32,8192]{1,0:T(8,128)(2,1)S(1)} %copy-done, bf16[32,8192]{1,0:T(8,128)(2,1)S(1)} %copy-done.1, bf16[32,8192]{1,0:T(8,128)(2,1)S(1)} %copy-done.2), custom_call_target="tpu_custom_call" | custom-call | tf_op jit(solution)/shard_map/pallas_call | solution.py:112
  15.5 1.4 %all-to-all-done.1 = bf16[8,128,128]{2,1,0:T(8,128)(2,1)S(1)} async-done(((bf16[8,128,128]{2,1,0:T(8,128)(2,1)}), bf16[8,128,128]{2,1,0:T(8,128)(2,1)S(1)}, u32[]{:S(2)}, u32[]{:S(2)}) %all-to-all-start.1) | async-done | bytes 262176 | tf_op jit(solution)/shard_map/all_to_all | solution.py:276
  17.0 4.0 %all-to-all-start = ((bf16[16,3,32,512]{3,2,1,0:T(8,128)(2,1)}), bf16[16,3,32,512]{3,2,1,0:T(8,128)(2,1)S(1)}, u32[]{:S(2)}, u32[]{:S(2)}) async-start(bf16[16,3,32,512]{3,2,1,0:T(8,128)(2,1)} %shard_map.73), calls=%async_computation | async-start | bytes 3145728 | tf_op jit(solution)/shard_map/all_to_all | solution.py:276
  21.1 4.3 %collective-permute-start = (bf16[4,256,128]{2,1,0:T(8,128)(2,1)S(1)}, bf16[4,256,128]{2,1,0:T(8,128)(2,1)S(1)}, u32[]{:S(2)}, u32[]{:S(2)}) collective-permute-start(bf16[4,256,128]{2,1,0:T(8,128)(2,1)S(1)} %shard_map.75.refs_0_), channel_id=1, source_target_pairs={{0,64},{64,128},{128,192},{192,256},{256,320},{320,384},{384,448},... | collective-permute-start | bytes 786440 | tf_op jit(solution)/shard_map/ppermute | solution.py:287
  25.4 8.6 %collective-permute-start.3 = (bf16[4,256,128]{2,1,0:T(8,128)(2,1)S(1)}, bf16[4,256,128]{2,1,0:T(8,128)(2,1)S(1)}, u32[]{:S(2)}, u32[]{:S(2)}) collective-permute-start(bf16[4,256,128]{2,1,0:T(8,128)(2,1)S(1)} %shard_map.75.refs_0_), channel_id=1, source_target_pairs={{0,448},{64,0},{128,64},{192,128},{256,192},{320,256},{384,320},{4... | collective-permute-start | bytes 786440 | tf_op jit(solution)/shard_map/ppermute | solution.py:288
  34.0 3.5 %collective-permute-done.refs_1_ = bf16[4,256,128]{2,1,0:T(8,128)(2,1)S(1)} collective-permute-done((bf16[4,256,128]{2,1,0:T(8,128)(2,1)S(1)}, bf16[4,256,128]{2,1,0:T(8,128)(2,1)S(1)}, u32[]{:S(2)}, u32[]{:S(2)}) %collective-permute-start) | collective-permute-done | bytes 262176 | tf_op jit(solution)/shard_map/ppermute | solution.py:287
  37.5 1.9 %collective-permute-start.1 = (bf16[4,256,128]{2,1,0:T(8,128)(2,1)S(1)}, bf16[4,256,128]{2,1,0:T(8,128)(2,1)S(1)}, u32[]{:S(2)}, u32[]{:S(2)}) collective-permute-start(bf16[4,256,128]{2,1,0:T(8,128)(2,1)S(1)} %collective-permute-done.refs_1_), channel_id=1, source_target_pairs={{0,64},{64,128},{128,192},{192,256},{256,320},{320,384},{384,448},... | collective-permute-start | bytes 786440 | tf_op jit(solution)/shard_map/ppermute | solution.py:287
  39.5 5.1 %collective-permute-start.4 = (bf16[4,256,128]{2,1,0:T(8,128)(2,1)S(1)}, bf16[4,256,128]{2,1,0:T(8,128)(2,1)S(1)}, u32[]{:S(2)}, u32[]{:S(2)}) collective-permute-start(bf16[4,256,128]{2,1,0:T(8,128)(2,1)S(1)} %collective-permute-done.3.refs_2_), channel_id=1, source_target_pairs={{0,448},{64,0},{128,64},{192,128},{256,192},{320,256},{384,320},{4... | collective-permute-start | bytes 786440 | tf_op jit(solution)/shard_map/ppermute | solution.py:288
  44.6 2.6 %collective-permute-done.1.refs_3_ = bf16[4,256,128]{2,1,0:T(8,128)(2,1)S(1)} collective-permute-done((bf16[4,256,128]{2,1,0:T(8,128)(2,1)S(1)}, bf16[4,256,128]{2,1,0:T(8,128)(2,1)S(1)}, u32[]{:S(2)}, u32[]{:S(2)}) %collective-permute-start.1) | collective-permute-done | bytes 262176 | tf_op jit(solution)/shard_map/ppermute | solution.py:287
  47.2 1.9 %collective-permute-start.2 = (bf16[4,256,128]{2,1,0:T(8,128)(2,1)S(1)}, bf16[4,256,128]{2,1,0:T(8,128)(2,1)S(1)}, u32[]{:S(2)}, u32[]{:S(2)}) collective-permute-start(bf16[4,256,128]{2,1,0:T(8,128)(2,1)S(1)} %collective-permute-done.1.refs_3_), channel_id=1, source_target_pairs={{0,64},{64,128},{128,192},{192,256},{256,320},{320,384},{384,448},... | collective-permute-start | bytes 786440 | tf_op jit(solution)/shard_map/ppermute | solution.py:287
  49.8 5.1 %collective-permute-start.5 = (bf16[4,256,128]{2,1,0:T(8,128)(2,1)S(1)}, bf16[4,256,128]{2,1,0:T(8,128)(2,1)S(1)}, u32[]{:S(2)}, u32[]{:S(2)}) collective-permute-start(bf16[4,256,128]{2,1,0:T(8,128)(2,1)S(1)} %collective-permute-done.4.refs_4_), channel_id=1, source_target_pairs={{0,448},{64,0},{128,64},{192,128},{256,192},{320,256},{384,320},{4... | collective-permute-start | bytes 786440 | tf_op jit(solution)/shard_map/ppermute | solution.py:288
  56.7 1.9 %collective-permute-start.6 = (bf16[4,256,128]{2,1,0:T(8,128)(2,1)S(1)}, bf16[4,256,128]{2,1,0:T(8,128)(2,1)S(1)}, u32[]{:S(2)}, u32[]{:S(2)}) collective-permute-start(bf16[4,256,128]{2,1,0:T(8,128)(2,1)S(1)} %collective-permute-done.2.refs_0_.refs_5_), channel_id=1, source_target_pairs={{0,64},{64,128},{128,192},{192,256},{256,320},{320,384},{384,448},... | collective-permute-start | bytes 786440 | tf_op jit(solution)/shard_map/ppermute | solution.py:290
  58.8 4.1 %all-to-all-done.nbr_ref = bf16[16,3,32,512]{3,2,1,0:T(8,128)(2,1)S(1)} async-done(((bf16[16,3,32,512]{3,2,1,0:T(8,128)(2,1)}), bf16[16,3,32,512]{3,2,1,0:T(8,128)(2,1)S(1)}, u32[]{:S(2)}, u32[]{:S(2)}) %all-to-all-start) | async-done | bytes 1572896 | tf_op jit(solution)/shard_map/all_to_all | solution.py:276
  63.0 2.6 %shard_map.76.value_ref = bf16[128,512]{1,0:T(8,128)(2,1)S(1)} custom-call(s32[2,2]{1,0:T(2,128)S(1)} %broadcast_and_fusion.table_ref, bf16[128,512]{1,0:T(8,128)(2,1)S(1)} %copy-done.9, bf16[2,128,512]{2,1,0:T(8,128)(2,1)S(1)} %copy-done.3, bf16[16,3,32,512]{3,2,1,0:T(8,128)(2,1)S(1)} %all-to-all-done.nbr_ref, ...), custom_call_target="tpu_custom_call" | custom-call | tf_op jit(solution)/shard_map/pallas_call | solution.py:72
  67.2 5.7 %all-to-all-start.2 = ((bf16[8,128,512]{2,1,0:T(8,128)(2,1)}), bf16[8,128,512]{2,1,0:T(8,128)(2,1)S(1)}, u32[]{:S(2)}, u32[]{:S(2)}) async-start(bf16[8,128,512]{2,1,0:T(8,128)(2,1)} %shard_map.77.refs_8_), calls=%async_computation.2 | async-start | bytes 2097152 | tf_op jit(solution)/shard_map/all_to_all | solution.py:276
  72.9 1.4 %shard_map.78 = (bf16[4,4,256,128]{3,2,1,0:T(8,128)(2,1)}, bf16[4,4,256,128]{3,2,1,0:T(8,128)(2,1)}) custom-call(bf16[4,256,128]{2,1,0:T(8,128)(2,1)S(1)} %shard_map.75.refs_0_, bf16[4,256,128]{2,1,0:T(8,128)(2,1)S(1)} %collective-permute-done.refs_1_, bf16[4,256,128]{2,1,0:T(8,128)(2,1)S(1)} %collective-permute-done.3.refs_2_, ...), custom_call_target="tpu_custom_call" | custom-call | tf_op jit(solution)/shard_map/pallas_call | solution.py:182
  74.4 1.9 %collective-permute-start.7 = (bf16[4,4,256,128]{3,2,1,0:T(8,128)(2,1)}, bf16[4,4,256,128]{3,2,1,0:T(8,128)(2,1)S(1)}, u32[]{:S(2)}, u32[]{:S(2)}) collective-permute-start(bf16[4,4,256,128]{3,2,1,0:T(8,128)(2,1)} %get-tuple-element.7.refs_0_), channel_id=1, source_target_pairs={{0,16},{16,0},{1,17},{17,1},{2,18},{18,2},{3,19},{19,3},{4,20},{20... | collective-permute-start | bytes 3145736 | tf_op jit(solution)/shard_map/ppermute | solution.py:313
  76.3 2.4 %collective-permute-start.8 = (bf16[4,4,256,128]{3,2,1,0:T(8,128)(2,1)}, bf16[4,4,256,128]{3,2,1,0:T(8,128)(2,1)S(1)}, u32[]{:S(2)}, u32[]{:S(2)}) collective-permute-start(bf16[4,4,256,128]{3,2,1,0:T(8,128)(2,1)} %get-tuple-element.8.refs_1_), channel_id=1, source_target_pairs={{0,16},{16,0},{1,17},{17,1},{2,18},{18,2},{3,19},{19,3},{4,20},{20... | collective-permute-start | bytes 3145736 | tf_op jit(solution)/shard_map/ppermute | solution.py:313
  79.1 2.1 %collective-permute-done.8.refs_3_ = bf16[4,4,256,128]{3,2,1,0:T(8,128)(2,1)S(1)} collective-permute-done((bf16[4,4,256,128]{3,2,1,0:T(8,128)(2,1)}, bf16[4,4,256,128]{3,2,1,0:T(8,128)(2,1)S(1)}, u32[]{:S(2)}, u32[]{:S(2)}) %collective-permute-start.8) | collective-permute-done | bytes 1048608 | tf_op jit(solution)/shard_map/ppermute | solution.py:313
  81.2 3.0 %all-to-all-done.2 = bf16[8,128,512]{2,1,0:T(8,128)(2,1)S(1)} async-done(((bf16[8,128,512]{2,1,0:T(8,128)(2,1)}), bf16[8,128,512]{2,1,0:T(8,128)(2,1)S(1)}, u32[]{:S(2)}, u32[]{:S(2)}) %all-to-all-start.2) | async-done | bytes 1048608 | tf_op jit(solution)/shard_map/all_to_all | solution.py:276
  84.1 4.0 %shard_map.79 = bf16[2,16,64,128]{3,2,1,0:T(8,128)(2,1)} custom-call(s32[1]{0:T(128)} %bitcast.1.plane_ref, bf16[2,4,128,512]{3,2,1,0:T(8,128)(2,1)S(1)} %bitcast.6, bf16[4,4,256,128]{3,2,1,0:T(8,128)(2,1)} %get-tuple-element.7.refs_0_, bf16[4,4,256,128]{3,2,1,0:T(8,128)(2,1)} %get-tuple-element.8.refs_1_, ...), custom_call_target="tpu_custom_call" | custom-call | tf_op jit(solution)/shard_map/pallas_call | solution.py:233
  88.2 7.5 %all-to-all-start.3 = ((bf16[32,64,128]{2,1,0:T(8,128)(2,1)}), bf16[32,64,128]{2,1,0:T(8,128)(2,1)S(1)}, u32[]{:S(2)}, u32[]{:S(2)}) async-start(bf16[32,64,128]{2,1,0:T(8,128)(2,1)} %bitcast.4), calls=%async_computation.3 | async-start | bytes 1048576 | tf_op jit(solution)/shard_map/all_to_all | solution.py:276
  95.7 17.7 %all-to-all-done.3 = bf16[32,64,128]{2,1,0:T(8,128)(2,1)S(1)} async-done(((bf16[32,64,128]{2,1,0:T(8,128)(2,1)}), bf16[32,64,128]{2,1,0:T(8,128)(2,1)S(1)}, u32[]{:S(2)}, u32[]{:S(2)}) %all-to-all-start.3) | async-done | bytes 524320 | tf_op jit(solution)/shard_map/all_to_all | solution.py:276
  (33 shorter events, 10.8 us)
Async XLA Ops:
  0.0 0.9 copy-start.8
  2.0 15.0 %all-to-all-start.1 = ((bf16[8,128,128]{2,1,0:T(8,128)(2,1)}), bf16[8,128,128]{2,1,0:T(8,128)(2,1)S(1)}, u32[]{:S(2)}, u32[]{:S(2)}) async-start(bf16[8,128,128]{2,1,0:T(8,128)(2,1)} %shard_map.74), calls=%async_computation.1 | async-start | bytes 524288 | tf_op jit(solution)/shard_map/all_to_all | solution.py:276
  11.1 1.0 copy-start
  12.2 1.0 copy-start.1
  13.2 1.0 copy-start.2
  15.5 43.1 %copy-start.10 = (s32[2,2]{1,0:T(2,128)S(1)}, s32[2,2]{1,0:T(2,128)}, u32[]{:S(2)}) copy-start(s32[2,2]{1,0:T(2,128)} %param.12) | copy-start | bytes 52
  15.5 47.5 %copy-start.3 = (bf16[2,128,512]{2,1,0:T(8,128)(2,1)S(1)}, bf16[2,128,512]{2,1,0:T(8,128)(2,1)}, u32[]{:S(2)}) copy-start(bf16[2,128,512]{2,1,0:T(8,128)(2,1)} %memory_ref.1) | copy-start | bytes 786436
  15.5 47.5 %copy-start.9 = (bf16[128,512]{1,0:T(8,128)(2,1)S(1)}, bf16[128,512]{1,0:T(8,128)(2,1)}, u32[]{:S(2)}) copy-start(bf16[128,512]{1,0:T(8,128)(2,1)} %query_ref.3) | copy-start | bytes 393220
  17.0 46.0 %all-to-all-start = ((bf16[16,3,32,512]{3,2,1,0:T(8,128)(2,1)}), bf16[16,3,32,512]{3,2,1,0:T(8,128)(2,1)S(1)}, u32[]{:S(2)}, u32[]{:S(2)}) async-start(bf16[16,3,32,512]{3,2,1,0:T(8,128)(2,1)} %shard_map.73), calls=%async_computation | async-start | bytes 3145728 | tf_op jit(solution)/shard_map/all_to_all | solution.py:276
  21.1 16.4 %collective-permute-start = (bf16[4,256,128]{2,1,0:T(8,128)(2,1)S(1)}, bf16[4,256,128]{2,1,0:T(8,128)(2,1)S(1)}, u32[]{:S(2)}, u32[]{:S(2)}) collective-permute-start(bf16[4,256,128]{2,1,0:T(8,128)(2,1)S(1)} %shard_map.75.refs_0_), channel_id=1, source_target_pairs={{0,64},{64,128},{128,192},{192,256},{256,320},{320,384},{384,448},... | collective-permute-start | bytes 786440 | tf_op jit(solution)/shard_map/ppermute | solution.py:287
  25.4 14.0 %collective-permute-start.3 = (bf16[4,256,128]{2,1,0:T(8,128)(2,1)S(1)}, bf16[4,256,128]{2,1,0:T(8,128)(2,1)S(1)}, u32[]{:S(2)}, u32[]{:S(2)}) collective-permute-start(bf16[4,256,128]{2,1,0:T(8,128)(2,1)S(1)} %shard_map.75.refs_0_), channel_id=1, source_target_pairs={{0,448},{64,0},{128,64},{192,128},{256,192},{320,256},{384,320},{4... | collective-permute-start | bytes 786440 | tf_op jit(solution)/shard_map/ppermute | solution.py:288
  37.5 9.7 %collective-permute-start.1 = (bf16[4,256,128]{2,1,0:T(8,128)(2,1)S(1)}, bf16[4,256,128]{2,1,0:T(8,128)(2,1)S(1)}, u32[]{:S(2)}, u32[]{:S(2)}) collective-permute-start(bf16[4,256,128]{2,1,0:T(8,128)(2,1)S(1)} %collective-permute-done.refs_1_), channel_id=1, source_target_pairs={{0,64},{64,128},{128,192},{192,256},{256,320},{320,384},{384,448},... | collective-permute-start | bytes 786440 | tf_op jit(solution)/shard_map/ppermute | solution.py:287
  39.5 10.4 %collective-permute-start.4 = (bf16[4,256,128]{2,1,0:T(8,128)(2,1)S(1)}, bf16[4,256,128]{2,1,0:T(8,128)(2,1)S(1)}, u32[]{:S(2)}, u32[]{:S(2)}) collective-permute-start(bf16[4,256,128]{2,1,0:T(8,128)(2,1)S(1)} %collective-permute-done.3.refs_2_), channel_id=1, source_target_pairs={{0,448},{64,0},{128,64},{192,128},{256,192},{320,256},{384,320},{4... | collective-permute-start | bytes 786440 | tf_op jit(solution)/shard_map/ppermute | solution.py:288
  47.2 9.5 %collective-permute-start.2 = (bf16[4,256,128]{2,1,0:T(8,128)(2,1)S(1)}, bf16[4,256,128]{2,1,0:T(8,128)(2,1)S(1)}, u32[]{:S(2)}, u32[]{:S(2)}) collective-permute-start(bf16[4,256,128]{2,1,0:T(8,128)(2,1)S(1)} %collective-permute-done.1.refs_3_), channel_id=1, source_target_pairs={{0,64},{64,128},{128,192},{192,256},{256,320},{320,384},{384,448},... | collective-permute-start | bytes 786440 | tf_op jit(solution)/shard_map/ppermute | solution.py:287
  49.1 0.7 copy-start.4
  49.8 9.0 %collective-permute-start.5 = (bf16[4,256,128]{2,1,0:T(8,128)(2,1)S(1)}, bf16[4,256,128]{2,1,0:T(8,128)(2,1)S(1)}, u32[]{:S(2)}, u32[]{:S(2)}) collective-permute-start(bf16[4,256,128]{2,1,0:T(8,128)(2,1)S(1)} %collective-permute-done.4.refs_4_), channel_id=1, source_target_pairs={{0,448},{64,0},{128,64},{192,128},{256,192},{320,256},{384,320},{4... | collective-permute-start | bytes 786440 | tf_op jit(solution)/shard_map/ppermute | solution.py:288
  55.0 0.7 copy-start.6
  56.7 9.5 %collective-permute-start.6 = (bf16[4,256,128]{2,1,0:T(8,128)(2,1)S(1)}, bf16[4,256,128]{2,1,0:T(8,128)(2,1)S(1)}, u32[]{:S(2)}, u32[]{:S(2)}) collective-permute-start(bf16[4,256,128]{2,1,0:T(8,128)(2,1)S(1)} %collective-permute-done.2.refs_0_.refs_5_), channel_id=1, source_target_pairs={{0,64},{64,128},{128,192},{192,256},{256,320},{320,384},{384,448},... | collective-permute-start | bytes 786440 | tf_op jit(solution)/shard_map/ppermute | solution.py:290
  65.6 7.4 %copy-start.5 = (bf16[4,256,128]{2,1,0:T(8,128)(2,1)S(1)}, bf16[4,256,128]{2,1,0:T(8,128)(2,1)}, u32[]{:S(2)}) copy-start(bf16[4,256,128]{2,1,0:T(8,128)(2,1)} %copy-done.4) | copy-start | bytes 786436
  65.6 7.3 %copy-start.7 = (bf16[4,256,128]{2,1,0:T(8,128)(2,1)S(1)}, bf16[4,256,128]{2,1,0:T(8,128)(2,1)}, u32[]{:S(2)}) copy-start(bf16[4,256,128]{2,1,0:T(8,128)(2,1)} %copy-done.6) | copy-start | bytes 786436
  67.2 16.9 %all-to-all-start.2 = ((bf16[8,128,512]{2,1,0:T(8,128)(2,1)}), bf16[8,128,512]{2,1,0:T(8,128)(2,1)S(1)}, u32[]{:S(2)}, u32[]{:S(2)}) async-start(bf16[8,128,512]{2,1,0:T(8,128)(2,1)} %shard_map.77.refs_8_), calls=%async_computation.2 | async-start | bytes 2097152 | tf_op jit(solution)/shard_map/all_to_all | solution.py:276
  74.4 4.8 %collective-permute-start.7 = (bf16[4,4,256,128]{3,2,1,0:T(8,128)(2,1)}, bf16[4,4,256,128]{3,2,1,0:T(8,128)(2,1)S(1)}, u32[]{:S(2)}, u32[]{:S(2)}) collective-permute-start(bf16[4,4,256,128]{3,2,1,0:T(8,128)(2,1)} %get-tuple-element.7.refs_0_), channel_id=1, source_target_pairs={{0,16},{16,0},{1,17},{17,1},{2,18},{18,2},{3,19},{19,3},{4,20},{20... | collective-permute-start | bytes 3145736 | tf_op jit(solution)/shard_map/ppermute | solution.py:313
  76.3 4.9 %collective-permute-start.8 = (bf16[4,4,256,128]{3,2,1,0:T(8,128)(2,1)}, bf16[4,4,256,128]{3,2,1,0:T(8,128)(2,1)S(1)}, u32[]{:S(2)}, u32[]{:S(2)}) collective-permute-start(bf16[4,4,256,128]{3,2,1,0:T(8,128)(2,1)} %get-tuple-element.8.refs_1_), channel_id=1, source_target_pairs={{0,16},{16,0},{1,17},{17,1},{2,18},{18,2},{3,19},{19,3},{4,20},{20... | collective-permute-start | bytes 3145736 | tf_op jit(solution)/shard_map/ppermute | solution.py:313
  88.2 25.3 %all-to-all-start.3 = ((bf16[32,64,128]{2,1,0:T(8,128)(2,1)}), bf16[32,64,128]{2,1,0:T(8,128)(2,1)S(1)}, u32[]{:S(2)}, u32[]{:S(2)}) async-start(bf16[32,64,128]{2,1,0:T(8,128)(2,1)} %bitcast.4), calls=%async_computation.3 | async-start | bytes 1048576 | tf_op jit(solution)/shard_map/all_to_all | solution.py:276

commit v6 on v5

--- a/solution.py
+++ b/solution.py
@@ -1,4 +1,3 @@
-import functools
 import math
 
 import jax
@@ -34,16 +33,19 @@
 def attention_kernel(table_ref, query_ref, memory_ref, nbr_ref, *refs):
     out_ref = refs[-1]
     stretches, per_stretch = table_ref.shape
-    pieces = nbr_ref.shape[0] // (stretches * per_stretch)
     heads = query_ref.shape[1] // HD
     for u in range(stretches):
         rows = slice(u * STRETCH, (u + 1) * STRETCH)
-        places = [pl.ds(table_ref[u, j] * pieces, pieces) for j in range(per_stretch)]
+        places = [table_ref[u, j] for j in range(per_stretch)]
         for h in range(heads):
             cols = slice(h * HD, (h + 1) * HD)
             nbr_query, nbr_key, nbr_value = (
                 jnp.concatenate(
-                    [nbr_ref[place, kind, :, cols].reshape(NBLEN, HD) for place in places],
+                    [
+                        nbr_ref[x, place, kind, :, cols]
+                        for place in places
+                        for x in range(nbr_ref.shape[0])
+                    ],
                     axis=0,
                 )
                 for kind in range(3)
@@ -101,17 +103,20 @@
 
 
 def pack_kernel(query_ref, key_ref, value_ref, out_ref):
-    groups, _, _, span = out_ref.shape
+    quarters, highs, _, _, span = out_ref.shape
     for kind, ref in enumerate((query_ref, key_ref, value_ref)):
-        for g in range(groups):
-            out_ref[g, kind] = ref[:, g * span : (g + 1) * span]
-
-
-def pack(query, key, value, groups):
+        for x in range(quarters):
+            for y in range(highs):
+                at = (y * quarters + x) * span
+                out_ref[x, y, kind] = ref[:, at : at + span]
+
+
+def pack(query, key, value, quarters, highs):
     rows, cols = query.shape
+    span = cols // (quarters * highs)
     return pl.pallas_call(
         pack_kernel,
-        out_shape=jax.ShapeDtypeStruct((groups, 3, rows, cols // groups), query.dtype),
+        out_shape=jax.ShapeDtypeStruct((quarters, highs, 3, rows, span), query.dtype),
         in_specs=[VMEM] * 3,
         out_specs=VMEM,
         compiler_params=PARAMS,
@@ -142,13 +147,13 @@
 
 
 def regroup_kernel(folded_ref, out_ref):
-    senders, quarters, quarter, width = folded_ref.shape
+    quarters, senders, quarter, width = folded_ref.shape
     part = width // 4
     for x in range(quarters):
         for k in range(2):
             out_ref[x, k * quarter : (k + 1) * quarter] = jnp.concatenate(
                 [
-                    folded_ref[s, x, :, at * part : (at + 1) * part]
+                    folded_ref[x, s, :, at * part : (at + 1) * part]
                     for at in (k, 2 + k)
                     for s in range(senders)
                 ],
@@ -157,7 +162,7 @@
 
 
 def regroup(folded):
-    _, quarters, quarter, width = folded.shape
+    quarters, _, quarter, width = folded.shape
     return pl.pallas_call(
         regroup_kernel,
         out_shape=jax.ShapeDtypeStruct((quarters, 2 * quarter, width), folded.dtype),
@@ -192,12 +197,12 @@
     out_ref = refs[-1]
     stacks = len(refs) // 2
     plane = plane_ref[0]
-    sides, quarters, tokens, span = context_ref.shape
+    quarters, sides, tokens, span = context_ref.shape
     width = refs[0].shape[-1]
     middle, half, part = width // 2, tokens // 2, width // 4
     planes = TOGETHER * stacks
     left = [
-        jnp.concatenate([context_ref[s, x] for s in range(sides)], axis=0)
+        jnp.concatenate([context_ref[x, s] for s in range(sides)], axis=0)
         for x in range(quarters)
     ]
 
@@ -223,17 +228,19 @@
                 for piece in range(2):
                     own = slice(i * width + piece * part, i * width + (piece + 1) * part)
                     sib = slice(own.start + middle, own.stop + middle)
-                    out_ref[s, 2 * target + piece] = jnp.concatenate(
+                    x = 2 * lax.rem(target, 2) + piece
+                    out_ref[x, s, lax.div(target, 2)] = jnp.concatenate(
                         [upper[:, own], upper[:, sib], lower[:, own], lower[:, sib]], axis=1
                     )
 
 
 def project(plane, context, own, sib):
-    sides, _, tokens, _ = context.shape
+    quarters, sides, tokens, _ = context.shape
+    highs = 2 * TOGETHER * len(own) // quarters
     return pl.pallas_call(
         project_kernel,
         out_shape=jax.ShapeDtypeStruct(
-            (sides, 2 * TOGETHER * len(own), tokens // 2, own[0].shape[-1]), jnp.bfloat16
+            (quarters, sides, highs, tokens // 2, own[0].shape[-1]), jnp.bfloat16
         ),
         in_specs=[pl.BlockSpec(memory_space=pltpu.SMEM)] + [VMEM] * (1 + len(own) + len(sib)),
         out_specs=VMEM,
@@ -242,18 +249,21 @@
 
 
 def add_kernel(core_ref, partial_ref, out_ref):
-    sides, senders, quarters, half, width = partial_ref.shape
+    quarters, sides, senders, half, width = partial_ref.shape
     middle, part = width // 2, width // 4
-    for s in range(sides):
+    together = width // (part * sides)
+    for first in range(0, quarters, together):
         sums = []
-        for x in range(quarters):
-            total = partial_ref[s, 0, x].astype(jnp.float32)
-            for sender in range(1, senders):
-                total += partial_ref[s, sender, x].astype(jnp.float32)
-            sums.append(total.astype(jnp.bfloat16))
+        for x in range(first, first + together):
+            for s in range(sides):
+                total = partial_ref[x, s, 0].astype(jnp.float32)
+                for sender in range(1, senders):
+                    total += partial_ref[x, s, sender].astype(jnp.float32)
+                sums.append(total.astype(jnp.bfloat16))
         for side in range(2):
             core = core_ref[0] if side == 0 else 1 - core_ref[0]
-            cols = pl.ds(pl.multiple_of((core * sides + s) * width, width), width)
+            at = (core * (quarters // together) + first // together) * width
+            cols = pl.ds(pl.multiple_of(at, width), width)
             for low in range(2):
                 at = low * middle + side * part
                 out_ref[low * half : (low + 1) * half, cols] = jnp.concatenate(
@@ -262,7 +272,7 @@
 
 
 def add(core, partial):
-    sides, _, quarters, half, width = partial.shape
+    quarters, sides, _, half, width = partial.shape
     return pl.pallas_call(
         add_kernel,
         out_shape=jax.ShapeDtypeStruct((2 * half, sides * quarters * width // 2), jnp.bfloat16),
@@ -273,7 +283,10 @@
 
 
 def exchange(value, axes):
-    return lax.all_to_all(value, axes, split_axis=0, concat_axis=0, tiled=True)
+    shape = value.shape
+    value = value.reshape(-1, *shape[len(axes) :])
+    value = lax.all_to_all(value, axes, split_axis=0, concat_axis=0, tiled=True)
+    return value.reshape(shape)
 
 
 OFFSETS = (0, -1, 1, -2, 2, -3, 3, -4)
@@ -298,34 +311,29 @@
     neighbour_value,
     neighbour_table,
     output_weight,
-    *,
-    groups,
 ):
-    folded = exchange(fold(output_weight, 8), ("yl", "x"))
-    blocks = ring(regroup(folded.reshape(2, 4, *folded.shape[1:])), "z", 8)
-
-    neighbours = pack(neighbour_query, neighbour_key, neighbour_value, groups)
-    neighbours = exchange(neighbours, TENSOR)
+    folded = fold(output_weight, 8)
+    folded = exchange(folded.reshape(4, 2, *folded.shape[1:]), ("x", "yl"))
+    blocks = ring(regroup(folded), "z", 8)
+
+    neighbours = pack(neighbour_query, neighbour_key, neighbour_value, 4, 4)
+    neighbours = exchange(neighbours, ("x", "yh"))
     table = neighbour_table & 3
     context = attention(table, decoder_query, decoder_memory, neighbours, blocks[-3:-1])
     context = repeat(context, 8, blocks[-1:])
     own = stack(blocks, context)
     sib = [lax.ppermute(block, "c", [(0, 1), (1, 0)]) for block in own]
-    context = exchange(context, ("yl", "x"))
-    context = context.reshape(2, 4, *context.shape[1:])
+    context = exchange(context.reshape(4, 2, *context.shape[1:]), ("x", "yl"))
     plane = lax.axis_index("z").astype(jnp.int32).reshape(1)
-    partial = project(plane, context, own, sib)
-    shape = partial.shape
-    partial = exchange(partial.reshape(2 * groups, *shape[2:]), ("yl", "yh", "x"))
+    partial = exchange(project(plane, context, own, sib), ("x", "yl", "yh"))
     core = lax.axis_index("c").astype(jnp.int32).reshape(1)
-    return add(core, partial.reshape(2, 4, 4, *shape[2:]))
+    return add(core, partial)
 
 
 def solution(mesh):
-    groups = mesh.shape["tensor"]
     inner = Mesh(mesh.devices.reshape(8, 2, 2, 4, 4), AXES)
     return jax.shard_map(
-        functools.partial(local, groups=groups),
+        local,
         mesh=inner,
         in_specs=(
             P(DP, TENSOR),

time: 115 us -> 114 us (level)
  the two profiles are of different devices: /device:TPU:8 before, /device:TPU:16 now
where the time goes in v6:
time: 114 us; the launch traced here: 113 us
  starting transfers between devices  58.4 us (51%)
  waiting for transfers between devices  37 us (32%)
  Pallas kernels  12.4 us (11%)
  local copies, waits for them, and re-layouts  5.49 us (5%)
    all_to_all x4, starting transfers between devices, exchange(): value = lax.all_to_all(value, axes, split_axis=0, concat_axis=0, tiled=True)  25.4 us
    all_to_all x4, waiting for transfers between devices, exchange(): value = lax.all_to_all(value, axes, split_axis=0, concat_axis=0, tiled=True)  23.4 us
    ppermute x3, starting transfers between devices, ring(): ahead = lax.ppermute(ahead, axis, down)  18.8 us
    ppermute x3, starting transfers between devices, ring(): behind = lax.ppermute(behind, axis, up)  7.95 us
    ppermute x3, waiting for transfers between devices, ring(): behind = lax.ppermute(behind, axis, up)  6.19 us
    unnamed x22, local copies, waits for them, and re-layouts  5.49 us
    ppermute x1, waiting for transfers between devices, ring(): return blocks + [lax.ppermute(behind, axis, up)]  4.66 us
    ppermute x2, starting transfers between devices, local(): sib = [lax.ppermute(block, 'c', [(0, 1), (1, 0)]) for block in own]  4.31 us
  transfers between devices with their start and end apart: 13, of which 10 were waited for; matrix products, arithmetic and copies ran while one was open for 0% of the time, Pallas kernels for 5%

profile of v6, /device:TPU:16, one launch (start us, length us, event | category | flops | bytes accessed | tf_op | source)
XLA Modules:
  0.0 113.5 jit_solution(13768057635607338926)
XLA Ops:
  2.0 5.3 %all-to-all-start.1 = ((bf16[8,128,128]{2,1,0:T(8,128)(2,1)}), bf16[8,128,128]{2,1,0:T(8,128)(2,1)S(1)}, u32[]{:S(2)}, u32[]{:S(2)}) async-start(bf16[8,128,128]{2,1,0:T(8,128)(2,1)} %shard_map.74), calls=%async_computation.1 | async-start | bytes 524288 | tf_op jit(solution)/shard_map/all_to_all | solution.py:288
  10.4 1.3 %shard_map.73 = bf16[4,4,3,32,512]{4,3,2,1,0:T(8,128)(2,1)} custom-call(bf16[32,8192]{1,0:T(8,128)(2,1)S(1)} %copy-done, bf16[32,8192]{1,0:T(8,128)(2,1)S(1)} %copy-done.1, bf16[32,8192]{1,0:T(8,128)(2,1)S(1)} %copy-done.2), custom_call_target="tpu_custom_call" | custom-call | tf_op jit(solution)/shard_map/pallas_call | solution.py:117
  11.7 2.9 %all-to-all-done.1 = bf16[8,128,128]{2,1,0:T(8,128)(2,1)S(1)} async-done(((bf16[8,128,128]{2,1,0:T(8,128)(2,1)}), bf16[8,128,128]{2,1,0:T(8,128)(2,1)S(1)}, u32[]{:S(2)}, u32[]{:S(2)}) %all-to-all-start.1) | async-done | bytes 262176 | tf_op jit(solution)/shard_map/all_to_all | solution.py:288
  14.6 7.4 %all-to-all-start = ((bf16[16,3,32,512]{3,2,1,0:T(8,128)(2,1)}), bf16[16,3,32,512]{3,2,1,0:T(8,128)(2,1)S(1)}, u32[]{:S(2)}, u32[]{:S(2)}) async-start(bf16[16,3,32,512]{3,2,1,0:T(8,128)(2,1)} %bitcast.2), calls=%async_computation | async-start | bytes 3145728 | tf_op jit(solution)/shard_map/all_to_all | solution.py:288
  22.1 4.1 %collective-permute-start = (bf16[4,256,128]{2,1,0:T(8,128)(2,1)S(1)}, bf16[4,256,128]{2,1,0:T(8,128)(2,1)S(1)}, u32[]{:S(2)}, u32[]{:S(2)}) collective-permute-start(bf16[4,256,128]{2,1,0:T(8,128)(2,1)S(1)} %shard_map.75.refs_0_), channel_id=1, source_target_pairs={{0,64},{64,128},{128,192},{192,256},{256,320},{320,384},{384,448},... | collective-permute-start | bytes 786440 | tf_op jit(solution)/shard_map/ppermute | solution.py:300
  26.2 8.6 %collective-permute-start.3 = (bf16[4,256,128]{2,1,0:T(8,128)(2,1)S(1)}, bf16[4,256,128]{2,1,0:T(8,128)(2,1)S(1)}, u32[]{:S(2)}, u32[]{:S(2)}) collective-permute-start(bf16[4,256,128]{2,1,0:T(8,128)(2,1)S(1)} %shard_map.75.refs_0_), channel_id=1, source_target_pairs={{0,448},{64,0},{128,64},{192,128},{256,192},{320,256},{384,320},{4... | collective-permute-start | bytes 786440 | tf_op jit(solution)/shard_map/ppermute | solution.py:301
  34.8 2.8 %collective-permute-done.refs_1_ = bf16[4,256,128]{2,1,0:T(8,128)(2,1)S(1)} collective-permute-done((bf16[4,256,128]{2,1,0:T(8,128)(2,1)S(1)}, bf16[4,256,128]{2,1,0:T(8,128)(2,1)S(1)}, u32[]{:S(2)}, u32[]{:S(2)}) %collective-permute-start) | collective-permute-done | bytes 262176 | tf_op jit(solution)/shard_map/ppermute | solution.py:300
  37.6 1.9 %collective-permute-start.1 = (bf16[4,256,128]{2,1,0:T(8,128)(2,1)S(1)}, bf16[4,256,128]{2,1,0:T(8,128)(2,1)S(1)}, u32[]{:S(2)}, u32[]{:S(2)}) collective-permute-start(bf16[4,256,128]{2,1,0:T(8,128)(2,1)S(1)} %collective-permute-done.refs_1_), channel_id=1, source_target_pairs={{0,64},{64,128},{128,192},{192,256},{256,320},{320,384},{384,448},... | collective-permute-start | bytes 786440 | tf_op jit(solution)/shard_map/ppermute | solution.py:300
  39.5 5.1 %collective-permute-start.4 = (bf16[4,256,128]{2,1,0:T(8,128)(2,1)S(1)}, bf16[4,256,128]{2,1,0:T(8,128)(2,1)S(1)}, u32[]{:S(2)}, u32[]{:S(2)}) collective-permute-start(bf16[4,256,128]{2,1,0:T(8,128)(2,1)S(1)} %collective-permute-done.3.refs_2_), channel_id=1, source_target_pairs={{0,448},{64,0},{128,64},{192,128},{256,192},{320,256},{384,320},{4... | collective-permute-start | bytes 786440 | tf_op jit(solution)/shard_map/ppermute | solution.py:301
  44.7 2.4 %collective-permute-done.1.refs_3_ = bf16[4,256,128]{2,1,0:T(8,128)(2,1)S(1)} collective-permute-done((bf16[4,256,128]{2,1,0:T(8,128)(2,1)S(1)}, bf16[4,256,128]{2,1,0:T(8,128)(2,1)S(1)}, u32[]{:S(2)}, u32[]{:S(2)}) %collective-permute-start.1) | collective-permute-done | bytes 262176 | tf_op jit(solution)/shard_map/ppermute | solution.py:300
  47.1 1.9 %collective-permute-start.2 = (bf16[4,256,128]{2,1,0:T(8,128)(2,1)S(1)}, bf16[4,256,128]{2,1,0:T(8,128)(2,1)S(1)}, u32[]{:S(2)}, u32[]{:S(2)}) collective-permute-start(bf16[4,256,128]{2,1,0:T(8,128)(2,1)S(1)} %collective-permute-done.1.refs_3_), channel_id=1, source_target_pairs={{0,64},{64,128},{128,192},{192,256},{256,320},{320,384},{384,448},... | collective-permute-start | bytes 786440 | tf_op jit(solution)/shard_map/ppermute | solution.py:300
  49.7 5.1 %collective-permute-start.5 = (bf16[4,256,128]{2,1,0:T(8,128)(2,1)S(1)}, bf16[4,256,128]{2,1,0:T(8,128)(2,1)S(1)}, u32[]{:S(2)}, u32[]{:S(2)}) collective-permute-start(bf16[4,256,128]{2,1,0:T(8,128)(2,1)S(1)} %collective-permute-done.4.refs_4_), channel_id=1, source_target_pairs={{0,448},{64,0},{128,64},{192,128},{256,192},{320,256},{384,320},{4... | collective-permute-start | bytes 786440 | tf_op jit(solution)/shard_map/ppermute | solution.py:301
  56.5 1.9 %collective-permute-start.6 = (bf16[4,256,128]{2,1,0:T(8,128)(2,1)S(1)}, bf16[4,256,128]{2,1,0:T(8,128)(2,1)S(1)}, u32[]{:S(2)}, u32[]{:S(2)}) collective-permute-start(bf16[4,256,128]{2,1,0:T(8,128)(2,1)S(1)} %collective-permute-done.2.refs_0_.refs_5_), channel_id=1, source_target_pairs={{0,64},{64,128},{128,192},{192,256},{256,320},{320,384},{384,448},... | collective-permute-start | bytes 786440 | tf_op jit(solution)/shard_map/ppermute | solution.py:303
  58.7 2.6 %shard_map.76.value_ref = bf16[128,512]{1,0:T(8,128)(2,1)S(1)} custom-call(s32[2,2]{1,0:T(2,128)S(1)} %broadcast_and_fusion.table_ref, bf16[128,512]{1,0:T(8,128)(2,1)S(1)} %copy-done.9, bf16[2,128,512]{2,1,0:T(8,128)(2,1)S(1)} %copy-done.3, bf16[4,4,3,32,512]{4,3,2,1,0:T(8,128)(2,1)S(1)} %bitcast.8, ...), custom_call_target="tpu_custom_call" | custom-call | tf_op jit(solution)/shard_map/pallas_call | solution.py:74
  61.4 4.7 %collective-permute-done.6.refs_0_.refs_7_ = bf16[4,256,128]{2,1,0:T(8,128)(2,1)S(1)} collective-permute-done((bf16[4,256,128]{2,1,0:T(8,128)(2,1)S(1)}, bf16[4,256,128]{2,1,0:T(8,128)(2,1)S(1)}, u32[]{:S(2)}, u32[]{:S(2)}) %collective-permute-start.6) | collective-permute-done | bytes 262176 | tf_op jit(solution)/shard_map/ppermute | solution.py:303
  67.1 5.2 %all-to-all-start.2 = ((bf16[8,128,512]{2,1,0:T(8,128)(2,1)}), bf16[8,128,512]{2,1,0:T(8,128)(2,1)S(1)}, u32[]{:S(2)}, u32[]{:S(2)}) async-start(bf16[8,128,512]{2,1,0:T(8,128)(2,1)} %shard_map.77.refs_8_), calls=%async_computation.2 | async-start | bytes 2097152 | tf_op jit(solution)/shard_map/all_to_all | solution.py:288
  72.3 1.4 %shard_map.78 = (bf16[4,4,256,128]{3,2,1,0:T(8,128)(2,1)}, bf16[4,4,256,128]{3,2,1,0:T(8,128)(2,1)}) custom-call(bf16[4,256,128]{2,1,0:T(8,128)(2,1)S(1)} %shard_map.75.refs_0_, bf16[4,256,128]{2,1,0:T(8,128)(2,1)S(1)} %collective-permute-done.refs_1_, bf16[4,256,128]{2,1,0:T(8,128)(2,1)S(1)} %collective-permute-done.3.refs_2_, ...), custom_call_target="tpu_custom_call" | custom-call | tf_op jit(solution)/shard_map/pallas_call | solution.py:187
  73.7 1.9 %collective-permute-start.7 = (bf16[4,4,256,128]{3,2,1,0:T(8,128)(2,1)}, bf16[4,4,256,128]{3,2,1,0:T(8,128)(2,1)S(1)}, u32[]{:S(2)}, u32[]{:S(2)}) collective-permute-start(bf16[4,4,256,128]{3,2,1,0:T(8,128)(2,1)} %get-tuple-element.7.refs_0_), channel_id=1, source_target_pairs={{0,16},{16,0},{1,17},{17,1},{2,18},{18,2},{3,19},{19,3},{4,20},{20... | collective-permute-start | bytes 3145736 | tf_op jit(solution)/shard_map/ppermute | solution.py:325
  75.6 2.4 %collective-permute-start.8 = (bf16[4,4,256,128]{3,2,1,0:T(8,128)(2,1)}, bf16[4,4,256,128]{3,2,1,0:T(8,128)(2,1)S(1)}, u32[]{:S(2)}, u32[]{:S(2)}) collective-permute-start(bf16[4,4,256,128]{3,2,1,0:T(8,128)(2,1)} %get-tuple-element.8.refs_1_), channel_id=1, source_target_pairs={{0,16},{16,0},{1,17},{17,1},{2,18},{18,2},{3,19},{19,3},{4,20},{20... | collective-permute-start | bytes 3145736 | tf_op jit(solution)/shard_map/ppermute | solution.py:325
  78.5 2.1 %collective-permute-done.8.refs_3_ = bf16[4,4,256,128]{3,2,1,0:T(8,128)(2,1)S(1)} collective-permute-done((bf16[4,4,256,128]{3,2,1,0:T(8,128)(2,1)}, bf16[4,4,256,128]{3,2,1,0:T(8,128)(2,1)S(1)}, u32[]{:S(2)}, u32[]{:S(2)}) %collective-permute-start.8) | collective-permute-done | bytes 1048608 | tf_op jit(solution)/shard_map/ppermute | solution.py:325
  80.5 3.9 %all-to-all-done.2 = bf16[8,128,512]{2,1,0:T(8,128)(2,1)S(1)} async-done(((bf16[8,128,512]{2,1,0:T(8,128)(2,1)}), bf16[8,128,512]{2,1,0:T(8,128)(2,1)S(1)}, u32[]{:S(2)}, u32[]{:S(2)}) %all-to-all-start.2) | async-done | bytes 1048608 | tf_op jit(solution)/shard_map/all_to_all | solution.py:288
  84.4 4.0 %shard_map.79 = bf16[4,2,4,64,128]{4,3,2,1,0:T(8,128)(2,1)} custom-call(s32[1]{0:T(128)} %bitcast.1.plane_ref, bf16[4,2,128,512]{3,2,1,0:T(8,128)(2,1)S(1)} %bitcast.9, bf16[4,4,256,128]{3,2,1,0:T(8,128)(2,1)} %get-tuple-element.7.refs_0_, bf16[4,4,256,128]{3,2,1,0:T(8,128)(2,1)} %get-tuple-element.8.refs_1_, ...), custom_call_target="tpu_custom_call" | custom-call | tf_op jit(solution)/shard_map/pallas_call | solution.py:240
  88.4 7.5 %all-to-all-start.3 = ((bf16[32,64,128]{2,1,0:T(8,128)(2,1)}), bf16[32,64,128]{2,1,0:T(8,128)(2,1)S(1)}, u32[]{:S(2)}, u32[]{:S(2)}) async-start(bf16[32,64,128]{2,1,0:T(8,128)(2,1)} %bitcast.6), calls=%async_computation.3 | async-start | bytes 1048576 | tf_op jit(solution)/shard_map/all_to_all | solution.py:288
  95.9 16.7 %all-to-all-done.3 = bf16[32,64,128]{2,1,0:T(8,128)(2,1)S(1)} async-done(((bf16[32,64,128]{2,1,0:T(8,128)(2,1)}), bf16[32,64,128]{2,1,0:T(8,128)(2,1)S(1)}, u32[]{:S(2)}, u32[]{:S(2)}) %all-to-all-start.3) | async-done | bytes 524320 | tf_op jit(solution)/shard_map/all_to_all | solution.py:288
  (33 shorter events, 10.2 us)
Async XLA Ops:
  0.0 0.9 copy-start.8
  2.0 12.6 %all-to-all-start.1 = ((bf16[8,128,128]{2,1,0:T(8,128)(2,1)}), bf16[8,128,128]{2,1,0:T(8,128)(2,1)S(1)}, u32[]{:S(2)}, u32[]{:S(2)}) async-start(bf16[8,128,128]{2,1,0:T(8,128)(2,1)} %shard_map.74), calls=%async_computation.1 | async-start | bytes 524288 | tf_op jit(solution)/shard_map/all_to_all | solution.py:288
  7.3 1.0 copy-start
  8.3 1.0 copy-start.1
  9.4 1.0 copy-start.2
  14.6 43.9 %copy-start.10 = (s32[2,2]{1,0:T(2,128)S(1)}, s32[2,2]{1,0:T(2,128)}, u32[]{:S(2)}) copy-start(s32[2,2]{1,0:T(2,128)} %param.12) | copy-start | bytes 52
  14.6 44.2 %copy-start.3 = (bf16[2,128,512]{2,1,0:T(8,128)(2,1)S(1)}, bf16[2,128,512]{2,1,0:T(8,128)(2,1)}, u32[]{:S(2)}) copy-start(bf16[2,128,512]{2,1,0:T(8,128)(2,1)} %memory_ref.1) | copy-start | bytes 786436
  14.6 44.2 %copy-start.9 = (bf16[128,512]{1,0:T(8,128)(2,1)S(1)}, bf16[128,512]{1,0:T(8,128)(2,1)}, u32[]{:S(2)}) copy-start(bf16[128,512]{1,0:T(8,128)(2,1)} %query_ref.3) | copy-start | bytes 393220
  14.6 44.2 %all-to-all-start = ((bf16[16,3,32,512]{3,2,1,0:T(8,128)(2,1)}), bf16[16,3,32,512]{3,2,1,0:T(8,128)(2,1)S(1)}, u32[]{:S(2)}, u32[]{:S(2)}) async-start(bf16[16,3,32,512]{3,2,1,0:T(8,128)(2,1)} %bitcast.2), calls=%async_computation | async-start | bytes 3145728 | tf_op jit(solution)/shard_map/all_to_all | solution.py:288
  22.1 15.5 %collective-permute-start = (bf16[4,256,128]{2,1,0:T(8,128)(2,1)S(1)}, bf16[4,256,128]{2,1,0:T(8,128)(2,1)S(1)}, u32[]{:S(2)}, u32[]{:S(2)}) collective-permute-start(bf16[4,256,128]{2,1,0:T(8,128)(2,1)S(1)} %shard_map.75.refs_0_), channel_id=1, source_target_pairs={{0,64},{64,128},{128,192},{192,256},{256,320},{320,384},{384,448},... | collective-permute-start | bytes 786440 | tf_op jit(solution)/shard_map/ppermute | solution.py:300
  26.2 13.3 %collective-permute-start.3 = (bf16[4,256,128]{2,1,0:T(8,128)(2,1)S(1)}, bf16[4,256,128]{2,1,0:T(8,128)(2,1)S(1)}, u32[]{:S(2)}, u32[]{:S(2)}) collective-permute-start(bf16[4,256,128]{2,1,0:T(8,128)(2,1)S(1)} %shard_map.75.refs_0_), channel_id=1, source_target_pairs={{0,448},{64,0},{128,64},{192,128},{256,192},{320,256},{384,320},{4... | collective-permute-start | bytes 786440 | tf_op jit(solution)/shard_map/ppermute | solution.py:301
  37.6 9.5 %collective-permute-start.1 = (bf16[4,256,128]{2,1,0:T(8,128)(2,1)S(1)}, bf16[4,256,128]{2,1,0:T(8,128)(2,1)S(1)}, u32[]{:S(2)}, u32[]{:S(2)}) collective-permute-start(bf16[4,256,128]{2,1,0:T(8,128)(2,1)S(1)} %collective-permute-done.refs_1_), channel_id=1, source_target_pairs={{0,64},{64,128},{128,192},{192,256},{256,320},{320,384},{384,448},... | collective-permute-start | bytes 786440 | tf_op jit(solution)/shard_map/ppermute | solution.py:300
  39.5 10.2 %collective-permute-start.4 = (bf16[4,256,128]{2,1,0:T(8,128)(2,1)S(1)}, bf16[4,256,128]{2,1,0:T(8,128)(2,1)S(1)}, u32[]{:S(2)}, u32[]{:S(2)}) collective-permute-start(bf16[4,256,128]{2,1,0:T(8,128)(2,1)S(1)} %collective-permute-done.3.refs_2_), channel_id=1, source_target_pairs={{0,448},{64,0},{128,64},{192,128},{256,192},{320,256},{384,320},{4... | collective-permute-start | bytes 786440 | tf_op jit(solution)/shard_map/ppermute | solution.py:301
  47.1 9.5 %collective-permute-start.2 = (bf16[4,256,128]{2,1,0:T(8,128)(2,1)S(1)}, bf16[4,256,128]{2,1,0:T(8,128)(2,1)S(1)}, u32[]{:S(2)}, u32[]{:S(2)}) collective-permute-start(bf16[4,256,128]{2,1,0:T(8,128)(2,1)S(1)} %collective-permute-done.1.refs_3_), channel_id=1, source_target_pairs={{0,64},{64,128},{128,192},{192,256},{256,320},{320,384},{384,448},... | collective-permute-start | bytes 786440 | tf_op jit(solution)/shard_map/ppermute | solution.py:300
  49.0 0.7 copy-start.4
  49.7 9.0 %collective-permute-start.5 = (bf16[4,256,128]{2,1,0:T(8,128)(2,1)S(1)}, bf16[4,256,128]{2,1,0:T(8,128)(2,1)S(1)}, u32[]{:S(2)}, u32[]{:S(2)}) collective-permute-start(bf16[4,256,128]{2,1,0:T(8,128)(2,1)S(1)} %collective-permute-done.4.refs_4_), channel_id=1, source_target_pairs={{0,448},{64,0},{128,64},{192,128},{256,192},{320,256},{384,320},{4... | collective-permute-start | bytes 786440 | tf_op jit(solution)/shard_map/ppermute | solution.py:301
  54.9 0.7 copy-start.6
  56.5 9.5 %collective-permute-start.6 = (bf16[4,256,128]{2,1,0:T(8,128)(2,1)S(1)}, bf16[4,256,128]{2,1,0:T(8,128)(2,1)S(1)}, u32[]{:S(2)}, u32[]{:S(2)}) collective-permute-start(bf16[4,256,128]{2,1,0:T(8,128)(2,1)S(1)} %collective-permute-done.2.refs_0_.refs_5_), channel_id=1, source_target_pairs={{0,64},{64,128},{128,192},{192,256},{256,320},{320,384},{384,448},... | collective-permute-start | bytes 786440 | tf_op jit(solution)/shard_map/ppermute | solution.py:303
  61.3 10.9 %copy-start.5 = (bf16[4,256,128]{2,1,0:T(8,128)(2,1)S(1)}, bf16[4,256,128]{2,1,0:T(8,128)(2,1)}, u32[]{:S(2)}) copy-start(bf16[4,256,128]{2,1,0:T(8,128)(2,1)} %copy-done.4) | copy-start | bytes 786436
  61.3 10.9 %copy-start.7 = (bf16[4,256,128]{2,1,0:T(8,128)(2,1)S(1)}, bf16[4,256,128]{2,1,0:T(8,128)(2,1)}, u32[]{:S(2)}) copy-start(bf16[4,256,128]{2,1,0:T(8,128)(2,1)} %copy-done.6) | copy-start | bytes 786436
  67.1 17.3 %all-to-all-start.2 = ((bf16[8,128,512]{2,1,0:T(8,128)(2,1)}), bf16[8,128,512]{2,1,0:T(8,128)(2,1)S(1)}, u32[]{:S(2)}, u32[]{:S(2)}) async-start(bf16[8,128,512]{2,1,0:T(8,128)(2,1)} %shard_map.77.refs_8_), calls=%async_computation.2 | async-start | bytes 2097152 | tf_op jit(solution)/shard_map/all_to_all | solution.py:288
  73.7 4.8 %collective-permute-start.7 = (bf16[4,4,256,128]{3,2,1,0:T(8,128)(2,1)}, bf16[4,4,256,128]{3,2,1,0:T(8,128)(2,1)S(1)}, u32[]{:S(2)}, u32[]{:S(2)}) collective-permute-start(bf16[4,4,256,128]{3,2,1,0:T(8,128)(2,1)} %get-tuple-element.7.refs_0_), channel_id=1, source_target_pairs={{0,16},{16,0},{1,17},{17,1},{2,18},{18,2},{3,19},{19,3},{4,20},{20... | collective-permute-start | bytes 3145736 | tf_op jit(solution)/shard_map/ppermute | solution.py:325
  75.6 4.9 %collective-permute-start.8 = (bf16[4,4,256,128]{3,2,1,0:T(8,128)(2,1)}, bf16[4,4,256,128]{3,2,1,0:T(8,128)(2,1)S(1)}, u32[]{:S(2)}, u32[]{:S(2)}) collective-permute-start(bf16[4,4,256,128]{3,2,1,0:T(8,128)(2,1)} %get-tuple-element.8.refs_1_), channel_id=1, source_target_pairs={{0,16},{16,0},{1,17},{17,1},{2,18},{18,2},{3,19},{19,3},{4,20},{20... | collective-permute-start | bytes 3145736 | tf_op jit(solution)/shard_map/ppermute | solution.py:325
  88.4 24.2 %all-to-all-start.3 = ((bf16[32,64,128]{2,1,0:T(8,128)(2,1)}), bf16[32,64,128]{2,1,0:T(8,128)(2,1)S(1)}, u32[]{:S(2)}, u32[]{:S(2)}) async-start(bf16[32,64,128]{2,1,0:T(8,128)(2,1)} %bitcast.6), calls=%async_computation.3 | async-start | bytes 1048576 | tf_op jit(solution)/shard_map/all_to_all | solution.py:288

commit v7 on v6

--- a/solution.py
+++ b/solution.py
@@ -68,6 +68,7 @@
 ANY = pl.BlockSpec(memory_space=pl.ANY)
 HBM = pl.BlockSpec(memory_space=pltpu.HBM)
 PARAMS = pltpu.CompilerParams(vmem_limit_bytes=16 * 2**20)
+WIDE = pltpu.CompilerParams(vmem_limit_bytes=60 * 2**20)
 
 
 def attention(table, query, memory, neighbours, after):
@@ -102,24 +103,48 @@
     )(value, *after)
 
 
-def pack_kernel(query_ref, key_ref, value_ref, out_ref):
+def pack_kernel(query_ref, key_ref, value_ref, out_ref, held, packed, in_sems, out_sems):
     quarters, highs, _, _, span = out_ref.shape
-    for kind, ref in enumerate((query_ref, key_ref, value_ref)):
+    loads = [
+        pltpu.make_async_copy(ref, held.at[kind], in_sems.at[kind])
+        for kind, ref in enumerate((query_ref, key_ref, value_ref))
+    ]
+    stores = [
+        pltpu.make_async_copy(
+            packed.at[x, :, kind], out_ref.at[x, :, kind], out_sems.at[x, kind]
+        )
+        for kind in range(len(loads))
+        for x in range(quarters)
+    ]
+    for load in loads:
+        load.start()
+    for kind, load in enumerate(loads):
+        load.wait()
         for x in range(quarters):
             for y in range(highs):
                 at = (y * quarters + x) * span
-                out_ref[x, y, kind] = ref[:, at : at + span]
+                packed[x, y, kind] = held[kind, :, at : at + span]
+            stores[kind * quarters + x].start()
+    for store in stores:
+        store.wait()
 
 
 def pack(query, key, value, quarters, highs):
     rows, cols = query.shape
     span = cols // (quarters * highs)
+    shape = (quarters, highs, 3, rows, span)
     return pl.pallas_call(
         pack_kernel,
-        out_shape=jax.ShapeDtypeStruct((quarters, highs, 3, rows, span), query.dtype),
-        in_specs=[VMEM] * 3,
-        out_specs=VMEM,
-        compiler_params=PARAMS,
+        out_shape=jax.ShapeDtypeStruct(shape, query.dtype),
+        in_specs=[HBM] * 3,
+        out_specs=HBM,
+        scratch_shapes=[
+            pltpu.VMEM((3, rows, cols), query.dtype),
+            pltpu.VMEM(shape, query.dtype),
+            pltpu.SemaphoreType.DMA((3,)),
+            pltpu.SemaphoreType.DMA((quarters, 3)),
+        ],
+        compiler_params=WIDE,
     )(query, key, value)
 
 
@@ -289,7 +314,7 @@
     return value.reshape(shape)
 
 
-OFFSETS = (0, -1, 1, -2, 2, -3, 3, -4)
+OFFSETS = (0, -1, 1, -2, 2, -3, 3, 4)
 
 
 def ring(value, axis, size):
@@ -300,7 +325,7 @@
         behind = lax.ppermute(behind, axis, up)
         ahead = lax.ppermute(ahead, axis, down)
         blocks += [behind, ahead]
-    return blocks + [lax.ppermute(behind, axis, up)]
+    return blocks + [lax.ppermute(ahead, axis, down)]
 
 
 def local(

time: 114 us -> 113 us (level)
  starting transfers between devices: 58.4 us -> 63 us
  waiting for transfers between devices: 37 us -> 33.1 us
  local copies, waits for them, and re-layouts: 5.49 us -> 2.36 us
    ppermute x3, waiting for transfers between devices: 6.19 us -> 0.7 us  [ring(): behind = lax.ppermute(behind, axis, up)]
    ppermute x3, waiting for transfers between devices: 0.25 us -> 4.41 us  [ring(): ahead = lax.ppermute(ahead, axis, down)]
    ppermute x1, waiting for transfers between devices: 4.66 us -> 0.54 us  [ring(): return blocks + [lax.ppermute(ahead, axis, down)]]
    ppermute x1, starting transfers between devices: 1.91 us -> 5.59 us  [ring(): return blocks + [lax.ppermute(ahead, axis, down)]]
    ppermute x3, starting transfers between devices: 18.8 us -> 22 us  [ring(): ahead = lax.ppermute(ahead, axis, down)]
    unnamed x22 -> x16, local copies, waits for them, and re-layouts: 5.49 us -> 2.36 us
    ppermute x3, starting transfers between devices: 7.95 us -> 5.75 us  [ring(): behind = lax.ppermute(behind, axis, up)]
    all_to_all x4, waiting for transfers between devices: 23.4 us -> 25 us  [exchange(): value = lax.all_to_all(value, axes, split_axis=0, concat_axis=0, tiled=True)]
  transfers between devices with their start and end apart: 13 -> 13, of which waited for: 10 -> 10; matrix products, arithmetic and copies ran while one was open for 0% -> 0% of each run, Pallas kernels for 5% -> 6%
where the time goes in v7:
time: 113 us; the launch traced here: 112 us
  starting transfers between devices  63 us (56%)
  waiting for transfers between devices  33.1 us (29%)
  Pallas kernels  13.4 us (12%)
  local copies, waits for them, and re-layouts  2.36 us (2%)
    all_to_all x4, starting transfers between devices, exchange(): value = lax.all_to_all(value, axes, split_axis=0, concat_axis=0, tiled=True)  25.4 us
    all_to_all x4, waiting for transfers between devices, exchange(): value = lax.all_to_all(value, axes, split_axis=0, concat_axis=0, tiled=True)  25 us
    ppermute x3, starting transfers between devices, ring(): ahead = lax.ppermute(ahead, axis, down)  22 us
    ppermute x3, starting transfers between devices, ring(): behind = lax.ppermute(behind, axis, up)  5.75 us
    ppermute x1, starting transfers between devices, ring(): return blocks + [lax.ppermute(ahead, axis, down)]  5.59 us
    ppermute x3, waiting for transfers between devices, ring(): ahead = lax.ppermute(ahead, axis, down)  4.41 us
    ppermute x2, starting transfers between devices, local(): sib = [lax.ppermute(block, 'c', [(0, 1), (1, 0)]) for block in own]  4.31 us
    pallas_call x1, Pallas kernels, project(): pl.pallas_call(project_kernel, out_shape=jax.ShapeDtypeStruct((quarters,...  4 us
  transfers between devices with their start and end apart: 13, of which 10 were waited for; matrix products, arithmetic and copies ran while one was open for 0% of the time, Pallas kernels for 6%

profile of v7, /device:TPU:16, one launch (start us, length us, event | category | flops | bytes accessed | tf_op | source)
XLA Modules:
  0.0 112.0 jit_solution(12595999208764360306)
XLA Ops:
  1.9 5.3 %all-to-all-start.1 = ((bf16[8,128,128]{2,1,0:T(8,128)(2,1)}), bf16[8,128,128]{2,1,0:T(8,128)(2,1)S(1)}, u32[]{:S(2)}, u32[]{:S(2)}) async-start(bf16[8,128,128]{2,1,0:T(8,128)(2,1)} %shard_map.74), calls=%async_computation.1 | async-start | bytes 524288 | tf_op jit(solution)/shard_map/all_to_all | solution.py:313
  7.2 2.3 %shard_map.73 = bf16[4,4,3,32,512]{4,3,2,1,0:T(8,128)(2,1)} custom-call(bf16[32,8192]{1,0:T(8,128)(2,1)} %query_ref.2, bf16[32,8192]{1,0:T(8,128)(2,1)} %key_ref.1, bf16[32,8192]{1,0:T(8,128)(2,1)} %value_ref.1), custom_call_target="tpu_custom_call" | custom-call | tf_op jit(solution)/shard_map/pallas_call | solution.py:136
  9.6 4.9 %all-to-all-done.1 = bf16[8,128,128]{2,1,0:T(8,128)(2,1)S(1)} async-done(((bf16[8,128,128]{2,1,0:T(8,128)(2,1)}), bf16[8,128,128]{2,1,0:T(8,128)(2,1)S(1)}, u32[]{:S(2)}, u32[]{:S(2)}) %all-to-all-start.1) | async-done | bytes 262176 | tf_op jit(solution)/shard_map/all_to_all | solution.py:313
  14.5 7.4 %all-to-all-start = ((bf16[16,3,32,512]{3,2,1,0:T(8,128)(2,1)}), bf16[16,3,32,512]{3,2,1,0:T(8,128)(2,1)S(1)}, u32[]{:S(2)}, u32[]{:S(2)}) async-start(bf16[16,3,32,512]{3,2,1,0:T(8,128)(2,1)} %bitcast.12), calls=%async_computation | async-start | bytes 3145728 | tf_op jit(solution)/shard_map/all_to_all | solution.py:313
  22.1 10.8 %collective-permute-start.3 = (bf16[4,256,128]{2,1,0:T(8,128)(2,1)S(1)}, bf16[4,256,128]{2,1,0:T(8,128)(2,1)S(1)}, u32[]{:S(2)}, u32[]{:S(2)}) collective-permute-start(bf16[4,256,128]{2,1,0:T(8,128)(2,1)S(1)} %shard_map.75.refs_0_), channel_id=1, source_target_pairs={{0,448},{64,0},{128,64},{192,128},{256,192},{320,256},{384,320},{4... | collective-permute-start | bytes 786440 | tf_op jit(solution)/shard_map/ppermute | solution.py:326
  32.9 1.9 %collective-permute-start = (bf16[4,256,128]{2,1,0:T(8,128)(2,1)S(1)}, bf16[4,256,128]{2,1,0:T(8,128)(2,1)S(1)}, u32[]{:S(2)}, u32[]{:S(2)}) collective-permute-start(bf16[4,256,128]{2,1,0:T(8,128)(2,1)S(1)} %shard_map.75.refs_0_), channel_id=1, source_target_pairs={{0,64},{64,128},{128,192},{192,256},{256,320},{320,384},{384,448},... | collective-permute-start | bytes 786440 | tf_op jit(solution)/shard_map/ppermute | solution.py:325
  34.8 1.9 %collective-permute-done.3.refs_2_ = bf16[4,256,128]{2,1,0:T(8,128)(2,1)S(1)} collective-permute-done((bf16[4,256,128]{2,1,0:T(8,128)(2,1)S(1)}, bf16[4,256,128]{2,1,0:T(8,128)(2,1)S(1)}, u32[]{:S(2)}, u32[]{:S(2)}) %collective-permute-start.3) | collective-permute-done | bytes 262176 | tf_op jit(solution)/shard_map/ppermute | solution.py:326
  36.7 5.6 %collective-permute-start.4 = (bf16[4,256,128]{2,1,0:T(8,128)(2,1)S(1)}, bf16[4,256,128]{2,1,0:T(8,128)(2,1)S(1)}, u32[]{:S(2)}, u32[]{:S(2)}) collective-permute-start(bf16[4,256,128]{2,1,0:T(8,128)(2,1)S(1)} %collective-permute-done.3.refs_2_), channel_id=1, source_target_pairs={{0,448},{64,0},{128,64},{192,128},{256,192},{320,256},{384,320},{4... | collective-permute-start | bytes 786440 | tf_op jit(solution)/shard_map/ppermute | solution.py:326
  42.3 1.9 %collective-permute-start.1 = (bf16[4,256,128]{2,1,0:T(8,128)(2,1)S(1)}, bf16[4,256,128]{2,1,0:T(8,128)(2,1)S(1)}, u32[]{:S(2)}, u32[]{:S(2)}) collective-permute-start(bf16[4,256,128]{2,1,0:T(8,128)(2,1)S(1)} %collective-permute-done.refs_1_), channel_id=1, source_target_pairs={{0,64},{64,128},{128,192},{192,256},{256,320},{320,384},{384,448},... | collective-permute-start | bytes 786440 | tf_op jit(solution)/shard_map/ppermute | solution.py:325
  44.3 1.9 %collective-permute-done.4.refs_4_ = bf16[4,256,128]{2,1,0:T(8,128)(2,1)S(1)} collective-permute-done((bf16[4,256,128]{2,1,0:T(8,128)(2,1)S(1)}, bf16[4,256,128]{2,1,0:T(8,128)(2,1)S(1)}, u32[]{:S(2)}, u32[]{:S(2)}) %collective-permute-start.4) | collective-permute-done | bytes 262176 | tf_op jit(solution)/shard_map/ppermute | solution.py:326
  46.2 5.6 %collective-permute-start.5 = (bf16[4,256,128]{2,1,0:T(8,128)(2,1)S(1)}, bf16[4,256,128]{2,1,0:T(8,128)(2,1)S(1)}, u32[]{:S(2)}, u32[]{:S(2)}) collective-permute-start(bf16[4,256,128]{2,1,0:T(8,128)(2,1)S(1)} %collective-permute-done.4.refs_4_), channel_id=1, source_target_pairs={{0,448},{64,0},{128,64},{192,128},{256,192},{320,256},{384,320},{4... | collective-permute-start | bytes 786440 | tf_op jit(solution)/shard_map/ppermute | solution.py:326
  52.5 1.9 %collective-permute-start.2 = (bf16[4,256,128]{2,1,0:T(8,128)(2,1)S(1)}, bf16[4,256,128]{2,1,0:T(8,128)(2,1)S(1)}, u32[]{:S(2)}, u32[]{:S(2)}) collective-permute-start(bf16[4,256,128]{2,1,0:T(8,128)(2,1)S(1)} %collective-permute-done.1.refs_3_), channel_id=1, source_target_pairs={{0,64},{64,128},{128,192},{192,256},{256,320},{320,384},{384,448},... | collective-permute-start | bytes 786440 | tf_op jit(solution)/shard_map/ppermute | solution.py:325
  55.7 5.6 %collective-permute-start.6 = (bf16[4,256,128]{2,1,0:T(8,128)(2,1)S(1)}, bf16[4,256,128]{2,1,0:T(8,128)(2,1)S(1)}, u32[]{:S(2)}, u32[]{:S(2)}) collective-permute-start(bf16[4,256,128]{2,1,0:T(8,128)(2,1)S(1)} %collective-permute-done.5.refs_1_.refs_6_), channel_id=1, source_target_pairs={{0,448},{64,0},{128,64},{192,128},{256,192},{320,256},{384,320},{4... | collective-permute-start | bytes 786440 | tf_op jit(solution)/shard_map/ppermute | solution.py:328
  62.0 2.6 %shard_map.76.value_ref = bf16[128,512]{1,0:T(8,128)(2,1)S(1)} custom-call(s32[2,2]{1,0:T(2,128)S(1)} %broadcast_and_fusion.table_ref, bf16[128,512]{1,0:T(8,128)(2,1)S(1)} %copy-done.6, bf16[2,128,512]{2,1,0:T(8,128)(2,1)S(1)} %copy-done, bf16[4,4,3,32,512]{4,3,2,1,0:T(8,128)(2,1)S(1)} %bitcast.8, ...), custom_call_target="tpu_custom_call" | custom-call | tf_op jit(solution)/shard_map/pallas_call | solution.py:75
  65.1 1.1 shard_map.77.refs_8_
  66.2 4.6 %all-to-all-start.2 = ((bf16[8,128,512]{2,1,0:T(8,128)(2,1)}), bf16[8,128,512]{2,1,0:T(8,128)(2,1)S(1)}, u32[]{:S(2)}, u32[]{:S(2)}) async-start(bf16[8,128,512]{2,1,0:T(8,128)(2,1)} %shard_map.77.refs_8_), calls=%async_computation.2 | async-start | bytes 2097152 | tf_op jit(solution)/shard_map/all_to_all | solution.py:313
  70.8 1.4 %shard_map.78 = (bf16[4,4,256,128]{3,2,1,0:T(8,128)(2,1)}, bf16[4,4,256,128]{3,2,1,0:T(8,128)(2,1)}) custom-call(bf16[4,256,128]{2,1,0:T(8,128)(2,1)S(1)} %shard_map.75.refs_0_, bf16[4,256,128]{2,1,0:T(8,128)(2,1)S(1)} %collective-permute-done.refs_1_, bf16[4,256,128]{2,1,0:T(8,128)(2,1)S(1)} %collective-permute-done.3.refs_2_, ...), custom_call_target="tpu_custom_call" | custom-call | tf_op jit(solution)/shard_map/pallas_call | solution.py:212
  72.3 1.9 %collective-permute-start.7 = (bf16[4,4,256,128]{3,2,1,0:T(8,128)(2,1)}, bf16[4,4,256,128]{3,2,1,0:T(8,128)(2,1)S(1)}, u32[]{:S(2)}, u32[]{:S(2)}) collective-permute-start(bf16[4,4,256,128]{3,2,1,0:T(8,128)(2,1)} %get-tuple-element.7.refs_0_), channel_id=1, source_target_pairs={{0,16},{16,0},{1,17},{17,1},{2,18},{18,2},{3,19},{19,3},{4,20},{20... | collective-permute-start | bytes 3145736 | tf_op jit(solution)/shard_map/ppermute | solution.py:350
  74.2 2.4 %collective-permute-start.8 = (bf16[4,4,256,128]{3,2,1,0:T(8,128)(2,1)}, bf16[4,4,256,128]{3,2,1,0:T(8,128)(2,1)S(1)}, u32[]{:S(2)}, u32[]{:S(2)}) collective-permute-start(bf16[4,4,256,128]{3,2,1,0:T(8,128)(2,1)} %get-tuple-element.8.refs_1_), channel_id=1, source_target_pairs={{0,16},{16,0},{1,17},{17,1},{2,18},{18,2},{3,19},{19,3},{4,20},{20... | collective-permute-start | bytes 3145736 | tf_op jit(solution)/shard_map/ppermute | solution.py:350
  77.0 2.1 %collective-permute-done.8.refs_3_ = bf16[4,4,256,128]{3,2,1,0:T(8,128)(2,1)S(1)} collective-permute-done((bf16[4,4,256,128]{3,2,1,0:T(8,128)(2,1)}, bf16[4,4,256,128]{3,2,1,0:T(8,128)(2,1)S(1)}, u32[]{:S(2)}, u32[]{:S(2)}) %collective-permute-start.8) | collective-permute-done | bytes 1048608 | tf_op jit(solution)/shard_map/ppermute | solution.py:350
  79.1 3.3 %all-to-all-done.2 = bf16[8,128,512]{2,1,0:T(8,128)(2,1)S(1)} async-done(((bf16[8,128,512]{2,1,0:T(8,128)(2,1)}), bf16[8,128,512]{2,1,0:T(8,128)(2,1)S(1)}, u32[]{:S(2)}, u32[]{:S(2)}) %all-to-all-start.2) | async-done | bytes 1048608 | tf_op jit(solution)/shard_map/all_to_all | solution.py:313
  82.4 4.0 %shard_map.79 = bf16[4,2,4,64,128]{4,3,2,1,0:T(8,128)(2,1)} custom-call(s32[1]{0:T(128)} %bitcast.1.plane_ref, bf16[4,2,128,512]{3,2,1,0:T(8,128)(2,1)S(1)} %bitcast.9, bf16[4,4,256,128]{3,2,1,0:T(8,128)(2,1)} %get-tuple-element.7.refs_0_, bf16[4,4,256,128]{3,2,1,0:T(8,128)(2,1)} %get-tuple-element.8.refs_1_, ...), custom_call_target="tpu_custom_call" | custom-call | tf_op jit(solution)/shard_map/pallas_call | solution.py:265
  86.4 8.1 %all-to-all-start.3 = ((bf16[32,64,128]{2,1,0:T(8,128)(2,1)}), bf16[32,64,128]{2,1,0:T(8,128)(2,1)S(1)}, u32[]{:S(2)}, u32[]{:S(2)}) async-start(bf16[32,64,128]{2,1,0:T(8,128)(2,1)} %bitcast.6), calls=%async_computation.3 | async-start | bytes 1048576 | tf_op jit(solution)/shard_map/all_to_all | solution.py:313
  94.4 16.7 %all-to-all-done.3 = bf16[32,64,128]{2,1,0:T(8,128)(2,1)S(1)} async-done(((bf16[32,64,128]{2,1,0:T(8,128)(2,1)}), bf16[32,64,128]{2,1,0:T(8,128)(2,1)S(1)}, u32[]{:S(2)}, u32[]{:S(2)}) %all-to-all-start.3) | async-done | bytes 524320 | tf_op jit(solution)/shard_map/all_to_all | solution.py:313
  (27 shorter events, 6.5 us)
Async XLA Ops:
  0.0 0.9 copy-start.5
  1.9 12.6 %all-to-all-start.1 = ((bf16[8,128,128]{2,1,0:T(8,128)(2,1)}), bf16[8,128,128]{2,1,0:T(8,128)(2,1)S(1)}, u32[]{:S(2)}, u32[]{:S(2)}) async-start(bf16[8,128,128]{2,1,0:T(8,128)(2,1)} %shard_map.74), calls=%async_computation.1 | async-start | bytes 524288 | tf_op jit(solution)/shard_map/all_to_all | solution.py:313
  14.5 46.7 %copy-start.7 = (s32[2,2]{1,0:T(2,128)S(1)}, s32[2,2]{1,0:T(2,128)}, u32[]{:S(2)}) copy-start(s32[2,2]{1,0:T(2,128)} %param.12) | copy-start | bytes 52
  14.5 47.4 %copy-start = (bf16[2,128,512]{2,1,0:T(8,128)(2,1)S(1)}, bf16[2,128,512]{2,1,0:T(8,128)(2,1)}, u32[]{:S(2)}) copy-start(bf16[2,128,512]{2,1,0:T(8,128)(2,1)} %memory_ref.1) | copy-start | bytes 786436
  14.5 47.4 %copy-start.6 = (bf16[128,512]{1,0:T(8,128)(2,1)S(1)}, bf16[128,512]{1,0:T(8,128)(2,1)}, u32[]{:S(2)}) copy-start(bf16[128,512]{1,0:T(8,128)(2,1)} %query_ref.3) | copy-start | bytes 393220
  14.5 47.4 %all-to-all-start = ((bf16[16,3,32,512]{3,2,1,0:T(8,128)(2,1)}), bf16[16,3,32,512]{3,2,1,0:T(8,128)(2,1)S(1)}, u32[]{:S(2)}, u32[]{:S(2)}) async-start(bf16[16,3,32,512]{3,2,1,0:T(8,128)(2,1)} %bitcast.12), calls=%async_computation | async-start | bytes 3145728 | tf_op jit(solution)/shard_map/all_to_all | solution.py:313
  22.1 14.7 %collective-permute-start.3 = (bf16[4,256,128]{2,1,0:T(8,128)(2,1)S(1)}, bf16[4,256,128]{2,1,0:T(8,128)(2,1)S(1)}, u32[]{:S(2)}, u32[]{:S(2)}) collective-permute-start(bf16[4,256,128]{2,1,0:T(8,128)(2,1)S(1)} %shard_map.75.refs_0_), channel_id=1, source_target_pairs={{0,448},{64,0},{128,64},{192,128},{256,192},{320,256},{384,320},{4... | collective-permute-start | bytes 786440 | tf_op jit(solution)/shard_map/ppermute | solution.py:326
  32.9 9.5 %collective-permute-start = (bf16[4,256,128]{2,1,0:T(8,128)(2,1)S(1)}, bf16[4,256,128]{2,1,0:T(8,128)(2,1)S(1)}, u32[]{:S(2)}, u32[]{:S(2)}) collective-permute-start(bf16[4,256,128]{2,1,0:T(8,128)(2,1)S(1)} %shard_map.75.refs_0_), channel_id=1, source_target_pairs={{0,64},{64,128},{128,192},{192,256},{256,320},{320,384},{384,448},... | collective-permute-start | bytes 786440 | tf_op jit(solution)/shard_map/ppermute | solution.py:325
  36.7 9.5 %collective-permute-start.4 = (bf16[4,256,128]{2,1,0:T(8,128)(2,1)S(1)}, bf16[4,256,128]{2,1,0:T(8,128)(2,1)S(1)}, u32[]{:S(2)}, u32[]{:S(2)}) collective-permute-start(bf16[4,256,128]{2,1,0:T(8,128)(2,1)S(1)} %collective-permute-done.3.refs_2_), channel_id=1, source_target_pairs={{0,448},{64,0},{128,64},{192,128},{256,192},{320,256},{384,320},{4... | collective-permute-start | bytes 786440 | tf_op jit(solution)/shard_map/ppermute | solution.py:326
  42.3 10.2 %collective-permute-start.1 = (bf16[4,256,128]{2,1,0:T(8,128)(2,1)S(1)}, bf16[4,256,128]{2,1,0:T(8,128)(2,1)S(1)}, u32[]{:S(2)}, u32[]{:S(2)}) collective-permute-start(bf16[4,256,128]{2,1,0:T(8,128)(2,1)S(1)} %collective-permute-done.refs_1_), channel_id=1, source_target_pairs={{0,64},{64,128},{128,192},{192,256},{256,320},{320,384},{384,448},... | collective-permute-start | bytes 786440 | tf_op jit(solution)/shard_map/ppermute | solution.py:325
  46.2 9.5 %collective-permute-start.5 = (bf16[4,256,128]{2,1,0:T(8,128)(2,1)S(1)}, bf16[4,256,128]{2,1,0:T(8,128)(2,1)S(1)}, u32[]{:S(2)}, u32[]{:S(2)}) collective-permute-start(bf16[4,256,128]{2,1,0:T(8,128)(2,1)S(1)} %collective-permute-done.4.refs_4_), channel_id=1, source_target_pairs={{0,448},{64,0},{128,64},{192,128},{256,192},{320,256},{384,320},{4... | collective-permute-start | bytes 786440 | tf_op jit(solution)/shard_map/ppermute | solution.py:326
  51.8 0.7 copy-start.1
  52.5 9.5 %collective-permute-start.2 = (bf16[4,256,128]{2,1,0:T(8,128)(2,1)S(1)}, bf16[4,256,128]{2,1,0:T(8,128)(2,1)S(1)}, u32[]{:S(2)}, u32[]{:S(2)}) collective-permute-start(bf16[4,256,128]{2,1,0:T(8,128)(2,1)S(1)} %collective-permute-done.1.refs_3_), channel_id=1, source_target_pairs={{0,64},{64,128},{128,192},{192,256},{256,320},{320,384},{384,448},... | collective-permute-start | bytes 786440 | tf_op jit(solution)/shard_map/ppermute | solution.py:325
  54.4 0.7 copy-start.3
  55.7 9.5 %collective-permute-start.6 = (bf16[4,256,128]{2,1,0:T(8,128)(2,1)S(1)}, bf16[4,256,128]{2,1,0:T(8,128)(2,1)S(1)}, u32[]{:S(2)}, u32[]{:S(2)}) collective-permute-start(bf16[4,256,128]{2,1,0:T(8,128)(2,1)S(1)} %collective-permute-done.5.refs_1_.refs_6_), channel_id=1, source_target_pairs={{0,448},{64,0},{128,64},{192,128},{256,192},{320,256},{384,320},{4... | collective-permute-start | bytes 786440 | tf_op jit(solution)/shard_map/ppermute | solution.py:328
  64.6 6.3 %copy-start.2 = (bf16[4,256,128]{2,1,0:T(8,128)(2,1)S(1)}, bf16[4,256,128]{2,1,0:T(8,128)(2,1)}, u32[]{:S(2)}) copy-start(bf16[4,256,128]{2,1,0:T(8,128)(2,1)} %copy-done.1) | copy-start | bytes 786436
  64.6 6.2 %copy-start.4 = (bf16[4,256,128]{2,1,0:T(8,128)(2,1)S(1)}, bf16[4,256,128]{2,1,0:T(8,128)(2,1)}, u32[]{:S(2)}) copy-start(bf16[4,256,128]{2,1,0:T(8,128)(2,1)} %copy-done.3) | copy-start | bytes 786436
  66.2 16.1 %all-to-all-start.2 = ((bf16[8,128,512]{2,1,0:T(8,128)(2,1)}), bf16[8,128,512]{2,1,0:T(8,128)(2,1)S(1)}, u32[]{:S(2)}, u32[]{:S(2)}) async-start(bf16[8,128,512]{2,1,0:T(8,128)(2,1)} %shard_map.77.refs_8_), calls=%async_computation.2 | async-start | bytes 2097152 | tf_op jit(solution)/shard_map/all_to_all | solution.py:313
  72.3 4.8 %collective-permute-start.7 = (bf16[4,4,256,128]{3,2,1,0:T(8,128)(2,1)}, bf16[4,4,256,128]{3,2,1,0:T(8,128)(2,1)S(1)}, u32[]{:S(2)}, u32[]{:S(2)}) collective-permute-start(bf16[4,4,256,128]{3,2,1,0:T(8,128)(2,1)} %get-tuple-element.7.refs_0_), channel_id=1, source_target_pairs={{0,16},{16,0},{1,17},{17,1},{2,18},{18,2},{3,19},{19,3},{4,20},{20... | collective-permute-start | bytes 3145736 | tf_op jit(solution)/shard_map/ppermute | solution.py:350
  74.2 4.9 %collective-permute-start.8 = (bf16[4,4,256,128]{3,2,1,0:T(8,128)(2,1)}, bf16[4,4,256,128]{3,2,1,0:T(8,128)(2,1)S(1)}, u32[]{:S(2)}, u32[]{:S(2)}) collective-permute-start(bf16[4,4,256,128]{3,2,1,0:T(8,128)(2,1)} %get-tuple-element.8.refs_1_), channel_id=1, source_target_pairs={{0,16},{16,0},{1,17},{17,1},{2,18},{18,2},{3,19},{19,3},{4,20},{20... | collective-permute-start | bytes 3145736 | tf_op jit(solution)/shard_map/ppermute | solution.py:350
  86.4 24.8 %all-to-all-start.3 = ((bf16[32,64,128]{2,1,0:T(8,128)(2,1)}), bf16[32,64,128]{2,1,0:T(8,128)(2,1)S(1)}, u32[]{:S(2)}, u32[]{:S(2)}) async-start(bf16[32,64,128]{2,1,0:T(8,128)(2,1)} %bitcast.6), calls=%async_computation.3 | async-start | bytes 1048576 | tf_op jit(solution)/shard_map/all_to_all | solution.py:313

commit v8 on v7

--- a/solution.py
+++ b/solution.py
@@ -21,7 +21,7 @@
 def softmax_rows(scores):
     row_top = jnp.max(scores, axis=-1, keepdims=True)
     expo = jnp.exp(scores - row_top)
-    return (expo / jnp.sum(expo, axis=-1, keepdims=True)).astype(jnp.bfloat16)
+    return (expo * (1.0 / jnp.sum(expo, axis=-1, keepdims=True))).astype(jnp.bfloat16)
 
 
 def rows_times_rows(left, right):
@@ -34,34 +34,43 @@
     out_ref = refs[-1]
     stretches, per_stretch = table_ref.shape
     heads = query_ref.shape[1] // HD
-    for u in range(stretches):
-        rows = slice(u * STRETCH, (u + 1) * STRETCH)
-        places = [table_ref[u, j] for j in range(per_stretch)]
-        for h in range(heads):
-            cols = slice(h * HD, (h + 1) * HD)
-            nbr_query, nbr_key, nbr_value = (
-                jnp.concatenate(
-                    [
-                        nbr_ref[x, place, kind, :, cols]
-                        for place in places
-                        for x in range(nbr_ref.shape[0])
-                    ],
-                    axis=0,
-                )
-                for kind in range(3)
-            )
-            enc_probs = softmax_rows(
-                rows_times_rows(nbr_query, memory_ref[0, rows, cols]) * SCALE
-            )
-            encoded = nbr_value.astype(jnp.float32) + jnp.dot(
-                enc_probs, memory_ref[1, rows, cols], preferred_element_type=jnp.float32
-            )
-            encoded = encoded.astype(jnp.bfloat16)
-            dec_probs = softmax_rows(
-                rows_times_rows(query_ref[rows, cols], nbr_key) * SCALE
-            )
-            context = jnp.dot(dec_probs, encoded, preferred_element_type=jnp.float32)
-            out_ref[rows, cols] = context.astype(jnp.bfloat16)
+    parts = [
+        (u, slice(u * STRETCH, (u + 1) * STRETCH), slice(h * HD, (h + 1) * HD))
+        for u in range(stretches)
+        for h in range(heads)
+    ]
+    places = [[table_ref[u, j] for j in range(per_stretch)] for u in range(stretches)]
+
+    def gathered(kind, u, cols):
+        return jnp.concatenate(
+            [
+                nbr_ref[x, place, kind, :, cols]
+                for place in places[u]
+                for x in range(nbr_ref.shape[0])
+            ],
+            axis=0,
+        )
+
+    enc_scores = [
+        rows_times_rows(gathered(0, u, cols), memory_ref[0, rows, cols]) * SCALE
+        for u, rows, cols in parts
+    ]
+    dec_scores = [
+        rows_times_rows(query_ref[rows, cols], gathered(1, u, cols)) * SCALE
+        for u, rows, cols in parts
+    ]
+    enc_probs = [softmax_rows(scores) for scores in enc_scores]
+    dec_probs = [softmax_rows(scores) for scores in dec_scores]
+    encoded = [
+        (
+            gathered(2, u, cols).astype(jnp.float32)
+            + jnp.dot(probs, memory_ref[1, rows, cols], preferred_element_type=jnp.float32)
+        ).astype(jnp.bfloat16)
+        for probs, (u, rows, cols) in zip(enc_probs, parts)
+    ]
+    for probs, values, (_, rows, cols) in zip(dec_probs, encoded, parts):
+        context = jnp.dot(probs, values, preferred_element_type=jnp.float32)
+        out_ref[rows, cols] = context.astype(jnp.bfloat16)
 
 
 VMEM = pl.BlockSpec(memory_space=pltpu.VMEM)
@@ -238,25 +247,28 @@
         lower = jnp.concatenate([own[:, middle:], sib[:, middle:]], axis=1)
         return jnp.concatenate([upper, lower], axis=0)
 
+    totals = []
     for pair in range(planes // 2):
         total = None
         for x in range(quarters):
             right = jnp.concatenate([rows_of(2 * pair, x), rows_of(2 * pair + 1, x)], axis=1)
             term = jnp.dot(left[x], right, preferred_element_type=jnp.float32)
             total = term if total is None else total + term
-        total = total.astype(jnp.bfloat16)
+        totals.append(total.astype(jnp.bfloat16))
+    for index in range(planes):
+        total = totals[index // 2]
+        first = index % 2 * width
+        target = lax.rem(plane + OFFSETS[index] + planes, planes)
         for s in range(sides):
             upper = total[s * tokens : s * tokens + half]
             lower = total[s * tokens + half : (s + 1) * tokens]
-            for i in range(2):
-                target = lax.rem(plane + OFFSETS[2 * pair + i] + planes, planes)
-                for piece in range(2):
-                    own = slice(i * width + piece * part, i * width + (piece + 1) * part)
-                    sib = slice(own.start + middle, own.stop + middle)
-                    x = 2 * lax.rem(target, 2) + piece
-                    out_ref[x, s, lax.div(target, 2)] = jnp.concatenate(
-                        [upper[:, own], upper[:, sib], lower[:, own], lower[:, sib]], axis=1
-                    )
+            for piece in range(2):
+                own = slice(first + piece * part, first + (piece + 1) * part)
+                sib = slice(own.start + middle, own.stop + middle)
+                x = 2 * lax.rem(target, 2) + piece
+                out_ref[x, s, lax.div(target, 2)] = jnp.concatenate(
+                    [upper[:, own], upper[:, sib], lower[:, own], lower[:, sib]], axis=1
+                )
 
 
 def project(plane, context, own, sib):

time: 113 us -> 113 us (level)
  transfers between devices with their start and end apart: 13 -> 13, of which waited for: 10 -> 10; matrix products, arithmetic and copies ran while one was open for 0% -> 0% of each run, Pallas kernels for 6% -> 5%
where the time goes in v8:
time: 113 us; the launch traced here: 112 us
  starting transfers between devices  63 us (56%)
  waiting for transfers between devices  33.9 us (30%)
  Pallas kernels  12.5 us (11%)
  local copies, waits for them, and re-layouts  2.36 us (2%)
    all_to_all x4, starting transfers between devices, exchange(): value = lax.all_to_all(value, axes, split_axis=0, concat_axis=0, tiled=True)  25.4 us
    all_to_all x4, waiting for transfers between devices, exchange(): value = lax.all_to_all(value, axes, split_axis=0, concat_axis=0, tiled=True)  25 us
    ppermute x3, starting transfers between devices, ring(): ahead = lax.ppermute(ahead, axis, down)  22 us
    ppermute x3, starting transfers between devices, ring(): behind = lax.ppermute(behind, axis, up)  5.75 us
    ppermute x1, starting transfers between devices, ring(): return blocks + [lax.ppermute(ahead, axis, down)]  5.59 us
    ppermute x3, waiting for transfers between devices, ring(): ahead = lax.ppermute(ahead, axis, down)  4.41 us
    ppermute x2, starting transfers between devices, local(): sib = [lax.ppermute(block, 'c', [(0, 1), (1, 0)]) for block in own]  4.31 us
    pallas_call x1, Pallas kernels, project(): pl.pallas_call(project_kernel, out_shape=jax.ShapeDtypeStruct((quarters,...  3.9 us
  transfers between devices with their start and end apart: 13, of which 10 were waited for; matrix products, arithmetic and copies ran while one was open for 0% of the time, Pallas kernels for 5%

profile of v8, /device:TPU:16, one launch (start us, length us, event | category | flops | bytes accessed | tf_op | source)
XLA Modules:
  0.0 111.9 jit_solution(9305183840680994058)
XLA Ops:
  1.9 5.3 %all-to-all-start.1 = ((bf16[8,128,128]{2,1,0:T(8,128)(2,1)}), bf16[8,128,128]{2,1,0:T(8,128)(2,1)S(1)}, u32[]{:S(2)}, u32[]{:S(2)}) async-start(bf16[8,128,128]{2,1,0:T(8,128)(2,1)} %shard_map.74), calls=%async_computation.1 | async-start | bytes 524288 | tf_op jit(solution)/shard_map/all_to_all | solution.py:325
  7.2 2.3 %shard_map.73 = bf16[4,4,3,32,512]{4,3,2,1,0:T(8,128)(2,1)} custom-call(bf16[32,8192]{1,0:T(8,128)(2,1)} %query_ref.2, bf16[32,8192]{1,0:T(8,128)(2,1)} %key_ref.1, bf16[32,8192]{1,0:T(8,128)(2,1)} %value_ref.1), custom_call_target="tpu_custom_call" | custom-call | tf_op jit(solution)/shard_map/pallas_call | solution.py:145
  9.6 4.9 %all-to-all-done.1 = bf16[8,128,128]{2,1,0:T(8,128)(2,1)S(1)} async-done(((bf16[8,128,128]{2,1,0:T(8,128)(2,1)}), bf16[8,128,128]{2,1,0:T(8,128)(2,1)S(1)}, u32[]{:S(2)}, u32[]{:S(2)}) %all-to-all-start.1) | async-done | bytes 262176 | tf_op jit(solution)/shard_map/all_to_all | solution.py:325
  14.5 7.4 %all-to-all-start = ((bf16[16,3,32,512]{3,2,1,0:T(8,128)(2,1)}), bf16[16,3,32,512]{3,2,1,0:T(8,128)(2,1)S(1)}, u32[]{:S(2)}, u32[]{:S(2)}) async-start(bf16[16,3,32,512]{3,2,1,0:T(8,128)(2,1)} %bitcast.12), calls=%async_computation | async-start | bytes 3145728 | tf_op jit(solution)/shard_map/all_to_all | solution.py:325
  22.1 10.8 %collective-permute-start.3 = (bf16[4,256,128]{2,1,0:T(8,128)(2,1)S(1)}, bf16[4,256,128]{2,1,0:T(8,128)(2,1)S(1)}, u32[]{:S(2)}, u32[]{:S(2)}) collective-permute-start(bf16[4,256,128]{2,1,0:T(8,128)(2,1)S(1)} %shard_map.75.refs_0_), channel_id=1, source_target_pairs={{0,448},{64,0},{128,64},{192,128},{256,192},{320,256},{384,320},{4... | collective-permute-start | bytes 786440 | tf_op jit(solution)/shard_map/ppermute | solution.py:338
  32.9 1.9 %collective-permute-start = (bf16[4,256,128]{2,1,0:T(8,128)(2,1)S(1)}, bf16[4,256,128]{2,1,0:T(8,128)(2,1)S(1)}, u32[]{:S(2)}, u32[]{:S(2)}) collective-permute-start(bf16[4,256,128]{2,1,0:T(8,128)(2,1)S(1)} %shard_map.75.refs_0_), channel_id=1, source_target_pairs={{0,64},{64,128},{128,192},{192,256},{256,320},{320,384},{384,448},... | collective-permute-start | bytes 786440 | tf_op jit(solution)/shard_map/ppermute | solution.py:337
  34.8 1.9 %collective-permute-done.3.refs_2_ = bf16[4,256,128]{2,1,0:T(8,128)(2,1)S(1)} collective-permute-done((bf16[4,256,128]{2,1,0:T(8,128)(2,1)S(1)}, bf16[4,256,128]{2,1,0:T(8,128)(2,1)S(1)}, u32[]{:S(2)}, u32[]{:S(2)}) %collective-permute-start.3) | collective-permute-done | bytes 262176 | tf_op jit(solution)/shard_map/ppermute | solution.py:338
  36.7 5.6 %collective-permute-start.4 = (bf16[4,256,128]{2,1,0:T(8,128)(2,1)S(1)}, bf16[4,256,128]{2,1,0:T(8,128)(2,1)S(1)}, u32[]{:S(2)}, u32[]{:S(2)}) collective-permute-start(bf16[4,256,128]{2,1,0:T(8,128)(2,1)S(1)} %collective-permute-done.3.refs_2_), channel_id=1, source_target_pairs={{0,448},{64,0},{128,64},{192,128},{256,192},{320,256},{384,320},{4... | collective-permute-start | bytes 786440 | tf_op jit(solution)/shard_map/ppermute | solution.py:338
  42.3 1.9 %collective-permute-start.1 = (bf16[4,256,128]{2,1,0:T(8,128)(2,1)S(1)}, bf16[4,256,128]{2,1,0:T(8,128)(2,1)S(1)}, u32[]{:S(2)}, u32[]{:S(2)}) collective-permute-start(bf16[4,256,128]{2,1,0:T(8,128)(2,1)S(1)} %collective-permute-done.refs_1_), channel_id=1, source_target_pairs={{0,64},{64,128},{128,192},{192,256},{256,320},{320,384},{384,448},... | collective-permute-start | bytes 786440 | tf_op jit(solution)/shard_map/ppermute | solution.py:337
  44.3 1.9 %collective-permute-done.4.refs_4_ = bf16[4,256,128]{2,1,0:T(8,128)(2,1)S(1)} collective-permute-done((bf16[4,256,128]{2,1,0:T(8,128)(2,1)S(1)}, bf16[4,256,128]{2,1,0:T(8,128)(2,1)S(1)}, u32[]{:S(2)}, u32[]{:S(2)}) %collective-permute-start.4) | collective-permute-done | bytes 262176 | tf_op jit(solution)/shard_map/ppermute | solution.py:338
  46.2 5.6 %collective-permute-start.5 = (bf16[4,256,128]{2,1,0:T(8,128)(2,1)S(1)}, bf16[4,256,128]{2,1,0:T(8,128)(2,1)S(1)}, u32[]{:S(2)}, u32[]{:S(2)}) collective-permute-start(bf16[4,256,128]{2,1,0:T(8,128)(2,1)S(1)} %collective-permute-done.4.refs_4_), channel_id=1, source_target_pairs={{0,448},{64,0},{128,64},{192,128},{256,192},{320,256},{384,320},{4... | collective-permute-start | bytes 786440 | tf_op jit(solution)/shard_map/ppermute | solution.py:338
  52.5 1.9 %collective-permute-start.2 = (bf16[4,256,128]{2,1,0:T(8,128)(2,1)S(1)}, bf16[4,256,128]{2,1,0:T(8,128)(2,1)S(1)}, u32[]{:S(2)}, u32[]{:S(2)}) collective-permute-start(bf16[4,256,128]{2,1,0:T(8,128)(2,1)S(1)} %collective-permute-done.1.refs_3_), channel_id=1, source_target_pairs={{0,64},{64,128},{128,192},{192,256},{256,320},{320,384},{384,448},... | collective-permute-start | bytes 786440 | tf_op jit(solution)/shard_map/ppermute | solution.py:337
  55.7 5.6 %collective-permute-start.6 = (bf16[4,256,128]{2,1,0:T(8,128)(2,1)S(1)}, bf16[4,256,128]{2,1,0:T(8,128)(2,1)S(1)}, u32[]{:S(2)}, u32[]{:S(2)}) collective-permute-start(bf16[4,256,128]{2,1,0:T(8,128)(2,1)S(1)} %collective-permute-done.5.refs_1_.refs_6_), channel_id=1, source_target_pairs={{0,448},{64,0},{128,64},{192,128},{256,192},{320,256},{384,320},{4... | collective-permute-start | bytes 786440 | tf_op jit(solution)/shard_map/ppermute | solution.py:340
  62.0 1.7 %shard_map.76.value_ref = bf16[128,512]{1,0:T(8,128)(2,1)S(1)} custom-call(s32[2,2]{1,0:T(2,128)S(1)} %broadcast_and_fusion.table_ref, bf16[128,512]{1,0:T(8,128)(2,1)S(1)} %copy-done.6, bf16[2,128,512]{2,1,0:T(8,128)(2,1)S(1)} %copy-done, bf16[4,4,3,32,512]{4,3,2,1,0:T(8,128)(2,1)S(1)} %bitcast.8, ...), custom_call_target="tpu_custom_call" | custom-call | tf_op jit(solution)/shard_map/pallas_call | solution.py:84
  63.7 1.4 %collective-permute-done.6.refs_0_.refs_7_ = bf16[4,256,128]{2,1,0:T(8,128)(2,1)S(1)} collective-permute-done((bf16[4,256,128]{2,1,0:T(8,128)(2,1)S(1)}, bf16[4,256,128]{2,1,0:T(8,128)(2,1)S(1)}, u32[]{:S(2)}, u32[]{:S(2)}) %collective-permute-start.6) | collective-permute-done | bytes 262176 | tf_op jit(solution)/shard_map/ppermute | solution.py:340
  66.2 4.6 %all-to-all-start.2 = ((bf16[8,128,512]{2,1,0:T(8,128)(2,1)}), bf16[8,128,512]{2,1,0:T(8,128)(2,1)S(1)}, u32[]{:S(2)}, u32[]{:S(2)}) async-start(bf16[8,128,512]{2,1,0:T(8,128)(2,1)} %shard_map.77.refs_8_), calls=%async_computation.2 | async-start | bytes 2097152 | tf_op jit(solution)/shard_map/all_to_all | solution.py:325
  70.8 1.4 %shard_map.78 = (bf16[4,4,256,128]{3,2,1,0:T(8,128)(2,1)}, bf16[4,4,256,128]{3,2,1,0:T(8,128)(2,1)}) custom-call(bf16[4,256,128]{2,1,0:T(8,128)(2,1)S(1)} %shard_map.75.refs_0_, bf16[4,256,128]{2,1,0:T(8,128)(2,1)S(1)} %collective-permute-done.refs_1_, bf16[4,256,128]{2,1,0:T(8,128)(2,1)S(1)} %collective-permute-done.3.refs_2_, ...), custom_call_target="tpu_custom_call" | custom-call | tf_op jit(solution)/shard_map/pallas_call | solution.py:221
  72.3 1.9 %collective-permute-start.7 = (bf16[4,4,256,128]{3,2,1,0:T(8,128)(2,1)}, bf16[4,4,256,128]{3,2,1,0:T(8,128)(2,1)S(1)}, u32[]{:S(2)}, u32[]{:S(2)}) collective-permute-start(bf16[4,4,256,128]{3,2,1,0:T(8,128)(2,1)} %get-tuple-element.7.refs_0_), channel_id=1, source_target_pairs={{0,16},{16,0},{1,17},{17,1},{2,18},{18,2},{3,19},{19,3},{4,20},{20... | collective-permute-start | bytes 3145736 | tf_op jit(solution)/shard_map/ppermute | solution.py:362
  74.2 2.4 %collective-permute-start.8 = (bf16[4,4,256,128]{3,2,1,0:T(8,128)(2,1)}, bf16[4,4,256,128]{3,2,1,0:T(8,128)(2,1)S(1)}, u32[]{:S(2)}, u32[]{:S(2)}) collective-permute-start(bf16[4,4,256,128]{3,2,1,0:T(8,128)(2,1)} %get-tuple-element.8.refs_1_), channel_id=1, source_target_pairs={{0,16},{16,0},{1,17},{17,1},{2,18},{18,2},{3,19},{19,3},{4,20},{20... | collective-permute-start | bytes 3145736 | tf_op jit(solution)/shard_map/ppermute | solution.py:362
  77.0 2.1 %collective-permute-done.8.refs_3_ = bf16[4,4,256,128]{3,2,1,0:T(8,128)(2,1)S(1)} collective-permute-done((bf16[4,4,256,128]{3,2,1,0:T(8,128)(2,1)}, bf16[4,4,256,128]{3,2,1,0:T(8,128)(2,1)S(1)}, u32[]{:S(2)}, u32[]{:S(2)}) %collective-permute-start.8) | collective-permute-done | bytes 1048608 | tf_op jit(solution)/shard_map/ppermute | solution.py:362
  79.1 3.3 %all-to-all-done.2 = bf16[8,128,512]{2,1,0:T(8,128)(2,1)S(1)} async-done(((bf16[8,128,512]{2,1,0:T(8,128)(2,1)}), bf16[8,128,512]{2,1,0:T(8,128)(2,1)S(1)}, u32[]{:S(2)}, u32[]{:S(2)}) %all-to-all-start.2) | async-done | bytes 1048608 | tf_op jit(solution)/shard_map/all_to_all | solution.py:325
  82.4 3.9 %shard_map.79 = bf16[4,2,4,64,128]{4,3,2,1,0:T(8,128)(2,1)} custom-call(s32[1]{0:T(128)} %bitcast.1.plane_ref, bf16[4,2,128,512]{3,2,1,0:T(8,128)(2,1)S(1)} %bitcast.9, bf16[4,4,256,128]{3,2,1,0:T(8,128)(2,1)} %get-tuple-element.7.refs_0_, bf16[4,4,256,128]{3,2,1,0:T(8,128)(2,1)} %get-tuple-element.8.refs_1_, ...), custom_call_target="tpu_custom_call" | custom-call | tf_op jit(solution)/shard_map/pallas_call | solution.py:277
  86.3 8.1 %all-to-all-start.3 = ((bf16[32,64,128]{2,1,0:T(8,128)(2,1)}), bf16[32,64,128]{2,1,0:T(8,128)(2,1)S(1)}, u32[]{:S(2)}, u32[]{:S(2)}) async-start(bf16[32,64,128]{2,1,0:T(8,128)(2,1)} %bitcast.6), calls=%async_computation.3 | async-start | bytes 1048576 | tf_op jit(solution)/shard_map/all_to_all | solution.py:325
  94.3 16.7 %all-to-all-done.3 = bf16[32,64,128]{2,1,0:T(8,128)(2,1)S(1)} async-done(((bf16[32,64,128]{2,1,0:T(8,128)(2,1)}), bf16[32,64,128]{2,1,0:T(8,128)(2,1)S(1)}, u32[]{:S(2)}, u32[]{:S(2)}) %all-to-all-start.3) | async-done | bytes 524320 | tf_op jit(solution)/shard_map/all_to_all | solution.py:325
  (27 shorter events, 7.0 us)
Async XLA Ops:
  0.0 0.9 copy-start.5
  1.9 12.6 %all-to-all-start.1 = ((bf16[8,128,128]{2,1,0:T(8,128)(2,1)}), bf16[8,128,128]{2,1,0:T(8,128)(2,1)S(1)}, u32[]{:S(2)}, u32[]{:S(2)}) async-start(bf16[8,128,128]{2,1,0:T(8,128)(2,1)} %shard_map.74), calls=%async_computation.1 | async-start | bytes 524288 | tf_op jit(solution)/shard_map/all_to_all | solution.py:325
  14.5 46.7 %copy-start.7 = (s32[2,2]{1,0:T(2,128)S(1)}, s32[2,2]{1,0:T(2,128)}, u32[]{:S(2)}) copy-start(s32[2,2]{1,0:T(2,128)} %param.12) | copy-start | bytes 52
  14.5 47.4 %copy-start = (bf16[2,128,512]{2,1,0:T(8,128)(2,1)S(1)}, bf16[2,128,512]{2,1,0:T(8,128)(2,1)}, u32[]{:S(2)}) copy-start(bf16[2,128,512]{2,1,0:T(8,128)(2,1)} %memory_ref.1) | copy-start | bytes 786436
  14.5 47.4 %copy-start.6 = (bf16[128,512]{1,0:T(8,128)(2,1)S(1)}, bf16[128,512]{1,0:T(8,128)(2,1)}, u32[]{:S(2)}) copy-start(bf16[128,512]{1,0:T(8,128)(2,1)} %query_ref.3) | copy-start | bytes 393220
  14.5 47.4 %all-to-all-start = ((bf16[16,3,32,512]{3,2,1,0:T(8,128)(2,1)}), bf16[16,3,32,512]{3,2,1,0:T(8,128)(2,1)S(1)}, u32[]{:S(2)}, u32[]{:S(2)}) async-start(bf16[16,3,32,512]{3,2,1,0:T(8,128)(2,1)} %bitcast.12), calls=%async_computation | async-start | bytes 3145728 | tf_op jit(solution)/shard_map/all_to_all | solution.py:325
  22.1 14.7 %collective-permute-start.3 = (bf16[4,256,128]{2,1,0:T(8,128)(2,1)S(1)}, bf16[4,256,128]{2,1,0:T(8,128)(2,1)S(1)}, u32[]{:S(2)}, u32[]{:S(2)}) collective-permute-start(bf16[4,256,128]{2,1,0:T(8,128)(2,1)S(1)} %shard_map.75.refs_0_), channel_id=1, source_target_pairs={{0,448},{64,0},{128,64},{192,128},{256,192},{320,256},{384,320},{4... | collective-permute-start | bytes 786440 | tf_op jit(solution)/shard_map/ppermute | solution.py:338
  32.9 9.5 %collective-permute-start = (bf16[4,256,128]{2,1,0:T(8,128)(2,1)S(1)}, bf16[4,256,128]{2,1,0:T(8,128)(2,1)S(1)}, u32[]{:S(2)}, u32[]{:S(2)}) collective-permute-start(bf16[4,256,128]{2,1,0:T(8,128)(2,1)S(1)} %shard_map.75.refs_0_), channel_id=1, source_target_pairs={{0,64},{64,128},{128,192},{192,256},{256,320},{320,384},{384,448},... | collective-permute-start | bytes 786440 | tf_op jit(solution)/shard_map/ppermute | solution.py:337
  36.7 9.5 %collective-permute-start.4 = (bf16[4,256,128]{2,1,0:T(8,128)(2,1)S(1)}, bf16[4,256,128]{2,1,0:T(8,128)(2,1)S(1)}, u32[]{:S(2)}, u32[]{:S(2)}) collective-permute-start(bf16[4,256,128]{2,1,0:T(8,128)(2,1)S(1)} %collective-permute-done.3.refs_2_), channel_id=1, source_target_pairs={{0,448},{64,0},{128,64},{192,128},{256,192},{320,256},{384,320},{4... | collective-permute-start | bytes 786440 | tf_op jit(solution)/shard_map/ppermute | solution.py:338
  42.3 10.2 %collective-permute-start.1 = (bf16[4,256,128]{2,1,0:T(8,128)(2,1)S(1)}, bf16[4,256,128]{2,1,0:T(8,128)(2,1)S(1)}, u32[]{:S(2)}, u32[]{:S(2)}) collective-permute-start(bf16[4,256,128]{2,1,0:T(8,128)(2,1)S(1)} %collective-permute-done.refs_1_), channel_id=1, source_target_pairs={{0,64},{64,128},{128,192},{192,256},{256,320},{320,384},{384,448},... | collective-permute-start | bytes 786440 | tf_op jit(solution)/shard_map/ppermute | solution.py:337
  46.2 9.5 %collective-permute-start.5 = (bf16[4,256,128]{2,1,0:T(8,128)(2,1)S(1)}, bf16[4,256,128]{2,1,0:T(8,128)(2,1)S(1)}, u32[]{:S(2)}, u32[]{:S(2)}) collective-permute-start(bf16[4,256,128]{2,1,0:T(8,128)(2,1)S(1)} %collective-permute-done.4.refs_4_), channel_id=1, source_target_pairs={{0,448},{64,0},{128,64},{192,128},{256,192},{320,256},{384,320},{4... | collective-permute-start | bytes 786440 | tf_op jit(solution)/shard_map/ppermute | solution.py:338
  51.8 0.7 copy-start.1
  52.5 9.5 %collective-permute-start.2 = (bf16[4,256,128]{2,1,0:T(8,128)(2,1)S(1)}, bf16[4,256,128]{2,1,0:T(8,128)(2,1)S(1)}, u32[]{:S(2)}, u32[]{:S(2)}) collective-permute-start(bf16[4,256,128]{2,1,0:T(8,128)(2,1)S(1)} %collective-permute-done.1.refs_3_), channel_id=1, source_target_pairs={{0,64},{64,128},{128,192},{192,256},{256,320},{320,384},{384,448},... | collective-permute-start | bytes 786440 | tf_op jit(solution)/shard_map/ppermute | solution.py:337
  54.4 0.7 copy-start.3
  55.7 9.5 %collective-permute-start.6 = (bf16[4,256,128]{2,1,0:T(8,128)(2,1)S(1)}, bf16[4,256,128]{2,1,0:T(8,128)(2,1)S(1)}, u32[]{:S(2)}, u32[]{:S(2)}) collective-permute-start(bf16[4,256,128]{2,1,0:T(8,128)(2,1)S(1)} %collective-permute-done.5.refs_1_.refs_6_), channel_id=1, source_target_pairs={{0,448},{64,0},{128,64},{192,128},{256,192},{320,256},{384,320},{4... | collective-permute-start | bytes 786440 | tf_op jit(solution)/shard_map/ppermute | solution.py:340
  63.7 7.1 %copy-start.2 = (bf16[4,256,128]{2,1,0:T(8,128)(2,1)S(1)}, bf16[4,256,128]{2,1,0:T(8,128)(2,1)}, u32[]{:S(2)}) copy-start(bf16[4,256,128]{2,1,0:T(8,128)(2,1)} %copy-done.1) | copy-start | bytes 786436
  63.7 7.1 %copy-start.4 = (bf16[4,256,128]{2,1,0:T(8,128)(2,1)S(1)}, bf16[4,256,128]{2,1,0:T(8,128)(2,1)}, u32[]{:S(2)}) copy-start(bf16[4,256,128]{2,1,0:T(8,128)(2,1)} %copy-done.3) | copy-start | bytes 786436
  66.2 16.1 %all-to-all-start.2 = ((bf16[8,128,512]{2,1,0:T(8,128)(2,1)}), bf16[8,128,512]{2,1,0:T(8,128)(2,1)S(1)}, u32[]{:S(2)}, u32[]{:S(2)}) async-start(bf16[8,128,512]{2,1,0:T(8,128)(2,1)} %shard_map.77.refs_8_), calls=%async_computation.2 | async-start | bytes 2097152 | tf_op jit(solution)/shard_map/all_to_all | solution.py:325
  72.3 4.8 %collective-permute-start.7 = (bf16[4,4,256,128]{3,2,1,0:T(8,128)(2,1)}, bf16[4,4,256,128]{3,2,1,0:T(8,128)(2,1)S(1)}, u32[]{:S(2)}, u32[]{:S(2)}) collective-permute-start(bf16[4,4,256,128]{3,2,1,0:T(8,128)(2,1)} %get-tuple-element.7.refs_0_), channel_id=1, source_target_pairs={{0,16},{16,0},{1,17},{17,1},{2,18},{18,2},{3,19},{19,3},{4,20},{20... | collective-permute-start | bytes 3145736 | tf_op jit(solution)/shard_map/ppermute | solution.py:362
  74.2 4.9 %collective-permute-start.8 = (bf16[4,4,256,128]{3,2,1,0:T(8,128)(2,1)}, bf16[4,4,256,128]{3,2,1,0:T(8,128)(2,1)S(1)}, u32[]{:S(2)}, u32[]{:S(2)}) collective-permute-start(bf16[4,4,256,128]{3,2,1,0:T(8,128)(2,1)} %get-tuple-element.8.refs_1_), channel_id=1, source_target_pairs={{0,16},{16,0},{1,17},{17,1},{2,18},{18,2},{3,19},{19,3},{4,20},{20... | collective-permute-start | bytes 3145736 | tf_op jit(solution)/shard_map/ppermute | solution.py:362
  86.3 24.8 %all-to-all-start.3 = ((bf16[32,64,128]{2,1,0:T(8,128)(2,1)}), bf16[32,64,128]{2,1,0:T(8,128)(2,1)S(1)}, u32[]{:S(2)}, u32[]{:S(2)}) async-start(bf16[32,64,128]{2,1,0:T(8,128)(2,1)} %bitcast.6), calls=%async_computation.3 | async-start | bytes 1048576 | tf_op jit(solution)/shard_map/all_to_all | solution.py:325

commit v9 on v8

--- a/solution.py
+++ b/solution.py
@@ -227,7 +227,7 @@
     )(*blocks, after)
 
 
-def project_kernel(plane_ref, context_ref, *refs):
+def project_kernel(plane_ref, _, context_ref, *refs):
     out_ref = refs[-1]
     stacks = len(refs) // 2
     plane = plane_ref[0]
@@ -271,7 +271,7 @@
                 )
 
 
-def project(plane, context, own, sib):
+def project(plane, core, context, own, sib):
     quarters, sides, tokens, _ = context.shape
     highs = 2 * TOGETHER * len(own) // quarters
     return pl.pallas_call(
@@ -279,10 +279,10 @@
         out_shape=jax.ShapeDtypeStruct(
             (quarters, sides, highs, tokens // 2, own[0].shape[-1]), jnp.bfloat16
         ),
-        in_specs=[pl.BlockSpec(memory_space=pltpu.SMEM)] + [VMEM] * (1 + len(own) + len(sib)),
-        out_specs=VMEM,
-        compiler_params=PARAMS,
-    )(plane, context, *own, *sib)
+        in_specs=[pl.BlockSpec(memory_space=pltpu.SMEM)] * 2 + [VMEM] * (1 + len(own) + len(sib)),
+        out_specs=VMEM,
+        compiler_params=PARAMS,
+    )(plane, core, context, *own, *sib)
 
 
 def add_kernel(core_ref, partial_ref, out_ref):
@@ -362,8 +362,8 @@
     sib = [lax.ppermute(block, "c", [(0, 1), (1, 0)]) for block in own]
     context = exchange(context.reshape(4, 2, *context.shape[1:]), ("x", "yl"))
     plane = lax.axis_index("z").astype(jnp.int32).reshape(1)
-    partial = exchange(project(plane, context, own, sib), ("x", "yl", "yh"))
     core = lax.axis_index("c").astype(jnp.int32).reshape(1)
+    partial = exchange(project(plane, core, context, own, sib), ("x", "yl", "yh"))
     return add(core, partial)
 
 

time: 113 us -> 112 us (level)
  blocking collectives: 0 us -> 24.6 us
  waiting for transfers between devices: 33.9 us -> 17.2 us
  starting transfers between devices: 63 us -> 54.9 us
    all_to_all x0 -> x1, blocking collectives: none -> 24.6 us  [exchange(): value = lax.all_to_all(value, axes, split_axis=0, concat_axis=0, tiled=True)]
    all_to_all x4 -> x3, waiting for transfers between devices: 25 us -> 8.23 us  [exchange(): value = lax.all_to_all(value, axes, split_axis=0, concat_axis=0, tiled=True)]
    all_to_all x4 -> x3, starting transfers between devices: 25.4 us -> 17.3 us  [exchange(): value = lax.all_to_all(value, axes, split_axis=0, concat_axis=0, tiled=True)]
  transfers between devices with their start and end apart: 13 -> 12, of which waited for: 10 -> 9; matrix products, arithmetic and copies ran while one was open for 0% -> 0% of each run, Pallas kernels for 5% -> 5%
where the time goes in v9:
time: 112 us; the launch traced here: 111 us
  starting transfers between devices  54.9 us (49%)
  blocking collectives  24.6 us (22%)
  waiting for transfers between devices  17.2 us (15%)
  Pallas kernels  11.6 us (10%)
  local copies, waits for them, and re-layouts  2.35 us (2%)
    all_to_all x1, blocking collectives, exchange(): value = lax.all_to_all(value, axes, split_axis=0, concat_axis=0, tiled=True)  24.6 us
    ppermute x3, starting transfers between devices, ring(): ahead = lax.ppermute(ahead, axis, down)  22 us
    all_to_all x3, starting transfers between devices, exchange(): value = lax.all_to_all(value, axes, split_axis=0, concat_axis=0, tiled=True)  17.3 us
    all_to_all x3, waiting for transfers between devices, exchange(): value = lax.all_to_all(value, axes, split_axis=0, concat_axis=0, tiled=True)  8.23 us
    ppermute x3, starting transfers between devices, ring(): behind = lax.ppermute(behind, axis, up)  5.75 us
    ppermute x1, starting transfers between devices, ring(): return blocks + [lax.ppermute(ahead, axis, down)]  5.59 us
    ppermute x3, waiting for transfers between devices, ring(): ahead = lax.ppermute(ahead, axis, down)  4.42 us
    ppermute x2, starting transfers between devices, local(): sib = [lax.ppermute(block, 'c', [(0, 1), (1, 0)]) for block in own]  4.31 us
  transfers between devices with their start and end apart: 12, of which 9 were waited for; matrix products, arithmetic and copies ran while one was open for 0% of the time, Pallas kernels for 5%

profile of v9, /device:TPU:16, one launch (start us, length us, event | category | flops | bytes accessed | tf_op | source)
XLA Modules:
  0.0 110.9 jit_solution(3797205557590479721)
XLA Ops:
  1.9 5.3 %all-to-all-start.1 = ((bf16[8,128,128]{2,1,0:T(8,128)(2,1)}), bf16[8,128,128]{2,1,0:T(8,128)(2,1)S(1)}, u32[]{:S(2)}, u32[]{:S(2)}) async-start(bf16[8,128,128]{2,1,0:T(8,128)(2,1)} %shard_map.74), calls=%async_computation.1 | async-start | bytes 524288 | tf_op jit(solution)/shard_map/all_to_all | solution.py:325
  7.2 2.3 %shard_map.73 = bf16[4,4,3,32,512]{4,3,2,1,0:T(8,128)(2,1)} custom-call(bf16[32,8192]{1,0:T(8,128)(2,1)} %query_ref.2, bf16[32,8192]{1,0:T(8,128)(2,1)} %key_ref.1, bf16[32,8192]{1,0:T(8,128)(2,1)} %value_ref.1), custom_call_target="tpu_custom_call" | custom-call | tf_op jit(solution)/shard_map/pallas_call | solution.py:145
  9.6 4.9 %all-to-all-done.1 = bf16[8,128,128]{2,1,0:T(8,128)(2,1)S(1)} async-done(((bf16[8,128,128]{2,1,0:T(8,128)(2,1)}), bf16[8,128,128]{2,1,0:T(8,128)(2,1)S(1)}, u32[]{:S(2)}, u32[]{:S(2)}) %all-to-all-start.1) | async-done | bytes 262176 | tf_op jit(solution)/shard_map/all_to_all | solution.py:325
  14.5 7.4 %all-to-all-start = ((bf16[16,3,32,512]{3,2,1,0:T(8,128)(2,1)}), bf16[16,3,32,512]{3,2,1,0:T(8,128)(2,1)S(1)}, u32[]{:S(2)}, u32[]{:S(2)}) async-start(bf16[16,3,32,512]{3,2,1,0:T(8,128)(2,1)} %bitcast.13), calls=%async_computation | async-start | bytes 3145728 | tf_op jit(solution)/shard_map/all_to_all | solution.py:325
  22.0 10.8 %collective-permute-start.3 = (bf16[4,256,128]{2,1,0:T(8,128)(2,1)S(1)}, bf16[4,256,128]{2,1,0:T(8,128)(2,1)S(1)}, u32[]{:S(2)}, u32[]{:S(2)}) collective-permute-start(bf16[4,256,128]{2,1,0:T(8,128)(2,1)S(1)} %shard_map.75.refs_0_), channel_id=1, source_target_pairs={{0,448},{64,0},{128,64},{192,128},{256,192},{320,256},{384,320},{4... | collective-permute-start | bytes 786440 | tf_op jit(solution)/shard_map/ppermute | solution.py:338
  32.8 1.9 %collective-permute-start = (bf16[4,256,128]{2,1,0:T(8,128)(2,1)S(1)}, bf16[4,256,128]{2,1,0:T(8,128)(2,1)S(1)}, u32[]{:S(2)}, u32[]{:S(2)}) collective-permute-start(bf16[4,256,128]{2,1,0:T(8,128)(2,1)S(1)} %shard_map.75.refs_0_), channel_id=1, source_target_pairs={{0,64},{64,128},{128,192},{192,256},{256,320},{320,384},{384,448},... | collective-permute-start | bytes 786440 | tf_op jit(solution)/shard_map/ppermute | solution.py:337
  34.8 1.9 %collective-permute-done.3.refs_2_ = bf16[4,256,128]{2,1,0:T(8,128)(2,1)S(1)} collective-permute-done((bf16[4,256,128]{2,1,0:T(8,128)(2,1)S(1)}, bf16[4,256,128]{2,1,0:T(8,128)(2,1)S(1)}, u32[]{:S(2)}, u32[]{:S(2)}) %collective-permute-start.3) | collective-permute-done | bytes 262176 | tf_op jit(solution)/shard_map/ppermute | solution.py:338
  36.7 5.6 %collective-permute-start.4 = (bf16[4,256,128]{2,1,0:T(8,128)(2,1)S(1)}, bf16[4,256,128]{2,1,0:T(8,128)(2,1)S(1)}, u32[]{:S(2)}, u32[]{:S(2)}) collective-permute-start(bf16[4,256,128]{2,1,0:T(8,128)(2,1)S(1)} %collective-permute-done.3.refs_2_), channel_id=1, source_target_pairs={{0,448},{64,0},{128,64},{192,128},{256,192},{320,256},{384,320},{4... | collective-permute-start | bytes 786440 | tf_op jit(solution)/shard_map/ppermute | solution.py:338
  42.3 1.9 %collective-permute-start.1 = (bf16[4,256,128]{2,1,0:T(8,128)(2,1)S(1)}, bf16[4,256,128]{2,1,0:T(8,128)(2,1)S(1)}, u32[]{:S(2)}, u32[]{:S(2)}) collective-permute-start(bf16[4,256,128]{2,1,0:T(8,128)(2,1)S(1)} %collective-permute-done.refs_1_), channel_id=1, source_target_pairs={{0,64},{64,128},{128,192},{192,256},{256,320},{320,384},{384,448},... | collective-permute-start | bytes 786440 | tf_op jit(solution)/shard_map/ppermute | solution.py:337
  44.3 1.9 %collective-permute-done.4.refs_4_ = bf16[4,256,128]{2,1,0:T(8,128)(2,1)S(1)} collective-permute-done((bf16[4,256,128]{2,1,0:T(8,128)(2,1)S(1)}, bf16[4,256,128]{2,1,0:T(8,128)(2,1)S(1)}, u32[]{:S(2)}, u32[]{:S(2)}) %collective-permute-start.4) | collective-permute-done | bytes 262176 | tf_op jit(solution)/shard_map/ppermute | solution.py:338
  46.2 5.6 %collective-permute-start.5 = (bf16[4,256,128]{2,1,0:T(8,128)(2,1)S(1)}, bf16[4,256,128]{2,1,0:T(8,128)(2,1)S(1)}, u32[]{:S(2)}, u32[]{:S(2)}) collective-permute-start(bf16[4,256,128]{2,1,0:T(8,128)(2,1)S(1)} %collective-permute-done.4.refs_4_), channel_id=1, source_target_pairs={{0,448},{64,0},{128,64},{192,128},{256,192},{320,256},{384,320},{4... | collective-permute-start | bytes 786440 | tf_op jit(solution)/shard_map/ppermute | solution.py:338
  52.5 1.9 %collective-permute-start.2 = (bf16[4,256,128]{2,1,0:T(8,128)(2,1)S(1)}, bf16[4,256,128]{2,1,0:T(8,128)(2,1)S(1)}, u32[]{:S(2)}, u32[]{:S(2)}) collective-permute-start(bf16[4,256,128]{2,1,0:T(8,128)(2,1)S(1)} %collective-permute-done.1.refs_3_), channel_id=1, source_target_pairs={{0,64},{64,128},{128,192},{192,256},{256,320},{320,384},{384,448},... | collective-permute-start | bytes 786440 | tf_op jit(solution)/shard_map/ppermute | solution.py:337
  55.6 5.6 %collective-permute-start.6 = (bf16[4,256,128]{2,1,0:T(8,128)(2,1)S(1)}, bf16[4,256,128]{2,1,0:T(8,128)(2,1)S(1)}, u32[]{:S(2)}, u32[]{:S(2)}) collective-permute-start(bf16[4,256,128]{2,1,0:T(8,128)(2,1)S(1)} %collective-permute-done.5.refs_1_.refs_6_), channel_id=1, source_target_pairs={{0,448},{64,0},{128,64},{192,128},{256,192},{320,256},{384,320},{4... | collective-permute-start | bytes 786440 | tf_op jit(solution)/shard_map/ppermute | solution.py:340
  62.0 1.8 %shard_map.76.value_ref = bf16[128,512]{1,0:T(8,128)(2,1)S(1)} custom-call(s32[2,2]{1,0:T(2,128)S(1)} %broadcast_and_fusion.table_ref, bf16[128,512]{1,0:T(8,128)(2,1)S(1)} %copy-done.6, bf16[2,128,512]{2,1,0:T(8,128)(2,1)S(1)} %copy-done, bf16[4,4,3,32,512]{4,3,2,1,0:T(8,128)(2,1)S(1)} %bitcast.8, ...), custom_call_target="tpu_custom_call" | custom-call | tf_op jit(solution)/shard_map/pallas_call | solution.py:84
  63.7 1.4 %collective-permute-done.6.refs_0_.refs_7_ = bf16[4,256,128]{2,1,0:T(8,128)(2,1)S(1)} collective-permute-done((bf16[4,256,128]{2,1,0:T(8,128)(2,1)S(1)}, bf16[4,256,128]{2,1,0:T(8,128)(2,1)S(1)}, u32[]{:S(2)}, u32[]{:S(2)}) %collective-permute-start.6) | collective-permute-done | bytes 262176 | tf_op jit(solution)/shard_map/ppermute | solution.py:340
  65.1 1.1 shard_map.77.refs_8_
  66.2 4.6 %all-to-all-start.2 = ((bf16[8,128,512]{2,1,0:T(8,128)(2,1)}), bf16[8,128,512]{2,1,0:T(8,128)(2,1)S(1)}, u32[]{:S(2)}, u32[]{:S(2)}) async-start(bf16[8,128,512]{2,1,0:T(8,128)(2,1)} %shard_map.77.refs_8_), calls=%async_computation.2 | async-start | bytes 2097152 | tf_op jit(solution)/shard_map/all_to_all | solution.py:325
  70.8 1.4 %shard_map.78 = (bf16[4,4,256,128]{3,2,1,0:T(8,128)(2,1)}, bf16[4,4,256,128]{3,2,1,0:T(8,128)(2,1)}) custom-call(bf16[4,256,128]{2,1,0:T(8,128)(2,1)S(1)} %shard_map.75.refs_0_, bf16[4,256,128]{2,1,0:T(8,128)(2,1)S(1)} %collective-permute-done.refs_1_, bf16[4,256,128]{2,1,0:T(8,128)(2,1)S(1)} %collective-permute-done.3.refs_2_, ...), custom_call_target="tpu_custom_call" | custom-call | tf_op jit(solution)/shard_map/pallas_call | solution.py:221
  72.2 1.9 %collective-permute-start.7 = (bf16[4,4,256,128]{3,2,1,0:T(8,128)(2,1)}, bf16[4,4,256,128]{3,2,1,0:T(8,128)(2,1)S(1)}, u32[]{:S(2)}, u32[]{:S(2)}) collective-permute-start(bf16[4,4,256,128]{3,2,1,0:T(8,128)(2,1)} %get-tuple-element.7.refs_0_), channel_id=1, source_target_pairs={{0,16},{16,0},{1,17},{17,1},{2,18},{18,2},{3,19},{19,3},{4,20},{20... | collective-permute-start | bytes 3145736 | tf_op jit(solution)/shard_map/ppermute | solution.py:362
  74.2 2.4 %collective-permute-start.8 = (bf16[4,4,256,128]{3,2,1,0:T(8,128)(2,1)}, bf16[4,4,256,128]{3,2,1,0:T(8,128)(2,1)S(1)}, u32[]{:S(2)}, u32[]{:S(2)}) collective-permute-start(bf16[4,4,256,128]{3,2,1,0:T(8,128)(2,1)} %get-tuple-element.8.refs_1_), channel_id=1, source_target_pairs={{0,16},{16,0},{1,17},{17,1},{2,18},{18,2},{3,19},{19,3},{4,20},{20... | collective-permute-start | bytes 3145736 | tf_op jit(solution)/shard_map/ppermute | solution.py:362
  77.0 2.1 %collective-permute-done.8.refs_3_ = bf16[4,4,256,128]{3,2,1,0:T(8,128)(2,1)S(1)} collective-permute-done((bf16[4,4,256,128]{3,2,1,0:T(8,128)(2,1)}, bf16[4,4,256,128]{3,2,1,0:T(8,128)(2,1)S(1)}, u32[]{:S(2)}, u32[]{:S(2)}) %collective-permute-start.8) | collective-permute-done | bytes 1048608 | tf_op jit(solution)/shard_map/ppermute | solution.py:362
  79.1 3.3 %all-to-all-done.2 = bf16[8,128,512]{2,1,0:T(8,128)(2,1)S(1)} async-done(((bf16[8,128,512]{2,1,0:T(8,128)(2,1)}), bf16[8,128,512]{2,1,0:T(8,128)(2,1)S(1)}, u32[]{:S(2)}, u32[]{:S(2)}) %all-to-all-start.2) | async-done | bytes 1048608 | tf_op jit(solution)/shard_map/all_to_all | solution.py:325
  82.3 3.1 %shard_map.79 = bf16[4,2,4,64,128]{4,3,2,1,0:T(8,128)(2,1)S(1)} custom-call(s32[1]{0:T(128)} %bitcast.1.plane_ref, s32[1]{0:T(128)} %bitcast._.core_ref, bf16[4,2,128,512]{3,2,1,0:T(8,128)(2,1)S(1)} %bitcast.9, bf16[4,4,256,128]{3,2,1,0:T(8,128)(2,1)} %get-tuple-element.7.refs_0_, bf16[4,4,256,128]{3,2,1,0:T(8,128)(2,1)} %get-tuple-element.8.refs_1_, ...), custom_call_target="tpu_custom_call" | custom-call | tf_op jit(solution)/shard_map/pallas_call | solution.py:277
  85.4 24.6 %all_to_all.20 = bf16[32,64,128]{2,1,0:T(8,128)(2,1)S(1)} all-to-all(bf16[32,64,128]{2,1,0:T(8,128)(2,1)S(1)} %bitcast.10), channel_id=1, replica_groups=mesh['z'=8,'yl'=2,'c'=2,'yh'=4,'x'=4] {'x','yl','yh'}, dimensions={0} | all-to-all | bytes 1048576 | tf_op jit(solution)/shard_map/all_to_all | solution.py:325
  (26 shorter events, 6.0 us)
Async XLA Ops:
  0.0 0.9 copy-start.5
  1.9 12.6 %all-to-all-start.1 = ((bf16[8,128,128]{2,1,0:T(8,128)(2,1)}), bf16[8,128,128]{2,1,0:T(8,128)(2,1)S(1)}, u32[]{:S(2)}, u32[]{:S(2)}) async-start(bf16[8,128,128]{2,1,0:T(8,128)(2,1)} %shard_map.74), calls=%async_computation.1 | async-start | bytes 524288 | tf_op jit(solution)/shard_map/all_to_all | solution.py:325
  14.5 46.7 %copy-start.7 = (s32[2,2]{1,0:T(2,128)S(1)}, s32[2,2]{1,0:T(2,128)}, u32[]{:S(2)}) copy-start(s32[2,2]{1,0:T(2,128)} %param.12) | copy-start | bytes 52
  14.5 47.4 %copy-start = (bf16[2,128,512]{2,1,0:T(8,128)(2,1)S(1)}, bf16[2,128,512]{2,1,0:T(8,128)(2,1)}, u32[]{:S(2)}) copy-start(bf16[2,128,512]{2,1,0:T(8,128)(2,1)} %memory_ref.1) | copy-start | bytes 786436
  14.5 47.4 %copy-start.6 = (bf16[128,512]{1,0:T(8,128)(2,1)S(1)}, bf16[128,512]{1,0:T(8,128)(2,1)}, u32[]{:S(2)}) copy-start(bf16[128,512]{1,0:T(8,128)(2,1)} %query_ref.3) | copy-start | bytes 393220
  14.5 47.4 %all-to-all-start = ((bf16[16,3,32,512]{3,2,1,0:T(8,128)(2,1)}), bf16[16,3,32,512]{3,2,1,0:T(8,128)(2,1)S(1)}, u32[]{:S(2)}, u32[]{:S(2)}) async-start(bf16[16,3,32,512]{3,2,1,0:T(8,128)(2,1)} %bitcast.13), calls=%async_computation | async-start | bytes 3145728 | tf_op jit(solution)/shard_map/all_to_all | solution.py:325
  22.0 14.7 %collective-permute-start.3 = (bf16[4,256,128]{2,1,0:T(8,128)(2,1)S(1)}, bf16[4,256,128]{2,1,0:T(8,128)(2,1)S(1)}, u32[]{:S(2)}, u32[]{:S(2)}) collective-permute-start(bf16[4,256,128]{2,1,0:T(8,128)(2,1)S(1)} %shard_map.75.refs_0_), channel_id=1, source_target_pairs={{0,448},{64,0},{128,64},{192,128},{256,192},{320,256},{384,320},{4... | collective-permute-start | bytes 786440 | tf_op jit(solution)/shard_map/ppermute | solution.py:338
  32.8 9.5 %collective-permute-start = (bf16[4,256,128]{2,1,0:T(8,128)(2,1)S(1)}, bf16[4,256,128]{2,1,0:T(8,128)(2,1)S(1)}, u32[]{:S(2)}, u32[]{:S(2)}) collective-permute-start(bf16[4,256,128]{2,1,0:T(8,128)(2,1)S(1)} %shard_map.75.refs_0_), channel_id=1, source_target_pairs={{0,64},{64,128},{128,192},{192,256},{256,320},{320,384},{384,448},... | collective-permute-start | bytes 786440 | tf_op jit(solution)/shard_map/ppermute | solution.py:337
  36.7 9.5 %collective-permute-start.4 = (bf16[4,256,128]{2,1,0:T(8,128)(2,1)S(1)}, bf16[4,256,128]{2,1,0:T(8,128)(2,1)S(1)}, u32[]{:S(2)}, u32[]{:S(2)}) collective-permute-start(bf16[4,256,128]{2,1,0:T(8,128)(2,1)S(1)} %collective-permute-done.3.refs_2_), channel_id=1, source_target_pairs={{0,448},{64,0},{128,64},{192,128},{256,192},{320,256},{384,320},{4... | collective-permute-start | bytes 786440 | tf_op jit(solution)/shard_map/ppermute | solution.py:338
  42.3 10.2 %collective-permute-start.1 = (bf16[4,256,128]{2,1,0:T(8,128)(2,1)S(1)}, bf16[4,256,128]{2,1,0:T(8,128)(2,1)S(1)}, u32[]{:S(2)}, u32[]{:S(2)}) collective-permute-start(bf16[4,256,128]{2,1,0:T(8,128)(2,1)S(1)} %collective-permute-done.refs_1_), channel_id=1, source_target_pairs={{0,64},{64,128},{128,192},{192,256},{256,320},{320,384},{384,448},... | collective-permute-start | bytes 786440 | tf_op jit(solution)/shard_map/ppermute | solution.py:337
  46.2 9.5 %collective-permute-start.5 = (bf16[4,256,128]{2,1,0:T(8,128)(2,1)S(1)}, bf16[4,256,128]{2,1,0:T(8,128)(2,1)S(1)}, u32[]{:S(2)}, u32[]{:S(2)}) collective-permute-start(bf16[4,256,128]{2,1,0:T(8,128)(2,1)S(1)} %collective-permute-done.4.refs_4_), channel_id=1, source_target_pairs={{0,448},{64,0},{128,64},{192,128},{256,192},{320,256},{384,320},{4... | collective-permute-start | bytes 786440 | tf_op jit(solution)/shard_map/ppermute | solution.py:338
  51.8 0.7 copy-start.1
  52.5 9.5 %collective-permute-start.2 = (bf16[4,256,128]{2,1,0:T(8,128)(2,1)S(1)}, bf16[4,256,128]{2,1,0:T(8,128)(2,1)S(1)}, u32[]{:S(2)}, u32[]{:S(2)}) collective-permute-start(bf16[4,256,128]{2,1,0:T(8,128)(2,1)S(1)} %collective-permute-done.1.refs_3_), channel_id=1, source_target_pairs={{0,64},{64,128},{128,192},{192,256},{256,320},{320,384},{384,448},... | collective-permute-start | bytes 786440 | tf_op jit(solution)/shard_map/ppermute | solution.py:337
  54.4 0.7 copy-start.3
  55.6 9.5 %collective-permute-start.6 = (bf16[4,256,128]{2,1,0:T(8,128)(2,1)S(1)}, bf16[4,256,128]{2,1,0:T(8,128)(2,1)S(1)}, u32[]{:S(2)}, u32[]{:S(2)}) collective-permute-start(bf16[4,256,128]{2,1,0:T(8,128)(2,1)S(1)} %collective-permute-done.5.refs_1_.refs_6_), channel_id=1, source_target_pairs={{0,448},{64,0},{128,64},{192,128},{256,192},{320,256},{384,320},{4... | collective-permute-start | bytes 786440 | tf_op jit(solution)/shard_map/ppermute | solution.py:340
  63.7 7.1 %copy-start.2 = (bf16[4,256,128]{2,1,0:T(8,128)(2,1)S(1)}, bf16[4,256,128]{2,1,0:T(8,128)(2,1)}, u32[]{:S(2)}) copy-start(bf16[4,256,128]{2,1,0:T(8,128)(2,1)} %copy-done.1) | copy-start | bytes 786436
  63.7 7.1 %copy-start.4 = (bf16[4,256,128]{2,1,0:T(8,128)(2,1)S(1)}, bf16[4,256,128]{2,1,0:T(8,128)(2,1)}, u32[]{:S(2)}) copy-start(bf16[4,256,128]{2,1,0:T(8,128)(2,1)} %copy-done.3) | copy-start | bytes 786436
  66.2 16.1 %all-to-all-start.2 = ((bf16[8,128,512]{2,1,0:T(8,128)(2,1)}), bf16[8,128,512]{2,1,0:T(8,128)(2,1)S(1)}, u32[]{:S(2)}, u32[]{:S(2)}) async-start(bf16[8,128,512]{2,1,0:T(8,128)(2,1)} %shard_map.77.refs_8_), calls=%async_computation.2 | async-start | bytes 2097152 | tf_op jit(solution)/shard_map/all_to_all | solution.py:325
  72.2 4.8 %collective-permute-start.7 = (bf16[4,4,256,128]{3,2,1,0:T(8,128)(2,1)}, bf16[4,4,256,128]{3,2,1,0:T(8,128)(2,1)S(1)}, u32[]{:S(2)}, u32[]{:S(2)}) collective-permute-start(bf16[4,4,256,128]{3,2,1,0:T(8,128)(2,1)} %get-tuple-element.7.refs_0_), channel_id=1, source_target_pairs={{0,16},{16,0},{1,17},{17,1},{2,18},{18,2},{3,19},{19,3},{4,20},{20... | collective-permute-start | bytes 3145736 | tf_op jit(solution)/shard_map/ppermute | solution.py:362
  74.2 4.9 %collective-permute-start.8 = (bf16[4,4,256,128]{3,2,1,0:T(8,128)(2,1)}, bf16[4,4,256,128]{3,2,1,0:T(8,128)(2,1)S(1)}, u32[]{:S(2)}, u32[]{:S(2)}) collective-permute-start(bf16[4,4,256,128]{3,2,1,0:T(8,128)(2,1)} %get-tuple-element.8.refs_1_), channel_id=1, source_target_pairs={{0,16},{16,0},{1,17},{17,1},{2,18},{18,2},{3,19},{19,3},{4,20},{20... | collective-permute-start | bytes 3145736 | tf_op jit(solution)/shard_map/ppermute | solution.py:362

commit v10 on v9

--- a/solution.py
+++ b/solution.py
@@ -235,10 +235,13 @@
     width = refs[0].shape[-1]
     middle, half, part = width // 2, tokens // 2, width // 4
     planes = TOGETHER * stacks
-    left = [
-        jnp.concatenate([context_ref[x, s] for s in range(sides)], axis=0)
-        for x in range(quarters)
-    ]
+    left = jnp.concatenate(
+        [
+            jnp.concatenate([context_ref[x, s] for s in range(sides)], axis=0)
+            for x in range(quarters)
+        ],
+        axis=1,
+    )
 
     def rows_of(index, x):
         own = refs[index // TOGETHER][index % TOGETHER, x]
@@ -249,11 +252,14 @@
 
     totals = []
     for pair in range(planes // 2):
-        total = None
-        for x in range(quarters):
-            right = jnp.concatenate([rows_of(2 * pair, x), rows_of(2 * pair + 1, x)], axis=1)
-            term = jnp.dot(left[x], right, preferred_element_type=jnp.float32)
-            total = term if total is None else total + term
+        right = jnp.concatenate(
+            [
+                jnp.concatenate([rows_of(2 * pair, x), rows_of(2 * pair + 1, x)], axis=1)
+                for x in range(quarters)
+            ],
+            axis=0,
+        )
+        total = jnp.dot(left, right, preferred_element_type=jnp.float32)
         totals.append(total.astype(jnp.bfloat16))
     for index in range(planes):
         total = totals[index // 2]

time: 112 us -> 112 us (level)
  no operation moved by 1% of the time
where the time goes in v10:
time: 112 us; the launch traced here: 111 us
  starting transfers between devices  54.9 us (49%)
  blocking collectives  24.6 us (22%)
  waiting for transfers between devices  17.2 us (15%)
  Pallas kernels  11.6 us (10%)
  local copies, waits for them, and re-layouts  2.35 us (2%)
    all_to_all x1, blocking collectives, exchange(): value = lax.all_to_all(value, axes, split_axis=0, concat_axis=0, tiled=True)  24.6 us
    ppermute x3, starting transfers between devices, ring(): ahead = lax.ppermute(ahead, axis, down)  22 us
    all_to_all x3, starting transfers between devices, exchange(): value = lax.all_to_all(value, axes, split_axis=0, concat_axis=0, tiled=True)  17.3 us
    all_to_all x3, waiting for transfers between devices, exchange(): value = lax.all_to_all(value, axes, split_axis=0, concat_axis=0, tiled=True)  8.23 us
    ppermute x3, starting transfers between devices, ring(): behind = lax.ppermute(behind, axis, up)  5.75 us
    ppermute x1, starting transfers between devices, ring(): return blocks + [lax.ppermute(ahead, axis, down)]  5.59 us
    ppermute x3, waiting for transfers between devices, ring(): ahead = lax.ppermute(ahead, axis, down)  4.42 us
    ppermute x2, starting transfers between devices, local(): sib = [lax.ppermute(block, 'c', [(0, 1), (1, 0)]) for block in own]  4.31 us
  transfers between devices with their start and end apart: 12, of which 9 were waited for; matrix products, arithmetic and copies ran while one was open for 0% of the time, Pallas kernels for 5%

profile of v10, /device:TPU:16, one launch (start us, length us, event | category | flops | bytes accessed | tf_op | source)
XLA Modules:
  0.0 110.8 jit_solution(18284887625868986771)
XLA Ops:
  1.9 5.3 %all-to-all-start.1 = ((bf16[8,128,128]{2,1,0:T(8,128)(2,1)}), bf16[8,128,128]{2,1,0:T(8,128)(2,1)S(1)}, u32[]{:S(2)}, u32[]{:S(2)}) async-start(bf16[8,128,128]{2,1,0:T(8,128)(2,1)} %shard_map.74), calls=%async_computation.1 | async-start | bytes 524288 | tf_op jit(solution)/shard_map/all_to_all | solution.py:331
  7.2 2.3 %shard_map.73 = bf16[4,4,3,32,512]{4,3,2,1,0:T(8,128)(2,1)} custom-call(bf16[32,8192]{1,0:T(8,128)(2,1)} %query_ref.2, bf16[32,8192]{1,0:T(8,128)(2,1)} %key_ref.1, bf16[32,8192]{1,0:T(8,128)(2,1)} %value_ref.1), custom_call_target="tpu_custom_call" | custom-call | tf_op jit(solution)/shard_map/pallas_call | solution.py:145
  9.6 4.9 %all-to-all-done.1 = bf16[8,128,128]{2,1,0:T(8,128)(2,1)S(1)} async-done(((bf16[8,128,128]{2,1,0:T(8,128)(2,1)}), bf16[8,128,128]{2,1,0:T(8,128)(2,1)S(1)}, u32[]{:S(2)}, u32[]{:S(2)}) %all-to-all-start.1) | async-done | bytes 262176 | tf_op jit(solution)/shard_map/all_to_all | solution.py:331
  14.5 7.4 %all-to-all-start = ((bf16[16,3,32,512]{3,2,1,0:T(8,128)(2,1)}), bf16[16,3,32,512]{3,2,1,0:T(8,128)(2,1)S(1)}, u32[]{:S(2)}, u32[]{:S(2)}) async-start(bf16[16,3,32,512]{3,2,1,0:T(8,128)(2,1)} %bitcast.13), calls=%async_computation | async-start | bytes 3145728 | tf_op jit(solution)/shard_map/all_to_all | solution.py:331
  22.0 10.8 %collective-permute-start.3 = (bf16[4,256,128]{2,1,0:T(8,128)(2,1)S(1)}, bf16[4,256,128]{2,1,0:T(8,128)(2,1)S(1)}, u32[]{:S(2)}, u32[]{:S(2)}) collective-permute-start(bf16[4,256,128]{2,1,0:T(8,128)(2,1)S(1)} %shard_map.75.refs_0_), channel_id=1, source_target_pairs={{0,448},{64,0},{128,64},{192,128},{256,192},{320,256},{384,320},{4... | collective-permute-start | bytes 786440 | tf_op jit(solution)/shard_map/ppermute | solution.py:344
  32.8 1.9 %collective-permute-start = (bf16[4,256,128]{2,1,0:T(8,128)(2,1)S(1)}, bf16[4,256,128]{2,1,0:T(8,128)(2,1)S(1)}, u32[]{:S(2)}, u32[]{:S(2)}) collective-permute-start(bf16[4,256,128]{2,1,0:T(8,128)(2,1)S(1)} %shard_map.75.refs_0_), channel_id=1, source_target_pairs={{0,64},{64,128},{128,192},{192,256},{256,320},{320,384},{384,448},... | collective-permute-start | bytes 786440 | tf_op jit(solution)/shard_map/ppermute | solution.py:343
  34.8 1.9 %collective-permute-done.3.refs_2_ = bf16[4,256,128]{2,1,0:T(8,128)(2,1)S(1)} collective-permute-done((bf16[4,256,128]{2,1,0:T(8,128)(2,1)S(1)}, bf16[4,256,128]{2,1,0:T(8,128)(2,1)S(1)}, u32[]{:S(2)}, u32[]{:S(2)}) %collective-permute-start.3) | collective-permute-done | bytes 262176 | tf_op jit(solution)/shard_map/ppermute | solution.py:344
  36.7 5.6 %collective-permute-start.4 = (bf16[4,256,128]{2,1,0:T(8,128)(2,1)S(1)}, bf16[4,256,128]{2,1,0:T(8,128)(2,1)S(1)}, u32[]{:S(2)}, u32[]{:S(2)}) collective-permute-start(bf16[4,256,128]{2,1,0:T(8,128)(2,1)S(1)} %collective-permute-done.3.refs_2_), channel_id=1, source_target_pairs={{0,448},{64,0},{128,64},{192,128},{256,192},{320,256},{384,320},{4... | collective-permute-start | bytes 786440 | tf_op jit(solution)/shard_map/ppermute | solution.py:344
  42.3 1.9 %collective-permute-start.1 = (bf16[4,256,128]{2,1,0:T(8,128)(2,1)S(1)}, bf16[4,256,128]{2,1,0:T(8,128)(2,1)S(1)}, u32[]{:S(2)}, u32[]{:S(2)}) collective-permute-start(bf16[4,256,128]{2,1,0:T(8,128)(2,1)S(1)} %collective-permute-done.refs_1_), channel_id=1, source_target_pairs={{0,64},{64,128},{128,192},{192,256},{256,320},{320,384},{384,448},... | collective-permute-start | bytes 786440 | tf_op jit(solution)/shard_map/ppermute | solution.py:343
  44.3 1.9 %collective-permute-done.4.refs_4_ = bf16[4,256,128]{2,1,0:T(8,128)(2,1)S(1)} collective-permute-done((bf16[4,256,128]{2,1,0:T(8,128)(2,1)S(1)}, bf16[4,256,128]{2,1,0:T(8,128)(2,1)S(1)}, u32[]{:S(2)}, u32[]{:S(2)}) %collective-permute-start.4) | collective-permute-done | bytes 262176 | tf_op jit(solution)/shard_map/ppermute | solution.py:344
  46.2 5.6 %collective-permute-start.5 = (bf16[4,256,128]{2,1,0:T(8,128)(2,1)S(1)}, bf16[4,256,128]{2,1,0:T(8,128)(2,1)S(1)}, u32[]{:S(2)}, u32[]{:S(2)}) collective-permute-start(bf16[4,256,128]{2,1,0:T(8,128)(2,1)S(1)} %collective-permute-done.4.refs_4_), channel_id=1, source_target_pairs={{0,448},{64,0},{128,64},{192,128},{256,192},{320,256},{384,320},{4... | collective-permute-start | bytes 786440 | tf_op jit(solution)/shard_map/ppermute | solution.py:344
  52.5 1.9 %collective-permute-start.2 = (bf16[4,256,128]{2,1,0:T(8,128)(2,1)S(1)}, bf16[4,256,128]{2,1,0:T(8,128)(2,1)S(1)}, u32[]{:S(2)}, u32[]{:S(2)}) collective-permute-start(bf16[4,256,128]{2,1,0:T(8,128)(2,1)S(1)} %collective-permute-done.1.refs_3_), channel_id=1, source_target_pairs={{0,64},{64,128},{128,192},{192,256},{256,320},{320,384},{384,448},... | collective-permute-start | bytes 786440 | tf_op jit(solution)/shard_map/ppermute | solution.py:343
  55.6 5.6 %collective-permute-start.6 = (bf16[4,256,128]{2,1,0:T(8,128)(2,1)S(1)}, bf16[4,256,128]{2,1,0:T(8,128)(2,1)S(1)}, u32[]{:S(2)}, u32[]{:S(2)}) collective-permute-start(bf16[4,256,128]{2,1,0:T(8,128)(2,1)S(1)} %collective-permute-done.5.refs_1_.refs_6_), channel_id=1, source_target_pairs={{0,448},{64,0},{128,64},{192,128},{256,192},{320,256},{384,320},{4... | collective-permute-start | bytes 786440 | tf_op jit(solution)/shard_map/ppermute | solution.py:346
  62.0 1.8 %shard_map.76.value_ref = bf16[128,512]{1,0:T(8,128)(2,1)S(1)} custom-call(s32[2,2]{1,0:T(2,128)S(1)} %broadcast_and_fusion.table_ref, bf16[128,512]{1,0:T(8,128)(2,1)S(1)} %copy-done.6, bf16[2,128,512]{2,1,0:T(8,128)(2,1)S(1)} %copy-done, bf16[4,4,3,32,512]{4,3,2,1,0:T(8,128)(2,1)S(1)} %bitcast.8, ...), custom_call_target="tpu_custom_call" | custom-call | tf_op jit(solution)/shard_map/pallas_call | solution.py:84
  63.7 1.4 %collective-permute-done.6.refs_0_.refs_7_ = bf16[4,256,128]{2,1,0:T(8,128)(2,1)S(1)} collective-permute-done((bf16[4,256,128]{2,1,0:T(8,128)(2,1)S(1)}, bf16[4,256,128]{2,1,0:T(8,128)(2,1)S(1)}, u32[]{:S(2)}, u32[]{:S(2)}) %collective-permute-start.6) | collective-permute-done | bytes 262176 | tf_op jit(solution)/shard_map/ppermute | solution.py:346
  65.1 1.1 shard_map.77.refs_8_
  66.2 4.6 %all-to-all-start.2 = ((bf16[8,128,512]{2,1,0:T(8,128)(2,1)}), bf16[8,128,512]{2,1,0:T(8,128)(2,1)S(1)}, u32[]{:S(2)}, u32[]{:S(2)}) async-start(bf16[8,128,512]{2,1,0:T(8,128)(2,1)} %shard_map.77.refs_8_), calls=%async_computation.2 | async-start | bytes 2097152 | tf_op jit(solution)/shard_map/all_to_all | solution.py:331
  70.8 1.4 %shard_map.78 = (bf16[4,4,256,128]{3,2,1,0:T(8,128)(2,1)}, bf16[4,4,256,128]{3,2,1,0:T(8,128)(2,1)}) custom-call(bf16[4,256,128]{2,1,0:T(8,128)(2,1)S(1)} %shard_map.75.refs_0_, bf16[4,256,128]{2,1,0:T(8,128)(2,1)S(1)} %collective-permute-done.refs_1_, bf16[4,256,128]{2,1,0:T(8,128)(2,1)S(1)} %collective-permute-done.3.refs_2_, ...), custom_call_target="tpu_custom_call" | custom-call | tf_op jit(solution)/shard_map/pallas_call | solution.py:221
  72.2 1.9 %collective-permute-start.7 = (bf16[4,4,256,128]{3,2,1,0:T(8,128)(2,1)}, bf16[4,4,256,128]{3,2,1,0:T(8,128)(2,1)S(1)}, u32[]{:S(2)}, u32[]{:S(2)}) collective-permute-start(bf16[4,4,256,128]{3,2,1,0:T(8,128)(2,1)} %get-tuple-element.7.refs_0_), channel_id=1, source_target_pairs={{0,16},{16,0},{1,17},{17,1},{2,18},{18,2},{3,19},{19,3},{4,20},{20... | collective-permute-start | bytes 3145736 | tf_op jit(solution)/shard_map/ppermute | solution.py:368
  74.2 2.4 %collective-permute-start.8 = (bf16[4,4,256,128]{3,2,1,0:T(8,128)(2,1)}, bf16[4,4,256,128]{3,2,1,0:T(8,128)(2,1)S(1)}, u32[]{:S(2)}, u32[]{:S(2)}) collective-permute-start(bf16[4,4,256,128]{3,2,1,0:T(8,128)(2,1)} %get-tuple-element.8.refs_1_), channel_id=1, source_target_pairs={{0,16},{16,0},{1,17},{17,1},{2,18},{18,2},{3,19},{19,3},{4,20},{20... | collective-permute-start | bytes 3145736 | tf_op jit(solution)/shard_map/ppermute | solution.py:368
  77.0 2.1 %collective-permute-done.8.refs_3_ = bf16[4,4,256,128]{3,2,1,0:T(8,128)(2,1)S(1)} collective-permute-done((bf16[4,4,256,128]{3,2,1,0:T(8,128)(2,1)}, bf16[4,4,256,128]{3,2,1,0:T(8,128)(2,1)S(1)}, u32[]{:S(2)}, u32[]{:S(2)}) %collective-permute-start.8) | collective-permute-done | bytes 1048608 | tf_op jit(solution)/shard_map/ppermute | solution.py:368
  79.1 3.3 %all-to-all-done.2 = bf16[8,128,512]{2,1,0:T(8,128)(2,1)S(1)} async-done(((bf16[8,128,512]{2,1,0:T(8,128)(2,1)}), bf16[8,128,512]{2,1,0:T(8,128)(2,1)S(1)}, u32[]{:S(2)}, u32[]{:S(2)}) %all-to-all-start.2) | async-done | bytes 1048608 | tf_op jit(solution)/shard_map/all_to_all | solution.py:331
  82.3 3.0 %shard_map.79 = bf16[4,2,4,64,128]{4,3,2,1,0:T(8,128)(2,1)S(1)} custom-call(s32[1]{0:T(128)} %bitcast.1.plane_ref, s32[1]{0:T(128)} %bitcast._.core_ref, bf16[4,2,128,512]{3,2,1,0:T(8,128)(2,1)S(1)} %bitcast.9, bf16[4,4,256,128]{3,2,1,0:T(8,128)(2,1)} %get-tuple-element.7.refs_0_, bf16[4,4,256,128]{3,2,1,0:T(8,128)(2,1)} %get-tuple-element.8.refs_1_, ...), custom_call_target="tpu_custom_call" | custom-call | tf_op jit(solution)/shard_map/pallas_call | solution.py:283
  85.4 24.6 %all_to_all.20 = bf16[32,64,128]{2,1,0:T(8,128)(2,1)S(1)} all-to-all(bf16[32,64,128]{2,1,0:T(8,128)(2,1)S(1)} %bitcast.10), channel_id=1, replica_groups=mesh['z'=8,'yl'=2,'c'=2,'yh'=4,'x'=4] {'x','yl','yh'}, dimensions={0} | all-to-all | bytes 1048576 | tf_op jit(solution)/shard_map/all_to_all | solution.py:331
  (26 shorter events, 6.0 us)
Async XLA Ops:
  0.0 0.9 copy-start.5
  1.9 12.6 %all-to-all-start.1 = ((bf16[8,128,128]{2,1,0:T(8,128)(2,1)}), bf16[8,128,128]{2,1,0:T(8,128)(2,1)S(1)}, u32[]{:S(2)}, u32[]{:S(2)}) async-start(bf16[8,128,128]{2,1,0:T(8,128)(2,1)} %shard_map.74), calls=%async_computation.1 | async-start | bytes 524288 | tf_op jit(solution)/shard_map/all_to_all | solution.py:331
  14.5 46.7 %copy-start.7 = (s32[2,2]{1,0:T(2,128)S(1)}, s32[2,2]{1,0:T(2,128)}, u32[]{:S(2)}) copy-start(s32[2,2]{1,0:T(2,128)} %param.12) | copy-start | bytes 52
  14.5 47.4 %copy-start = (bf16[2,128,512]{2,1,0:T(8,128)(2,1)S(1)}, bf16[2,128,512]{2,1,0:T(8,128)(2,1)}, u32[]{:S(2)}) copy-start(bf16[2,128,512]{2,1,0:T(8,128)(2,1)} %memory_ref.1) | copy-start | bytes 786436
  14.5 47.4 %copy-start.6 = (bf16[128,512]{1,0:T(8,128)(2,1)S(1)}, bf16[128,512]{1,0:T(8,128)(2,1)}, u32[]{:S(2)}) copy-start(bf16[128,512]{1,0:T(8,128)(2,1)} %query_ref.3) | copy-start | bytes 393220
  14.5 47.4 %all-to-all-start = ((bf16[16,3,32,512]{3,2,1,0:T(8,128)(2,1)}), bf16[16,3,32,512]{3,2,1,0:T(8,128)(2,1)S(1)}, u32[]{:S(2)}, u32[]{:S(2)}) async-start(bf16[16,3,32,512]{3,2,1,0:T(8,128)(2,1)} %bitcast.13), calls=%async_computation | async-start | bytes 3145728 | tf_op jit(solution)/shard_map/all_to_all | solution.py:331
  22.0 14.7 %collective-permute-start.3 = (bf16[4,256,128]{2,1,0:T(8,128)(2,1)S(1)}, bf16[4,256,128]{2,1,0:T(8,128)(2,1)S(1)}, u32[]{:S(2)}, u32[]{:S(2)}) collective-permute-start(bf16[4,256,128]{2,1,0:T(8,128)(2,1)S(1)} %shard_map.75.refs_0_), channel_id=1, source_target_pairs={{0,448},{64,0},{128,64},{192,128},{256,192},{320,256},{384,320},{4... | collective-permute-start | bytes 786440 | tf_op jit(solution)/shard_map/ppermute | solution.py:344
  32.8 9.5 %collective-permute-start = (bf16[4,256,128]{2,1,0:T(8,128)(2,1)S(1)}, bf16[4,256,128]{2,1,0:T(8,128)(2,1)S(1)}, u32[]{:S(2)}, u32[]{:S(2)}) collective-permute-start(bf16[4,256,128]{2,1,0:T(8,128)(2,1)S(1)} %shard_map.75.refs_0_), channel_id=1, source_target_pairs={{0,64},{64,128},{128,192},{192,256},{256,320},{320,384},{384,448},... | collective-permute-start | bytes 786440 | tf_op jit(solution)/shard_map/ppermute | solution.py:343
  36.7 9.5 %collective-permute-start.4 = (bf16[4,256,128]{2,1,0:T(8,128)(2,1)S(1)}, bf16[4,256,128]{2,1,0:T(8,128)(2,1)S(1)}, u32[]{:S(2)}, u32[]{:S(2)}) collective-permute-start(bf16[4,256,128]{2,1,0:T(8,128)(2,1)S(1)} %collective-permute-done.3.refs_2_), channel_id=1, source_target_pairs={{0,448},{64,0},{128,64},{192,128},{256,192},{320,256},{384,320},{4... | collective-permute-start | bytes 786440 | tf_op jit(solution)/shard_map/ppermute | solution.py:344
  42.3 10.2 %collective-permute-start.1 = (bf16[4,256,128]{2,1,0:T(8,128)(2,1)S(1)}, bf16[4,256,128]{2,1,0:T(8,128)(2,1)S(1)}, u32[]{:S(2)}, u32[]{:S(2)}) collective-permute-start(bf16[4,256,128]{2,1,0:T(8,128)(2,1)S(1)} %collective-permute-done.refs_1_), channel_id=1, source_target_pairs={{0,64},{64,128},{128,192},{192,256},{256,320},{320,384},{384,448},... | collective-permute-start | bytes 786440 | tf_op jit(solution)/shard_map/ppermute | solution.py:343
  46.2 9.5 %collective-permute-start.5 = (bf16[4,256,128]{2,1,0:T(8,128)(2,1)S(1)}, bf16[4,256,128]{2,1,0:T(8,128)(2,1)S(1)}, u32[]{:S(2)}, u32[]{:S(2)}) collective-permute-start(bf16[4,256,128]{2,1,0:T(8,128)(2,1)S(1)} %collective-permute-done.4.refs_4_), channel_id=1, source_target_pairs={{0,448},{64,0},{128,64},{192,128},{256,192},{320,256},{384,320},{4... | collective-permute-start | bytes 786440 | tf_op jit(solution)/shard_map/ppermute | solution.py:344
  51.8 0.7 copy-start.1
  52.5 9.5 %collective-permute-start.2 = (bf16[4,256,128]{2,1,0:T(8,128)(2,1)S(1)}, bf16[4,256,128]{2,1,0:T(8,128)(2,1)S(1)}, u32[]{:S(2)}, u32[]{:S(2)}) collective-permute-start(bf16[4,256,128]{2,1,0:T(8,128)(2,1)S(1)} %collective-permute-done.1.refs_3_), channel_id=1, source_target_pairs={{0,64},{64,128},{128,192},{192,256},{256,320},{320,384},{384,448},... | collective-permute-start | bytes 786440 | tf_op jit(solution)/shard_map/ppermute | solution.py:343
  54.4 0.7 copy-start.3
  55.6 9.5 %collective-permute-start.6 = (bf16[4,256,128]{2,1,0:T(8,128)(2,1)S(1)}, bf16[4,256,128]{2,1,0:T(8,128)(2,1)S(1)}, u32[]{:S(2)}, u32[]{:S(2)}) collective-permute-start(bf16[4,256,128]{2,1,0:T(8,128)(2,1)S(1)} %collective-permute-done.5.refs_1_.refs_6_), channel_id=1, source_target_pairs={{0,448},{64,0},{128,64},{192,128},{256,192},{320,256},{384,320},{4... | collective-permute-start | bytes 786440 | tf_op jit(solution)/shard_map/ppermute | solution.py:346
  63.7 7.1 %copy-start.2 = (bf16[4,256,128]{2,1,0:T(8,128)(2,1)S(1)}, bf16[4,256,128]{2,1,0:T(8,128)(2,1)}, u32[]{:S(2)}) copy-start(bf16[4,256,128]{2,1,0:T(8,128)(2,1)} %copy-done.1) | copy-start | bytes 786436
  63.7 7.1 %copy-start.4 = (bf16[4,256,128]{2,1,0:T(8,128)(2,1)S(1)}, bf16[4,256,128]{2,1,0:T(8,128)(2,1)}, u32[]{:S(2)}) copy-start(bf16[4,256,128]{2,1,0:T(8,128)(2,1)} %copy-done.3) | copy-start | bytes 786436
  66.2 16.1 %all-to-all-start.2 = ((bf16[8,128,512]{2,1,0:T(8,128)(2,1)}), bf16[8,128,512]{2,1,0:T(8,128)(2,1)S(1)}, u32[]{:S(2)}, u32[]{:S(2)}) async-start(bf16[8,128,512]{2,1,0:T(8,128)(2,1)} %shard_map.77.refs_8_), calls=%async_computation.2 | async-start | bytes 2097152 | tf_op jit(solution)/shard_map/all_to_all | solution.py:331
  72.2 4.8 %collective-permute-start.7 = (bf16[4,4,256,128]{3,2,1,0:T(8,128)(2,1)}, bf16[4,4,256,128]{3,2,1,0:T(8,128)(2,1)S(1)}, u32[]{:S(2)}, u32[]{:S(2)}) collective-permute-start(bf16[4,4,256,128]{3,2,1,0:T(8,128)(2,1)} %get-tuple-element.7.refs_0_), channel_id=1, source_target_pairs={{0,16},{16,0},{1,17},{17,1},{2,18},{18,2},{3,19},{19,3},{4,20},{20... | collective-permute-start | bytes 3145736 | tf_op jit(solution)/shard_map/ppermute | solution.py:368
  74.2 4.9 %collective-permute-start.8 = (bf16[4,4,256,128]{3,2,1,0:T(8,128)(2,1)}, bf16[4,4,256,128]{3,2,1,0:T(8,128)(2,1)S(1)}, u32[]{:S(2)}, u32[]{:S(2)}) collective-permute-start(bf16[4,4,256,128]{3,2,1,0:T(8,128)(2,1)} %get-tuple-element.8.refs_1_), channel_id=1, source_target_pairs={{0,16},{16,0},{1,17},{17,1},{2,18},{18,2},{3,19},{19,3},{4,20},{20... | collective-permute-start | bytes 3145736 | tf_op jit(solution)/shard_map/ppermute | solution.py:368

commit v11 on v10

--- a/solution.py
+++ b/solution.py
@@ -20,7 +20,7 @@
 
 def softmax_rows(scores):
     row_top = jnp.max(scores, axis=-1, keepdims=True)
-    expo = jnp.exp(scores - row_top)
+    expo = jnp.exp((scores - row_top) * SCALE)
     return (expo * (1.0 / jnp.sum(expo, axis=-1, keepdims=True))).astype(jnp.bfloat16)
 
 
@@ -52,11 +52,11 @@
         )
 
     enc_scores = [
-        rows_times_rows(gathered(0, u, cols), memory_ref[0, rows, cols]) * SCALE
+        rows_times_rows(gathered(0, u, cols), memory_ref[0, rows, cols])
         for u, rows, cols in parts
     ]
     dec_scores = [
-        rows_times_rows(query_ref[rows, cols], gathered(1, u, cols)) * SCALE
+        rows_times_rows(query_ref[rows, cols], gathered(1, u, cols))
         for u, rows, cols in parts
     ]
     enc_probs = [softmax_rows(scores) for scores in enc_scores]

time: 112 us -> 112 us (level)
  no operation moved by 1% of the time
where the time goes in v11:
time: 112 us; the launch traced here: 111 us
  starting transfers between devices  54.9 us (49%)
  blocking collectives  24.6 us (22%)
  waiting for transfers between devices  17.2 us (15%)
  Pallas kernels  11.6 us (10%)
  local copies, waits for them, and re-layouts  2.35 us (2%)
    all_to_all x1, blocking collectives, exchange(): value = lax.all_to_all(value, axes, split_axis=0, concat_axis=0, tiled=True)  24.6 us
    ppermute x3, starting transfers between devices, ring(): ahead = lax.ppermute(ahead, axis, down)  22 us
    all_to_all x3, starting transfers between devices, exchange(): value = lax.all_to_all(value, axes, split_axis=0, concat_axis=0, tiled=True)  17.3 us
    all_to_all x3, waiting for transfers between devices, exchange(): value = lax.all_to_all(value, axes, split_axis=0, concat_axis=0, tiled=True)  8.23 us
    ppermute x3, starting transfers between devices, ring(): behind = lax.ppermute(behind, axis, up)  5.75 us
    ppermute x1, starting transfers between devices, ring(): return blocks + [lax.ppermute(ahead, axis, down)]  5.59 us
    ppermute x3, waiting for transfers between devices, ring(): ahead = lax.ppermute(ahead, axis, down)  4.42 us
    ppermute x2, starting transfers between devices, local(): sib = [lax.ppermute(block, 'c', [(0, 1), (1, 0)]) for block in own]  4.31 us
  transfers between devices with their start and end apart: 12, of which 9 were waited for; matrix products, arithmetic and copies ran while one was open for 0% of the time, Pallas kernels for 5%

profile of v11, /device:TPU:16, one launch (start us, length us, event | category | flops | bytes accessed | tf_op | source)
XLA Modules:
  0.0 110.8 jit_solution(5660105956701203944)
XLA Ops:
  1.9 5.3 %all-to-all-start.1 = ((bf16[8,128,128]{2,1,0:T(8,128)(2,1)}), bf16[8,128,128]{2,1,0:T(8,128)(2,1)S(1)}, u32[]{:S(2)}, u32[]{:S(2)}) async-start(bf16[8,128,128]{2,1,0:T(8,128)(2,1)} %shard_map.74), calls=%async_computation.1 | async-start | bytes 524288 | tf_op jit(solution)/shard_map/all_to_all | solution.py:331
  7.2 2.3 %shard_map.73 = bf16[4,4,3,32,512]{4,3,2,1,0:T(8,128)(2,1)} custom-call(bf16[32,8192]{1,0:T(8,128)(2,1)} %query_ref.2, bf16[32,8192]{1,0:T(8,128)(2,1)} %key_ref.1, bf16[32,8192]{1,0:T(8,128)(2,1)} %value_ref.1), custom_call_target="tpu_custom_call" | custom-call | tf_op jit(solution)/shard_map/pallas_call | solution.py:145
  9.6 4.9 %all-to-all-done.1 = bf16[8,128,128]{2,1,0:T(8,128)(2,1)S(1)} async-done(((bf16[8,128,128]{2,1,0:T(8,128)(2,1)}), bf16[8,128,128]{2,1,0:T(8,128)(2,1)S(1)}, u32[]{:S(2)}, u32[]{:S(2)}) %all-to-all-start.1) | async-done | bytes 262176 | tf_op jit(solution)/shard_map/all_to_all | solution.py:331
  14.5 7.4 %all-to-all-start = ((bf16[16,3,32,512]{3,2,1,0:T(8,128)(2,1)}), bf16[16,3,32,512]{3,2,1,0:T(8,128)(2,1)S(1)}, u32[]{:S(2)}, u32[]{:S(2)}) async-start(bf16[16,3,32,512]{3,2,1,0:T(8,128)(2,1)} %bitcast.13), calls=%async_computation | async-start | bytes 3145728 | tf_op jit(solution)/shard_map/all_to_all | solution.py:331
  22.0 10.8 %collective-permute-start.3 = (bf16[4,256,128]{2,1,0:T(8,128)(2,1)S(1)}, bf16[4,256,128]{2,1,0:T(8,128)(2,1)S(1)}, u32[]{:S(2)}, u32[]{:S(2)}) collective-permute-start(bf16[4,256,128]{2,1,0:T(8,128)(2,1)S(1)} %shard_map.75.refs_0_), channel_id=1, source_target_pairs={{0,448},{64,0},{128,64},{192,128},{256,192},{320,256},{384,320},{4... | collective-permute-start | bytes 786440 | tf_op jit(solution)/shard_map/ppermute | solution.py:344
  32.8 1.9 %collective-permute-start = (bf16[4,256,128]{2,1,0:T(8,128)(2,1)S(1)}, bf16[4,256,128]{2,1,0:T(8,128)(2,1)S(1)}, u32[]{:S(2)}, u32[]{:S(2)}) collective-permute-start(bf16[4,256,128]{2,1,0:T(8,128)(2,1)S(1)} %shard_map.75.refs_0_), channel_id=1, source_target_pairs={{0,64},{64,128},{128,192},{192,256},{256,320},{320,384},{384,448},... | collective-permute-start | bytes 786440 | tf_op jit(solution)/shard_map/ppermute | solution.py:343
  34.8 1.9 %collective-permute-done.3.refs_2_ = bf16[4,256,128]{2,1,0:T(8,128)(2,1)S(1)} collective-permute-done((bf16[4,256,128]{2,1,0:T(8,128)(2,1)S(1)}, bf16[4,256,128]{2,1,0:T(8,128)(2,1)S(1)}, u32[]{:S(2)}, u32[]{:S(2)}) %collective-permute-start.3) | collective-permute-done | bytes 262176 | tf_op jit(solution)/shard_map/ppermute | solution.py:344
  36.7 5.6 %collective-permute-start.4 = (bf16[4,256,128]{2,1,0:T(8,128)(2,1)S(1)}, bf16[4,256,128]{2,1,0:T(8,128)(2,1)S(1)}, u32[]{:S(2)}, u32[]{:S(2)}) collective-permute-start(bf16[4,256,128]{2,1,0:T(8,128)(2,1)S(1)} %collective-permute-done.3.refs_2_), channel_id=1, source_target_pairs={{0,448},{64,0},{128,64},{192,128},{256,192},{320,256},{384,320},{4... | collective-permute-start | bytes 786440 | tf_op jit(solution)/shard_map/ppermute | solution.py:344
  42.3 1.9 %collective-permute-start.1 = (bf16[4,256,128]{2,1,0:T(8,128)(2,1)S(1)}, bf16[4,256,128]{2,1,0:T(8,128)(2,1)S(1)}, u32[]{:S(2)}, u32[]{:S(2)}) collective-permute-start(bf16[4,256,128]{2,1,0:T(8,128)(2,1)S(1)} %collective-permute-done.refs_1_), channel_id=1, source_target_pairs={{0,64},{64,128},{128,192},{192,256},{256,320},{320,384},{384,448},... | collective-permute-start | bytes 786440 | tf_op jit(solution)/shard_map/ppermute | solution.py:343
  44.3 1.9 %collective-permute-done.4.refs_4_ = bf16[4,256,128]{2,1,0:T(8,128)(2,1)S(1)} collective-permute-done((bf16[4,256,128]{2,1,0:T(8,128)(2,1)S(1)}, bf16[4,256,128]{2,1,0:T(8,128)(2,1)S(1)}, u32[]{:S(2)}, u32[]{:S(2)}) %collective-permute-start.4) | collective-permute-done | bytes 262176 | tf_op jit(solution)/shard_map/ppermute | solution.py:344
  46.2 5.6 %collective-permute-start.5 = (bf16[4,256,128]{2,1,0:T(8,128)(2,1)S(1)}, bf16[4,256,128]{2,1,0:T(8,128)(2,1)S(1)}, u32[]{:S(2)}, u32[]{:S(2)}) collective-permute-start(bf16[4,256,128]{2,1,0:T(8,128)(2,1)S(1)} %collective-permute-done.4.refs_4_), channel_id=1, source_target_pairs={{0,448},{64,0},{128,64},{192,128},{256,192},{320,256},{384,320},{4... | collective-permute-start | bytes 786440 | tf_op jit(solution)/shard_map/ppermute | solution.py:344
  52.5 1.9 %collective-permute-start.2 = (bf16[4,256,128]{2,1,0:T(8,128)(2,1)S(1)}, bf16[4,256,128]{2,1,0:T(8,128)(2,1)S(1)}, u32[]{:S(2)}, u32[]{:S(2)}) collective-permute-start(bf16[4,256,128]{2,1,0:T(8,128)(2,1)S(1)} %collective-permute-done.1.refs_3_), channel_id=1, source_target_pairs={{0,64},{64,128},{128,192},{192,256},{256,320},{320,384},{384,448},... | collective-permute-start | bytes 786440 | tf_op jit(solution)/shard_map/ppermute | solution.py:343
  55.6 5.6 %collective-permute-start.6 = (bf16[4,256,128]{2,1,0:T(8,128)(2,1)S(1)}, bf16[4,256,128]{2,1,0:T(8,128)(2,1)S(1)}, u32[]{:S(2)}, u32[]{:S(2)}) collective-permute-start(bf16[4,256,128]{2,1,0:T(8,128)(2,1)S(1)} %collective-permute-done.5.refs_1_.refs_6_), channel_id=1, source_target_pairs={{0,448},{64,0},{128,64},{192,128},{256,192},{320,256},{384,320},{4... | collective-permute-start | bytes 786440 | tf_op jit(solution)/shard_map/ppermute | solution.py:346
  62.0 1.7 %shard_map.76.value_ref = bf16[128,512]{1,0:T(8,128)(2,1)S(1)} custom-call(s32[2,2]{1,0:T(2,128)S(1)} %broadcast_and_fusion.table_ref, bf16[128,512]{1,0:T(8,128)(2,1)S(1)} %copy-done.6, bf16[2,128,512]{2,1,0:T(8,128)(2,1)S(1)} %copy-done, bf16[4,4,3,32,512]{4,3,2,1,0:T(8,128)(2,1)S(1)} %bitcast.8, ...), custom_call_target="tpu_custom_call" | custom-call | tf_op jit(solution)/shard_map/pallas_call | solution.py:84
  63.7 1.4 %collective-permute-done.6.refs_0_.refs_7_ = bf16[4,256,128]{2,1,0:T(8,128)(2,1)S(1)} collective-permute-done((bf16[4,256,128]{2,1,0:T(8,128)(2,1)S(1)}, bf16[4,256,128]{2,1,0:T(8,128)(2,1)S(1)}, u32[]{:S(2)}, u32[]{:S(2)}) %collective-permute-start.6) | collective-permute-done | bytes 262176 | tf_op jit(solution)/shard_map/ppermute | solution.py:346
  65.1 1.1 shard_map.77.refs_8_
  66.2 4.6 %all-to-all-start.2 = ((bf16[8,128,512]{2,1,0:T(8,128)(2,1)}), bf16[8,128,512]{2,1,0:T(8,128)(2,1)S(1)}, u32[]{:S(2)}, u32[]{:S(2)}) async-start(bf16[8,128,512]{2,1,0:T(8,128)(2,1)} %shard_map.77.refs_8_), calls=%async_computation.2 | async-start | bytes 2097152 | tf_op jit(solution)/shard_map/all_to_all | solution.py:331
  70.8 1.4 %shard_map.78 = (bf16[4,4,256,128]{3,2,1,0:T(8,128)(2,1)}, bf16[4,4,256,128]{3,2,1,0:T(8,128)(2,1)}) custom-call(bf16[4,256,128]{2,1,0:T(8,128)(2,1)S(1)} %shard_map.75.refs_0_, bf16[4,256,128]{2,1,0:T(8,128)(2,1)S(1)} %collective-permute-done.refs_1_, bf16[4,256,128]{2,1,0:T(8,128)(2,1)S(1)} %collective-permute-done.3.refs_2_, ...), custom_call_target="tpu_custom_call" | custom-call | tf_op jit(solution)/shard_map/pallas_call | solution.py:221
  72.2 1.9 %collective-permute-start.7 = (bf16[4,4,256,128]{3,2,1,0:T(8,128)(2,1)}, bf16[4,4,256,128]{3,2,1,0:T(8,128)(2,1)S(1)}, u32[]{:S(2)}, u32[]{:S(2)}) collective-permute-start(bf16[4,4,256,128]{3,2,1,0:T(8,128)(2,1)} %get-tuple-element.7.refs_0_), channel_id=1, source_target_pairs={{0,16},{16,0},{1,17},{17,1},{2,18},{18,2},{3,19},{19,3},{4,20},{20... | collective-permute-start | bytes 3145736 | tf_op jit(solution)/shard_map/ppermute | solution.py:368
  74.2 2.4 %collective-permute-start.8 = (bf16[4,4,256,128]{3,2,1,0:T(8,128)(2,1)}, bf16[4,4,256,128]{3,2,1,0:T(8,128)(2,1)S(1)}, u32[]{:S(2)}, u32[]{:S(2)}) collective-permute-start(bf16[4,4,256,128]{3,2,1,0:T(8,128)(2,1)} %get-tuple-element.8.refs_1_), channel_id=1, source_target_pairs={{0,16},{16,0},{1,17},{17,1},{2,18},{18,2},{3,19},{19,3},{4,20},{20... | collective-permute-start | bytes 3145736 | tf_op jit(solution)/shard_map/ppermute | solution.py:368
  77.0 2.1 %collective-permute-done.8.refs_3_ = bf16[4,4,256,128]{3,2,1,0:T(8,128)(2,1)S(1)} collective-permute-done((bf16[4,4,256,128]{3,2,1,0:T(8,128)(2,1)}, bf16[4,4,256,128]{3,2,1,0:T(8,128)(2,1)S(1)}, u32[]{:S(2)}, u32[]{:S(2)}) %collective-permute-start.8) | collective-permute-done | bytes 1048608 | tf_op jit(solution)/shard_map/ppermute | solution.py:368
  79.1 3.3 %all-to-all-done.2 = bf16[8,128,512]{2,1,0:T(8,128)(2,1)S(1)} async-done(((bf16[8,128,512]{2,1,0:T(8,128)(2,1)}), bf16[8,128,512]{2,1,0:T(8,128)(2,1)S(1)}, u32[]{:S(2)}, u32[]{:S(2)}) %all-to-all-start.2) | async-done | bytes 1048608 | tf_op jit(solution)/shard_map/all_to_all | solution.py:331
  82.3 3.0 %shard_map.79 = bf16[4,2,4,64,128]{4,3,2,1,0:T(8,128)(2,1)S(1)} custom-call(s32[1]{0:T(128)} %bitcast.1.plane_ref, s32[1]{0:T(128)} %bitcast._.core_ref, bf16[4,2,128,512]{3,2,1,0:T(8,128)(2,1)S(1)} %bitcast.9, bf16[4,4,256,128]{3,2,1,0:T(8,128)(2,1)} %get-tuple-element.7.refs_0_, bf16[4,4,256,128]{3,2,1,0:T(8,128)(2,1)} %get-tuple-element.8.refs_1_, ...), custom_call_target="tpu_custom_call" | custom-call | tf_op jit(solution)/shard_map/pallas_call | solution.py:283
  85.4 24.6 %all_to_all.20 = bf16[32,64,128]{2,1,0:T(8,128)(2,1)S(1)} all-to-all(bf16[32,64,128]{2,1,0:T(8,128)(2,1)S(1)} %bitcast.10), channel_id=1, replica_groups=mesh['z'=8,'yl'=2,'c'=2,'yh'=4,'x'=4] {'x','yl','yh'}, dimensions={0} | all-to-all | bytes 1048576 | tf_op jit(solution)/shard_map/all_to_all | solution.py:331
  (26 shorter events, 6.0 us)
Async XLA Ops:
  0.0 0.9 copy-start.5
  1.9 12.6 %all-to-all-start.1 = ((bf16[8,128,128]{2,1,0:T(8,128)(2,1)}), bf16[8,128,128]{2,1,0:T(8,128)(2,1)S(1)}, u32[]{:S(2)}, u32[]{:S(2)}) async-start(bf16[8,128,128]{2,1,0:T(8,128)(2,1)} %shard_map.74), calls=%async_computation.1 | async-start | bytes 524288 | tf_op jit(solution)/shard_map/all_to_all | solution.py:331
  14.5 46.7 %copy-start.7 = (s32[2,2]{1,0:T(2,128)S(1)}, s32[2,2]{1,0:T(2,128)}, u32[]{:S(2)}) copy-start(s32[2,2]{1,0:T(2,128)} %param.12) | copy-start | bytes 52
  14.5 47.4 %copy-start = (bf16[2,128,512]{2,1,0:T(8,128)(2,1)S(1)}, bf16[2,128,512]{2,1,0:T(8,128)(2,1)}, u32[]{:S(2)}) copy-start(bf16[2,128,512]{2,1,0:T(8,128)(2,1)} %memory_ref.1) | copy-start | bytes 786436
  14.5 47.4 %copy-start.6 = (bf16[128,512]{1,0:T(8,128)(2,1)S(1)}, bf16[128,512]{1,0:T(8,128)(2,1)}, u32[]{:S(2)}) copy-start(bf16[128,512]{1,0:T(8,128)(2,1)} %query_ref.3) | copy-start | bytes 393220
  14.5 47.4 %all-to-all-start = ((bf16[16,3,32,512]{3,2,1,0:T(8,128)(2,1)}), bf16[16,3,32,512]{3,2,1,0:T(8,128)(2,1)S(1)}, u32[]{:S(2)}, u32[]{:S(2)}) async-start(bf16[16,3,32,512]{3,2,1,0:T(8,128)(2,1)} %bitcast.13), calls=%async_computation | async-start | bytes 3145728 | tf_op jit(solution)/shard_map/all_to_all | solution.py:331
  22.0 14.7 %collective-permute-start.3 = (bf16[4,256,128]{2,1,0:T(8,128)(2,1)S(1)}, bf16[4,256,128]{2,1,0:T(8,128)(2,1)S(1)}, u32[]{:S(2)}, u32[]{:S(2)}) collective-permute-start(bf16[4,256,128]{2,1,0:T(8,128)(2,1)S(1)} %shard_map.75.refs_0_), channel_id=1, source_target_pairs={{0,448},{64,0},{128,64},{192,128},{256,192},{320,256},{384,320},{4... | collective-permute-start | bytes 786440 | tf_op jit(solution)/shard_map/ppermute | solution.py:344
  32.8 9.5 %collective-permute-start = (bf16[4,256,128]{2,1,0:T(8,128)(2,1)S(1)}, bf16[4,256,128]{2,1,0:T(8,128)(2,1)S(1)}, u32[]{:S(2)}, u32[]{:S(2)}) collective-permute-start(bf16[4,256,128]{2,1,0:T(8,128)(2,1)S(1)} %shard_map.75.refs_0_), channel_id=1, source_target_pairs={{0,64},{64,128},{128,192},{192,256},{256,320},{320,384},{384,448},... | collective-permute-start | bytes 786440 | tf_op jit(solution)/shard_map/ppermute | solution.py:343
  36.7 9.5 %collective-permute-start.4 = (bf16[4,256,128]{2,1,0:T(8,128)(2,1)S(1)}, bf16[4,256,128]{2,1,0:T(8,128)(2,1)S(1)}, u32[]{:S(2)}, u32[]{:S(2)}) collective-permute-start(bf16[4,256,128]{2,1,0:T(8,128)(2,1)S(1)} %collective-permute-done.3.refs_2_), channel_id=1, source_target_pairs={{0,448},{64,0},{128,64},{192,128},{256,192},{320,256},{384,320},{4... | collective-permute-start | bytes 786440 | tf_op jit(solution)/shard_map/ppermute | solution.py:344
  42.3 10.2 %collective-permute-start.1 = (bf16[4,256,128]{2,1,0:T(8,128)(2,1)S(1)}, bf16[4,256,128]{2,1,0:T(8,128)(2,1)S(1)}, u32[]{:S(2)}, u32[]{:S(2)}) collective-permute-start(bf16[4,256,128]{2,1,0:T(8,128)(2,1)S(1)} %collective-permute-done.refs_1_), channel_id=1, source_target_pairs={{0,64},{64,128},{128,192},{192,256},{256,320},{320,384},{384,448},... | collective-permute-start | bytes 786440 | tf_op jit(solution)/shard_map/ppermute | solution.py:343
  46.2 9.5 %collective-permute-start.5 = (bf16[4,256,128]{2,1,0:T(8,128)(2,1)S(1)}, bf16[4,256,128]{2,1,0:T(8,128)(2,1)S(1)}, u32[]{:S(2)}, u32[]{:S(2)}) collective-permute-start(bf16[4,256,128]{2,1,0:T(8,128)(2,1)S(1)} %collective-permute-done.4.refs_4_), channel_id=1, source_target_pairs={{0,448},{64,0},{128,64},{192,128},{256,192},{320,256},{384,320},{4... | collective-permute-start | bytes 786440 | tf_op jit(solution)/shard_map/ppermute | solution.py:344
  51.8 0.7 copy-start.1
  52.5 9.5 %collective-permute-start.2 = (bf16[4,256,128]{2,1,0:T(8,128)(2,1)S(1)}, bf16[4,256,128]{2,1,0:T(8,128)(2,1)S(1)}, u32[]{:S(2)}, u32[]{:S(2)}) collective-permute-start(bf16[4,256,128]{2,1,0:T(8,128)(2,1)S(1)} %collective-permute-done.1.refs_3_), channel_id=1, source_target_pairs={{0,64},{64,128},{128,192},{192,256},{256,320},{320,384},{384,448},... | collective-permute-start | bytes 786440 | tf_op jit(solution)/shard_map/ppermute | solution.py:343
  54.4 0.7 copy-start.3
  55.6 9.5 %collective-permute-start.6 = (bf16[4,256,128]{2,1,0:T(8,128)(2,1)S(1)}, bf16[4,256,128]{2,1,0:T(8,128)(2,1)S(1)}, u32[]{:S(2)}, u32[]{:S(2)}) collective-permute-start(bf16[4,256,128]{2,1,0:T(8,128)(2,1)S(1)} %collective-permute-done.5.refs_1_.refs_6_), channel_id=1, source_target_pairs={{0,448},{64,0},{128,64},{192,128},{256,192},{320,256},{384,320},{4... | collective-permute-start | bytes 786440 | tf_op jit(solution)/shard_map/ppermute | solution.py:346
  63.7 7.1 %copy-start.2 = (bf16[4,256,128]{2,1,0:T(8,128)(2,1)S(1)}, bf16[4,256,128]{2,1,0:T(8,128)(2,1)}, u32[]{:S(2)}) copy-start(bf16[4,256,128]{2,1,0:T(8,128)(2,1)} %copy-done.1) | copy-start | bytes 786436
  63.7 7.1 %copy-start.4 = (bf16[4,256,128]{2,1,0:T(8,128)(2,1)S(1)}, bf16[4,256,128]{2,1,0:T(8,128)(2,1)}, u32[]{:S(2)}) copy-start(bf16[4,256,128]{2,1,0:T(8,128)(2,1)} %copy-done.3) | copy-start | bytes 786436
  66.2 16.1 %all-to-all-start.2 = ((bf16[8,128,512]{2,1,0:T(8,128)(2,1)}), bf16[8,128,512]{2,1,0:T(8,128)(2,1)S(1)}, u32[]{:S(2)}, u32[]{:S(2)}) async-start(bf16[8,128,512]{2,1,0:T(8,128)(2,1)} %shard_map.77.refs_8_), calls=%async_computation.2 | async-start | bytes 2097152 | tf_op jit(solution)/shard_map/all_to_all | solution.py:331
  72.2 4.8 %collective-permute-start.7 = (bf16[4,4,256,128]{3,2,1,0:T(8,128)(2,1)}, bf16[4,4,256,128]{3,2,1,0:T(8,128)(2,1)S(1)}, u32[]{:S(2)}, u32[]{:S(2)}) collective-permute-start(bf16[4,4,256,128]{3,2,1,0:T(8,128)(2,1)} %get-tuple-element.7.refs_0_), channel_id=1, source_target_pairs={{0,16},{16,0},{1,17},{17,1},{2,18},{18,2},{3,19},{19,3},{4,20},{20... | collective-permute-start | bytes 3145736 | tf_op jit(solution)/shard_map/ppermute | solution.py:368
  74.2 4.9 %collective-permute-start.8 = (bf16[4,4,256,128]{3,2,1,0:T(8,128)(2,1)}, bf16[4,4,256,128]{3,2,1,0:T(8,128)(2,1)S(1)}, u32[]{:S(2)}, u32[]{:S(2)}) collective-permute-start(bf16[4,4,256,128]{3,2,1,0:T(8,128)(2,1)} %get-tuple-element.8.refs_1_), channel_id=1, source_target_pairs={{0,16},{16,0},{1,17},{17,1},{2,18},{18,2},{3,19},{19,3},{4,20},{20... | collective-permute-start | bytes 3145736 | tf_op jit(solution)/shard_map/ppermute | solution.py:368
